TPU v7x, 32 devices: a whole 2x2x4 slice. The times are simulated.
32 devices in a mesh: dp: 16 (over z, x, core), tensor: 2 (over y).
Axes of the slice: x: 2, y: 2, z: 4, core: 2. Of those that a mesh axis runs over, the one named last changes fastest.
Arguments:
- tokens_in: float32 [40960, 1024], P(('dp', 'tensor')), may hold values from -6 to 6
- condition: bfloat16 [40, 1024], P(None, 'dp'), may hold values from -6 to 6
- out_grad: float32 [40960, 1024], P(('dp', 'tensor')), may hold values from -6 to 6
- qkv_weight: float32 [1024, 3, 1024], P('dp', None, 'tensor'), may hold values from -0.1875 to 0.1875
- out_weight: float32 [1024, 1024], P('tensor', 'dp'), may hold values from -0.375 to 0.375
- up_weight: float32 [1024, 4096], P('dp', 'tensor'), may hold values from -0.1875 to 0.1875
- down_weight: float32 [4096, 1024], P('tensor', 'dp'), may hold values from -0.09375 to 0.09375
- ada_weight: float32 [1024, 6144], P('dp'), may hold values from -0.1875 to 0.1875
- bias_all: float32 [14336], replicated, may hold values from -1.5 to 1.5
- qkv_first: float32 [1024, 3, 1024], P('dp', None, 'tensor'), may hold values from -178.09947 to 178.09947
- out_first: float32 [1024, 1024], P('tensor', 'dp'), may hold values from -32.10734 to 32.10734
- up_first: float32 [1024, 4096], P('dp', 'tensor'), may hold values from -28.16 to 28.16
- down_first: float32 [4096, 1024], P('tensor', 'dp'), may hold values from -56.32 to 56.32
- ada_first: float32 [1024, 6144], P('dp'), may hold values from -53.429844 to 53.429844
- bias_first: float32 [14336], replicated, may hold values from -89.049736 to 89.049736
- qkv_second: float32 [1024, 3, 1024], P('dp', None, 'tensor'), may hold values from 8617.984 to 34406.4
- out_second: float32 [1024, 1024], P('tensor', 'dp'), may hold values from 280.08447 to 1118.208
- up_second: float32 [1024, 4096], P('dp', 'tensor'), may hold values from 215.4496 to 860.16
- down_second: float32 [4096, 1024], P('tensor', 'dp'), may hold values from 861.7984 to 3440.64
- ada_second: float32 [1024, 6144], P('dp'), may hold values from 775.6185 to 3096.576
- bias_second: float32 [14336], replicated, may hold values from 2154.496 to 8601.6
Outputs:
- block_out: float32 [40960, 1024], P(('dp', 'tensor'))
- tokens_grad: float32 [40960, 1024], P(('dp', 'tensor'))
- condition_grad: float32 [40, 1024], P(None, 'dp')
- qkv_first_new: float32 [1024, 3, 1024], P('dp', None, 'tensor')
- qkv_second_new: float32 [1024, 3, 1024], P('dp', None, 'tensor')
- qkv_weight_new: float32 [1024, 3, 1024], P('dp', None, 'tensor')
- out_first_new: float32 [1024, 1024], P('tensor', 'dp')
- out_second_new: float32 [1024, 1024], P('tensor', 'dp')
- out_weight_new: float32 [1024, 1024], P('tensor', 'dp')
- up_first_new: float32 [1024, 4096], P('dp', 'tensor')
- up_second_new: float32 [1024, 4096], P('dp', 'tensor')
- up_weight_new: float32 [1024, 4096], P('dp', 'tensor')
- down_first_new: float32 [4096, 1024], P('tensor', 'dp')
- down_second_new: float32 [4096, 1024], P('tensor', 'dp')
- down_weight_new: float32 [4096, 1024], P('tensor', 'dp')
- ada_first_new: float32 [1024, 6144], P('dp')
- ada_second_new: float32 [1024, 6144], P('dp')
- ada_weight_new: float32 [1024, 6144], P('dp')
- bias_first_new: float32 [14336], replicated
- bias_second_new: float32 [14336], replicated
- bias_all_new: float32 [14336], replicated
All inputs are finite; a program needn't handle non-finite values.
Results may differ from a plain program's by a relative error of at most 0.023.
The roundings to bfloat16 on the way count: a program that leaves them out, or rounds other values in their place, can miss the bound.
Values may be sent and summed in bfloat16 or wider, within the bound.
No kernel may reach another device: no remote copies, remote signals or barrier semaphores. Data moves between devices by JAX's collectives and lax.ppermute only.
A program may use at most 320 MiB of HBM per device.

v0:
```python
import math

import jax
import jax.numpy as jnp
from jax import lax
from jax.sharding import PartitionSpec as P

D = 1024
HD = 64
FF = 4096
L = 1024
STEP = 10


eps_norm = 1e-06
beta_one = 0.9
beta_two = 0.95
adam_eps = 1e-08
decay_rate = 0.01
highest = lax.Precision.HIGHEST


def partner(block, axis, distance):
    count = lax.axis_size(axis)
    route = []
    for low in range(count):
        high = low | 1 << distance
        if high != low and high < count:
            route += [(low, high), (high, low)]
    return lax.ppermute(block, axis, route)


def layer_norm(values):
    center = values - jnp.mean(values, axis=-1, keepdims=True)
    spread = jnp.mean(center * center, axis=-1, keepdims=True)
    return center * lax.rsqrt(spread + eps_norm)


def gelu_tanh(values):
    return jax.nn.gelu(values, approximate=True)


def norm_back(values, cotangent):
    unused, pullback = jax.vjp(layer_norm, values)
    return pullback(cotangent)[0]


def adam_update(weight, gradient, first_old, second, step_rate):
    first_new = beta_one * first_old + (1.0 - beta_one) * gradient
    second_new = beta_two * second + (1.0 - beta_two) * gradient * gradient
    first_hat = first_new / (1.0 - beta_one**STEP)
    second_hat = second_new / (1.0 - beta_two**STEP)
    weight_new = weight - step_rate * (
        first_hat / (jnp.sqrt(second_hat) + adam_eps) + decay_rate * weight
    )
    return (first_new, second_new, weight_new)


def attn_rows(values):
    return lax.all_gather(values, "tensor", axis=0, tiled=True)


def window_start(parity, block_index):
    return L * ((parity + block_index) // 2)


def attend_forward(query_low, key_ext, value_ext, parity):
    token_rows, local_width = query_low.shape
    local_heads = local_width // HD
    half_rows = L // 2
    block_count = token_rows // half_rows
    score_scale = HD ** (-0.5)
    query_blocks = query_low.reshape(block_count, half_rows, local_heads, HD)

    def block_step(unused, inputs):
        query_block, block_index = inputs
        start_row = window_start(parity, block_index)
        block_keys = lax.dynamic_slice_in_dim(key_ext, start_row, L, 0).reshape(L, local_heads, HD)
        block_values = lax.dynamic_slice_in_dim(value_ext, start_row, L, 0).reshape(
            L, local_heads, HD
        )
        scores = (
            jnp.einsum("qhd,khd->hqk", query_block, block_keys, preferred_element_type=jnp.float32)
            * score_scale
        )
        row_max = jnp.max(scores, axis=-1, keepdims=True)
        exp_scores = jnp.exp(scores - row_max)
        row_sum = jnp.sum(exp_scores, axis=-1, keepdims=True)
        prob_rows = exp_scores / row_sum
        head_out = jnp.einsum(
            "hqk,khd->qhd",
            prob_rows.astype(jnp.bfloat16),
            block_values,
            preferred_element_type=jnp.float32,
        )
        log_total = (row_max + jnp.log(row_sum))[..., 0]
        return (unused, (head_out.astype(jnp.bfloat16).reshape(half_rows, local_width), log_total))

    unused, (head_blocks, log_totals) = lax.scan(
        block_step,
        jnp.zeros((), jnp.int32),
        (query_blocks, jnp.arange(block_count, dtype=jnp.int32)),
    )
    return (head_blocks.reshape(token_rows, local_width), log_totals)


def attend_backward(query_low, key_ext, value_ext, heads_grad, log_totals, parity):
    token_rows, local_width = query_low.shape
    local_heads = local_width // HD
    half_rows = L // 2
    block_count = token_rows // half_rows
    score_scale = HD ** (-0.5)
    query_blocks = query_low.reshape(block_count, half_rows, local_heads, HD)
    grad_blocks = heads_grad.reshape(block_count, half_rows, local_heads, HD)

    def block_step(carried, inputs):
        key_acc, value_acc = carried
        query_block, grad_block, log_block, block_index = inputs
        start_row = window_start(parity, block_index)
        block_keys = lax.dynamic_slice_in_dim(key_ext, start_row, L, 0).reshape(L, local_heads, HD)
        block_values = lax.dynamic_slice_in_dim(value_ext, start_row, L, 0).reshape(
            L, local_heads, HD
        )
        scores = (
            jnp.einsum("qhd,khd->hqk", query_block, block_keys, preferred_element_type=jnp.float32)
            * score_scale
        )
        prob_rows = jnp.exp(scores - log_block[..., None])
        prob_grad = jnp.einsum(
            "qhd,khd->hqk", grad_block, block_values, preferred_element_type=jnp.float32
        )
        row_dot = jnp.sum(prob_rows * prob_grad, axis=-1, keepdims=True)
        score_grad = (prob_rows * (prob_grad - row_dot)).astype(jnp.bfloat16)
        query_part = jnp.einsum(
            "hqk,khd->qhd", score_grad, block_keys, preferred_element_type=jnp.float32
        )
        query_part = (query_part * score_scale).astype(jnp.bfloat16)
        key_part = (
            jnp.einsum("hqk,qhd->khd", score_grad, query_block, preferred_element_type=jnp.float32)
            * score_scale
        )
        value_part = jnp.einsum(
            "hqk,qhd->khd",
            prob_rows.astype(jnp.bfloat16),
            grad_block,
            preferred_element_type=jnp.float32,
        )
        key_acc = lax.dynamic_update_slice_in_dim(
            key_acc,
            lax.dynamic_slice_in_dim(key_acc, start_row, L, 0) + key_part.reshape(L, local_width),
            start_row,
            0,
        )
        value_acc = lax.dynamic_update_slice_in_dim(
            value_acc,
            lax.dynamic_slice_in_dim(value_acc, start_row, L, 0)
            + value_part.reshape(L, local_width),
            start_row,
            0,
        )
        return ((key_acc, value_acc), query_part.reshape(half_rows, local_width))

    zero_ext = jnp.zeros((key_ext.shape[0], local_width), jnp.float32)
    (key_acc, value_acc), query_grad_blocks = lax.scan(
        block_step,
        (zero_ext, zero_ext),
        (query_blocks, grad_blocks, log_totals, jnp.arange(block_count, dtype=jnp.int32)),
    )
    return (query_grad_blocks.reshape(token_rows, local_width), key_acc, value_acc)


def on_device(
    tokens_in,
    condition,
    out_grad,
    qkv_weight,
    out_weight,
    up_weight,
    down_weight,
    ada_weight,
    bias_all,
    qkv_first,
    out_first,
    up_first,
    down_first,
    ada_first,
    bias_first,
    qkv_second,
    out_second,
    up_second,
    down_second,
    ada_second,
    bias_second,
):
    tensor_count = lax.axis_size("tensor")
    tensor_index = lax.axis_index("tensor")
    dp_index = lax.axis_index("dp")
    parity = dp_index % 2
    row_count = tokens_in.shape[0]
    latent_count = condition.shape[0]
    local_width = D // tensor_count
    local_hidden = FF // tensor_count
    half_rows = L // 2
    token_rows = row_count * tensor_count
    cond_value = condition.astype(jnp.float32)
    silu_low = jax.nn.silu(cond_value).astype(jnp.bfloat16)
    ada_low = ada_weight.astype(jnp.bfloat16)
    ada_part = jnp.dot(silu_low, ada_low, preferred_element_type=jnp.float32)
    modulation = lax.psum(ada_part, "dp") + bias_all[4 * D + FF :]
    qkv_gathered, out_gathered, up_gathered, down_gathered = (
        lax.all_gather(qkv_weight.astype(jnp.bfloat16), "dp", axis=0, tiled=True),
        lax.all_gather(out_weight.astype(jnp.bfloat16), "dp", axis=1, tiled=True),
        lax.all_gather(up_weight.astype(jnp.bfloat16), "dp", axis=0, tiled=True),
        lax.all_gather(down_weight.astype(jnp.bfloat16), "dp", axis=1, tiled=True),
    )
    local_latents = row_count // L + 2
    row_start = (dp_index * tensor_count + tensor_index) * row_count
    first_latent = row_start // L
    row_latent = (row_start + jnp.arange(row_count, dtype=jnp.int32)) // L - first_latent
    latent_pick = (
        row_latent[:, None] == jnp.arange(local_latents, dtype=jnp.int32)[None, :]
    ).astype(jnp.float32)
    mod_padded = jnp.concatenate(
        [modulation, jnp.zeros((local_latents, 6 * D), jnp.float32)], axis=0
    )
    mod_local = lax.dynamic_slice_in_dim(mod_padded, first_latent, local_latents, 0)
    mod_rows = jnp.dot(
        latent_pick, mod_local, precision=highest, preferred_element_type=jnp.float32
    )
    shift_attn = mod_rows[:, 0:D]
    scale_attn = mod_rows[:, D : 2 * D]
    gate_attn = mod_rows[:, 2 * D : 3 * D]
    shift_mlp = mod_rows[:, 3 * D : 4 * D]
    scale_mlp = mod_rows[:, 4 * D : 5 * D]
    gate_mlp = mod_rows[:, 5 * D : 6 * D]
    norm_attn = layer_norm(tokens_in)
    attn_input = attn_rows((norm_attn * (1.0 + scale_attn) + shift_attn).astype(jnp.bfloat16))
    projected = jnp.einsum(
        "td,dkc->tkc", attn_input, qkv_gathered, preferred_element_type=jnp.float32
    )
    query_bias = lax.dynamic_slice_in_dim(bias_all, tensor_index * local_width, local_width, 0)
    value_bias = lax.dynamic_slice_in_dim(bias_all, D + tensor_index * local_width, local_width, 0)
    query_low = (projected[:, 0] + query_bias).astype(jnp.bfloat16)
    key_low = projected[:, 1].astype(jnp.bfloat16)
    value_low = (projected[:, 2] + value_bias).astype(jnp.bfloat16)
    send_start = (1 - parity) * (token_rows - half_rows)
    own_start = parity * half_rows
    rim_start = (1 - parity) * token_rows
    rim_send = jnp.stack(
        [
            lax.dynamic_slice_in_dim(key_low, send_start, half_rows, 0),
            lax.dynamic_slice_in_dim(value_low, send_start, half_rows, 0),
        ]
    )
    rim_recv = partner(rim_send, "dp", 0)
    ext_zero = jnp.zeros((token_rows + half_rows, local_width), jnp.bfloat16)
    key_ext = lax.dynamic_update_slice_in_dim(
        lax.dynamic_update_slice_in_dim(ext_zero, key_low, own_start, 0), rim_recv[0], rim_start, 0
    )
    value_ext = lax.dynamic_update_slice_in_dim(
        lax.dynamic_update_slice_in_dim(ext_zero, value_low, own_start, 0),
        rim_recv[1],
        rim_start,
        0,
    )
    head_low, log_totals = attend_forward(query_low, key_ext, value_ext, parity)
    attn_value = (
        lax.psum_scatter(
            jnp.dot(head_low, out_gathered, preferred_element_type=jnp.float32).astype(
                jnp.bfloat16
            ),
            "tensor",
            scatter_dimension=0,
            tiled=True,
        ).astype(jnp.float32)
        + bias_all[2 * D : 3 * D]
    )
    residual_mid = tokens_in + gate_attn * attn_value
    norm_mlp = layer_norm(residual_mid)
    mlp_low = (norm_mlp * (1.0 + scale_mlp) + shift_mlp).astype(jnp.bfloat16)
    down_bias = bias_all[3 * D + FF : 4 * D + FF]
    mlp_grad = (out_grad * gate_mlp).astype(jnp.bfloat16)

    def mlp_rows(values):
        return lax.all_gather(values, "tensor", axis=0, tiled=True)

    def mlp_total(values):
        return lax.psum_scatter(
            values.astype(jnp.bfloat16), "tensor", scatter_dimension=0, tiled=True
        ).astype(jnp.float32)

    mlp_gathered = mlp_rows(mlp_low)
    up_bias = lax.dynamic_slice_in_dim(
        bias_all, 3 * D + tensor_index * local_hidden, local_hidden, 0
    )
    up_value = jnp.dot(mlp_gathered, up_gathered, preferred_element_type=jnp.float32) + up_bias
    hidden_low = gelu_tanh(up_value).astype(jnp.bfloat16)
    mlp_value = (
        mlp_total(jnp.dot(hidden_low, down_gathered, preferred_element_type=jnp.float32))
        + down_bias
    )
    grad_gathered = mlp_rows(mlp_grad)
    hidden_grad = jnp.einsum(
        "td,fd->tf", grad_gathered, down_gathered, preferred_element_type=jnp.float32
    )
    unused, gelu_pull = jax.vjp(gelu_tanh, up_value)
    up_grad = gelu_pull(hidden_grad)[0].astype(jnp.bfloat16)
    down_wgrad = jnp.einsum(
        "tf,td->fd", hidden_low, grad_gathered, preferred_element_type=jnp.float32
    )
    up_wgrad = jnp.einsum("td,tf->df", mlp_gathered, up_grad, preferred_element_type=jnp.float32)
    up_bias_grad = lax.dynamic_update_slice_in_dim(
        jnp.zeros((FF,), jnp.float32),
        jnp.sum(up_grad.astype(jnp.float32), axis=0),
        tensor_index * local_hidden,
        0,
    )
    mlp_norm_grad = mlp_total(
        jnp.einsum("tf,df->td", up_grad, up_gathered, preferred_element_type=jnp.float32)
    )
    block_out = residual_mid + gate_mlp * mlp_value
    mid_grad = out_grad + norm_back(residual_mid, mlp_norm_grad * (1.0 + scale_mlp))
    attn_grad = (mid_grad * gate_attn).astype(jnp.bfloat16)
    attn_grad_rows = attn_rows(attn_grad)
    out_wgrad = jnp.einsum(
        "tc,td->cd", head_low, attn_grad_rows, preferred_element_type=jnp.float32
    )
    heads_grad = jnp.einsum(
        "td,cd->tc", attn_grad_rows, out_gathered, preferred_element_type=jnp.float32
    ).astype(jnp.bfloat16)
    query_grad, key_acc, value_acc = attend_backward(
        query_low, key_ext, value_ext, heads_grad, log_totals, parity
    )
    rim_grad = jnp.stack(
        [
            lax.dynamic_slice_in_dim(key_acc, rim_start, half_rows, 0),
            lax.dynamic_slice_in_dim(value_acc, rim_start, half_rows, 0),
        ]
    )
    rim_back = partner(rim_grad.astype(jnp.bfloat16), "dp", 0).astype(rim_grad.dtype)
    key_own = lax.dynamic_slice_in_dim(key_acc, own_start, token_rows, 0)
    key_own = lax.dynamic_update_slice_in_dim(
        key_own,
        lax.dynamic_slice_in_dim(key_own, send_start, half_rows, 0) + rim_back[0],
        send_start,
        0,
    )
    value_own = lax.dynamic_slice_in_dim(value_acc, own_start, token_rows, 0)
    value_own = lax.dynamic_update_slice_in_dim(
        value_own,
        lax.dynamic_slice_in_dim(value_own, send_start, half_rows, 0) + rim_back[1],
        send_start,
        0,
    )
    key_grad = key_own.astype(jnp.bfloat16)
    value_grad = value_own.astype(jnp.bfloat16)
    qkv_grad = jnp.stack([query_grad, key_grad, value_grad], axis=1)
    qkv_wgrad = jnp.einsum("td,tkc->dkc", attn_input, qkv_grad, preferred_element_type=jnp.float32)
    attn_norm_grad = lax.psum_scatter(
        jnp.einsum(
            "tkc,dkc->td", qkv_grad, qkv_gathered, preferred_element_type=jnp.float32
        ).astype(jnp.bfloat16),
        "tensor",
        scatter_dimension=0,
        tiled=True,
    ).astype(jnp.float32)
    tokens_grad = mid_grad + norm_back(tokens_in, attn_norm_grad * (1.0 + scale_attn))
    mod_grad_rows = jnp.concatenate(
        [
            attn_norm_grad,
            attn_norm_grad * norm_attn,
            mid_grad * attn_value,
            mlp_norm_grad,
            mlp_norm_grad * norm_mlp,
            out_grad * mlp_value,
        ],
        axis=1,
    )
    mod_grad_local = jnp.dot(
        latent_pick.T, mod_grad_rows, precision=highest, preferred_element_type=jnp.float32
    )
    mod_grad_all = lax.dynamic_update_slice_in_dim(
        jnp.zeros((latent_count + local_latents, 6 * D), jnp.float32),
        mod_grad_local,
        first_latent,
        0,
    )[:latent_count]
    query_slot = lax.dynamic_update_slice_in_dim(
        jnp.zeros((D,), jnp.float32),
        jnp.sum(query_grad.astype(jnp.float32), axis=0),
        tensor_index * local_width,
        0,
    )
    value_slot = lax.dynamic_update_slice_in_dim(
        jnp.zeros((D,), jnp.float32),
        jnp.sum(value_grad.astype(jnp.float32), axis=0),
        tensor_index * local_width,
        0,
    )
    bias_part = jnp.concatenate(
        [
            query_slot,
            value_slot,
            jnp.sum(attn_grad.astype(jnp.float32), axis=0),
            up_bias_grad,
            jnp.sum(mlp_grad.astype(jnp.float32), axis=0),
            jnp.zeros((6 * D,), jnp.float32),
        ]
    )
    mod_grad, bias_summed = lax.psum((mod_grad_all, bias_part), ("dp", "tensor"))
    bias_grad = jnp.concatenate([bias_summed[: 4 * D + FF], jnp.sum(mod_grad, axis=0)])
    ada_wgrad = jnp.dot(
        silu_low.astype(jnp.float32).T,
        mod_grad,
        precision=highest,
        preferred_element_type=jnp.float32,
    )
    cond_inner = jnp.dot(
        mod_grad,
        ada_low.astype(jnp.float32).T,
        precision=highest,
        preferred_element_type=jnp.float32,
    )
    unused, silu_pull = jax.vjp(jax.nn.silu, cond_value)
    condition_grad = silu_pull(cond_inner)[0]
    qkv_summed, out_summed, up_summed, down_summed = (
        lax.psum_scatter(
            qkv_wgrad.astype(jnp.bfloat16), "dp", scatter_dimension=0, tiled=True
        ).astype(jnp.float32),
        lax.psum_scatter(
            out_wgrad.astype(jnp.bfloat16), "dp", scatter_dimension=1, tiled=True
        ).astype(jnp.float32),
        lax.psum_scatter(
            up_wgrad.astype(jnp.bfloat16), "dp", scatter_dimension=0, tiled=True
        ).astype(jnp.float32),
        lax.psum_scatter(
            down_wgrad.astype(jnp.bfloat16), "dp", scatter_dimension=1, tiled=True
        ).astype(jnp.float32),
    )
    qkv_new = adam_update(qkv_weight, qkv_summed, qkv_first, qkv_second, 3.0 / math.sqrt(D))
    out_new = adam_update(out_weight, out_summed, out_first, out_second, 3.0 / math.sqrt(D // 4))
    up_new = adam_update(up_weight, up_summed, up_first, up_second, 3.0 / math.sqrt(D))
    down_new = adam_update(down_weight, down_summed, down_first, down_second, 3.0 / math.sqrt(FF))
    ada_new = adam_update(ada_weight, ada_wgrad, ada_first, ada_second, 3.0 / math.sqrt(D))
    bias_new = adam_update(bias_all, bias_grad, bias_first, bias_second, 0.9)
    return (
        block_out,
        tokens_grad,
        condition_grad,
        qkv_new[0],
        qkv_new[1],
        qkv_new[2],
        out_new[0],
        out_new[1],
        out_new[2],
        up_new[0],
        up_new[1],
        up_new[2],
        down_new[0],
        down_new[1],
        down_new[2],
        ada_new[0],
        ada_new[1],
        ada_new[2],
        bias_new[0],
        bias_new[1],
        bias_new[2],
    )


def solution(mesh):
    placed = (
        P(("dp", "tensor"), None),
        P(None, "dp"),
        P(("dp", "tensor"), None),
        P("dp", None, "tensor"),
        P("tensor", "dp"),
        P("dp", "tensor"),
        P("tensor", "dp"),
        P("dp", None),
        P(),
        P("dp", None, "tensor"),
        P("tensor", "dp"),
        P("dp", "tensor"),
        P("tensor", "dp"),
        P("dp", None),
        P(),
        P("dp", None, "tensor"),
        P("tensor", "dp"),
        P("dp", "tensor"),
        P("tensor", "dp"),
        P("dp", None),
        P(),
    )
    return jax.shard_map(
        on_device,
        mesh=mesh,
        in_specs=placed,
        out_specs=(
            P(("dp", "tensor"), None),
            P(("dp", "tensor"), None),
            P(None, "dp"),
            P("dp", None, "tensor"),
            P("dp", None, "tensor"),
            P("dp", None, "tensor"),
            P("tensor", "dp"),
            P("tensor", "dp"),
            P("tensor", "dp"),
            P("dp", "tensor"),
            P("dp", "tensor"),
            P("dp", "tensor"),
            P("tensor", "dp"),
            P("tensor", "dp"),
            P("tensor", "dp"),
            P("dp", None),
            P("dp", None),
            P("dp", None),
            P(),
            P(),
            P(),
        ),
        check_vma=False,
    )
```

profile of v0, /device:TPU:0, one launch (start us, length us, event | category | flops | bytes accessed | tf_op | source)
XLA Modules:
  0.0 1857.2 jit_solution(16101743699554683970)
XLA Ops:
  16.1 91.8 %all-reduce.4.cloned.1.call-done = f32[40,6144]{1,0:T(8,128)} async-done(((f32[40,6144]{1,0:T(8,128)}), f32[40,6144]{1,0:T(8,128)}) %all-reduce.4.cloned.1.call-update) | async-done | bytes 983056 | tf_op jit(solution)/shard_map/psum | solution.py:209
  109.4 16.4 fusion.55
  133.7 65.7 %all-gather.9.cloned.1.call-done = bf16[2560,1024]{1,0:T(8,128)(2,1)} async-done(((bf16[1280,1024]{1,0:T(8,128)(2,1)}), bf16[2560,1024]{1,0:T(8,128)(2,1)}) %all-gather.9.cloned.1.call-update) | async-done | bytes 5242896 | tf_op jit(solution)/shard_map/all_gather | solution.py:60
  199.4 48.0 %all-gather.11.cloned.1.call-done = bf16[1024,3,512]{2,0,1:T(8,128)(2,1)} async-done(((bf16[64,3,512]{2,0,1:T(8,128)(2,1)}), bf16[1024,3,512]{2,0,1:T(8,128)(2,1)}) %all-gather.11.cloned.1.call-update) | async-done | bytes 3145744 | tf_op jit(solution)/shard_map/all_gather | solution.py:211
  247.4 11.3 fusion.44
  310.7 96.0 %while.30 = (s32[]{:T(128)}, bf16[5,512,512]{2,1,0:T(8,128)(2,1)}, f32[5,8,512]{2,1,0:T(8,128)}, s32[5]{0:T(128)S(1)}, s32[]{:T(128)}, /*index=5*/bf16[3072,512]...) while((s32[]{:T(128)}, bf16[5,512,512]{2,1,0:T(8,128)(2,1)}, ...), condition=%wide.region_6.7_spmd, body=%wide.region_3.6_spmd.sunk | while | flops 1111748608 | bytes 59900272 | solution.py:99
  417.7 62.2 %reduce-scatter.9.cloned.1.call-done = bf16[1280,1024]{1,0:T(8,128)(2,1)} async-done(((bf16[2560,1024]{1,0:T(8,128)(2,1)}), bf16[1280,1024]{1,0:T(8,128)(2,1)}) %reduce-scatter.9.cloned.1.call-update) | async-done | bytes 2621456 | tf_op jit(solution)/shard_map/reduce_scatter | solution.py:268
  498.3 35.0 %all-gather.17.cloned.1.call-done = bf16[1024,2048]{1,0:T(8,128)(2,1)} async-done(((bf16[64,2048]{1,0:T(8,128)(2,1)}), bf16[1024,2048]{1,0:T(8,128)(2,1)}) %all-gather.17.cloned.1.call-update) | async-done | bytes 4194320 | tf_op jit(solution)/shard_map/all_gather | solution.py:213
  533.3 69.3 %all-gather.15.cloned.1.call-done = bf16[2560,1024]{1,0:T(8,128)(2,1)} async-done(((bf16[1280,1024]{1,0:T(8,128)(2,1)}), bf16[2560,1024]{1,0:T(8,128)(2,1)}) %all-gather.15.cloned.1.call-update) | async-done | bytes 5242896 | tf_op jit(solution)/shard_map/all_gather | solution.py:285
  602.6 24.3 %multiply_convert_fusion.1 = (bf16[2560,2048]{1,0:T(8,128)(2,1)}, f32[2560,2048]{1,0:T(8,128)}) fusion(f32[2048]{0:T(1024)S(1)} %dynamic_slice.120, bf16[2560,1024]{1,0:T(8,128)(2,1)} %all-gather.15.cloned.1.call-done, bf16[1024,2048]{1,0:T(8,128)(2,1)} %all-gather.17.cloned.1.call-done), kind=kOutput, calls=%fused_computation.60 | convolution fusion | flops 10789847040 | bytes 40902656 | tf_op jit(solution)/shard_map/dot_general | solution.py:296
  626.9 46.5 %all-gather.21.cloned.1.call-done = bf16[2560,1024]{1,0:T(8,128)(2,1)} async-done(((bf16[1280,1024]{1,0:T(8,128)(2,1)}), bf16[2560,1024]{1,0:T(8,128)(2,1)}) %all-gather.21.cloned.1.call-update) | async-done | bytes 5242896 | tf_op jit(solution)/shard_map/all_gather | solution.py:285
  673.4 16.8 convolution_convert_fusion.5
  690.3 72.8 %reduce-scatter.23.cloned.1.call-done = bf16[2048,64]{0,1:T(8,128)(2,1)} async-done(((bf16[2048,1024]{0,1:T(8,128)(2,1)}), bf16[2048,64]{0,1:T(8,128)(2,1)}) %reduce-scatter.23.cloned.1.call-update) | async-done | bytes 262160 | tf_op jit(solution)/shard_map/reduce_scatter | solution.py:436
  765.6 49.6 %all-gather.19.cloned.1.call-done = bf16[2048,1024]{0,1:T(8,128)(2,1)} async-done(((bf16[2048,64]{0,1:T(8,128)(2,1)}), bf16[2048,1024]{0,1:T(8,128)(2,1)}) %all-gather.19.cloned.1.call-update) | async-done | bytes 4194320 | tf_op jit(solution)/shard_map/all_gather | solution.py:214
  815.3 28.9 %convert_reduce_fusion = (f32[2048]{0:T(1024)}, bf16[2560,2048]{1,0:T(8,128)(2,1)S(1)}) fusion(f32[2560,2048]{1,0:T(8,128)} %get-tuple-element.388, f32[2048]{0:T(1024)S(1)} %dynamic_slice.120, bf16[2560,1024]{1,0:T(8,128)(2,1)} %all-gather.21.cloned.1.call-done, bf16[2048,1024]{0,1:T(8,128)(2,1)} %all-gather.19.cloned.1.call-done), kind=kOutput, calls=%fused_computation.59 | convolution fusion | flops 10858002432 | bytes 40910848 | tf_op jit(solution)/shard_map/td,fd->tf/dot_general | solution.py:303
  848.1 12.7 convolution_convert_fusion
  860.9 16.8 convolution_convert_fusion.1
  877.7 47.4 %reduce-scatter.13.cloned.1.call-done = bf16[1280,1024]{1,0:T(8,128)(2,1)} async-done(((bf16[2560,1024]{1,0:T(8,128)(2,1)}), bf16[1280,1024]{1,0:T(8,128)(2,1)}) %reduce-scatter.13.cloned.1.call-update) | async-done | bytes 2621456 | tf_op jit(solution)/shard_map/reduce_scatter | solution.py:288
  930.9 62.8 %reduce-scatter.11.cloned.1.call-done = bf16[1280,1024]{1,0:T(8,128)(2,1)} async-done(((bf16[2560,1024]{1,0:T(8,128)(2,1)}), bf16[1280,1024]{1,0:T(8,128)(2,1)}) %reduce-scatter.11.cloned.1.call-update) | async-done | bytes 2621456 | tf_op jit(solution)/shard_map/reduce_scatter | solution.py:288
  1011.1 17.3 convolution_convert_fusion.4
  1028.4 51.3 %all-gather.23.cloned.1.call-done = bf16[2560,1024]{1,0:T(8,128)(2,1)} async-done(((bf16[1280,1024]{1,0:T(8,128)(2,1)}), bf16[2560,1024]{1,0:T(8,128)(2,1)}) %all-gather.23.cloned.1.call-update) | async-done | bytes 5242896 | tf_op jit(solution)/shard_map/all_gather | solution.py:60
  1103.9 376.6 %while.31 = (s32[]{:T(128)}, f32[3072,512]{1,0:T(8,128)}, f32[3072,512]{1,0:T(8,128)}, bf16[5,512,512]{1,2,0:T(8,128)(2,1)}, s32[5]{0:T(128)S(1)}, /*index=5*/s3...) while((s32[]{:T(128)}, f32[3072,512]{1,0:T(8,128)}, ...), condition=%wide.region_16.17_spmd, body=%wide.region_14.16_spmd.sunk | while | flops 2736779264 | bytes 371835424 | solution.py:164
  1135.9 14.5 multiply_reduce_fusion.9
  1211.2 14.4 multiply_reduce_fusion.9
  1286.2 14.4 multiply_reduce_fusion.9
  1361.3 14.4 multiply_reduce_fusion.9
  1436.4 14.4 multiply_reduce_fusion.9
  1520.8 40.2 %psum.23 = f32[14336]{0:T(1024)S(1)} all-reduce(f32[14336]{0:T(1024)S(1)} %broadcast_dynamic-update-slice_fusion), channel_id=1, replica_groups=mesh['dp'=16,'tensor'=2] {'dp','tensor'}, use_global_device_ids=true, to_apply=%region_30.31 | all-reduce | flops 14336 | bytes 114688 | tf_op jit(solution)/shard_map/psum | solution.py:410
  1561.0 13.3 fusion.46
  1614.1 15.1 fusion.54
  1637.7 67.5 %reduce-scatter.17.cloned.1.call-done = bf16[64,3,512]{2,0,1:T(8,128)(2,1)} async-done(((bf16[1024,3,512]{2,0,1:T(8,128)(2,1)}), bf16[64,3,512]{2,0,1:T(8,128)(2,1)}) %reduce-scatter.17.cloned.1.call-update) | async-done | bytes 196624 | tf_op jit(solution)/shard_map/reduce_scatter | solution.py:427
  1707.6 131.6 %all-reduce.6.cloned.1.call-done = f32[40,6144]{1,0:T(8,128)} async-done(((f32[40,6144]{1,0:T(8,128)}), f32[40,6144]{1,0:T(8,128)}) %all-reduce.6.cloned.1.call-update) | async-done | bytes 983056 | tf_op jit(solution)/shard_map/psum | solution.py:410
  (474 shorter events, 646.6 us)
Async XLA Ops:
  7.2 100.7 %all-reduce.4.cloned.1.call-start = ((), (), s32[]{:S(2)}) async-start(), calls=%async_computation.8 | async-start | bytes 1966080 | tf_op jit(solution)/shard_map/psum | solution.py:209
  9.9 189.5 %all-gather.9.cloned.1.call-start = ((), (), s32[]{:S(2)}) async-start(), calls=%async_computation.9 | async-start | bytes 7864320 | tf_op jit(solution)/shard_map/all_gather | solution.py:60
  10.0 99.3 %copy-start.30 = (s32[1280]{0:T(1024)}, s32[1280]{0:T(1024)S(1)}, u32[]{:S(2)}) copy-start(s32[1280]{0:T(1024)S(1)} %fusion.82) | copy-start | bytes 15364
  12.9 112.9 %copy-start.28 = (f32[1280]{0:T(1024)}, f32[1280]{0:T(1024)S(1)}, u32[]{:S(2)}) copy-start(f32[1280]{0:T(1024)S(1)} %broadcast_multiply_fusion.1) | copy-start | bytes 15364
  16.0 109.7 %copy-start.38 = (f32[1280]{0:T(1024)}, f32[1280]{0:T(1024)S(1)}, u32[]{:S(2)}) copy-start(f32[1280]{0:T(1024)S(1)} %fusion.85) | copy-start | bytes 15364
  131.7 115.7 %all-gather.11.cloned.1.call-start = ((), (), s32[]{:S(2)}) async-start(), calls=%async_computation.10 | async-start | bytes 3342336 | tf_op jit(solution)/shard_map/all_gather | solution.py:211
  132.5 274.3 %all-gather.13.cloned.1.call-start = ((), (), s32[]{:S(2)}) async-start(), calls=%async_computation.11 | async-start | bytes 1114112 | tf_op jit(solution)/shard_map/all_gather | solution.py:212
  133.2 346.7 %reduce-scatter.9.cloned.1.call-start = ((), (), s32[]{:S(2)}) async-start(), calls=%async_computation.12 | async-start | bytes 7864320 | tf_op jit(solution)/shard_map/reduce_scatter | solution.py:268
  273.5 27.8 %collective-permute-start = (bf16[2,512,512]{2,1,0:T(8,128)(2,1)}, bf16[2,512,512]{2,1,0:T(8,128)(2,1)}, u32[]{:S(2)}, u32[]{:S(2)}) collective-permute-start(bf16[2,512,512]{2,1,0:T(8,128)(2,1)} %pad_maximum_fusion.5), channel_id=1, source_target_pairs={{0,2},{2,0},{4,6},{6,4},{8,10},{10,8},{12,14},{14,12},{16,18},{18,... | collective-permute-start | bytes 3145736 | tf_op jit(solution)/shard_map/ppermute | solution.py:30
  415.2 118.1 %all-gather.17.cloned.1.call-start = ((), (), s32[]{:S(2)}) async-start(), calls=%async_computation.14 | async-start | bytes 4456448 | tf_op jit(solution)/shard_map/all_gather | solution.py:213
  417.0 185.6 %all-gather.15.cloned.1.call-start = ((), (), s32[]{:S(2)}) async-start(), calls=%async_computation.13 | async-start | bytes 7864320 | tf_op jit(solution)/shard_map/all_gather | solution.py:285
  485.8 507.9 %copy-start.32 = (f32[1280]{0:T(1024)}, f32[1280]{0:T(1024)S(1)}, u32[]{:S(2)}) copy-start(f32[1280]{0:T(1024)S(1)} %broadcast_multiply_fusion) | copy-start | bytes 15364
  497.5 175.9 %all-gather.21.cloned.1.call-start = ((), (), s32[]{:S(2)}) async-start(), calls=%async_computation.17 | async-start | bytes 7864320 | tf_op jit(solution)/shard_map/all_gather | solution.py:285
  498.2 264.9 %reduce-scatter.23.cloned.1.call-start = ((), (), s32[]{:S(2)}) async-start(), calls=%async_computation.25 | async-start | bytes 4456448 | tf_op jit(solution)/shard_map/reduce_scatter | solution.py:436
  690.2 125.0 %all-gather.19.cloned.1.call-start = ((), (), s32[]{:S(2)}) async-start(), calls=%async_computation.15 | async-start | bytes 4456448 | tf_op jit(solution)/shard_map/all_gather | solution.py:214
  765.6 159.6 %reduce-scatter.13.cloned.1.call-start = ((), (), s32[]{:S(2)}) async-start(), calls=%async_computation.18 | async-start | bytes 7864320 | tf_op jit(solution)/shard_map/reduce_scatter | solution.py:288
  860.8 132.9 %reduce-scatter.11.cloned.1.call-start = ((), (), s32[]{:S(2)}) async-start(), calls=%async_computation.16 | async-start | bytes 7864320 | tf_op jit(solution)/shard_map/reduce_scatter | solution.py:288
  877.7 116.0 %copy-start.41 = (f32[1280]{0:T(1024)S(1)}, f32[1280]{0:T(1024)}, u32[]{:S(2)}) copy-start(f32[1280]{0:T(1024)} %copy-done.40) | copy-start | bytes 15364
  877.7 116.0 %copy-start.50 = (f32[1024]{0:T(1024)S(1)}, f32[1024]{0:T(1024)}, u32[]{:S(2)}) copy-start(f32[1024]{0:T(1024)} %get-tuple-element.383) | copy-start | bytes 12292
  877.7 202.1 %all-gather.23.cloned.1.call-start = ((), (), s32[]{:S(2)}) async-start(), calls=%async_computation.19 | async-start | bytes 7864320 | tf_op jit(solution)/shard_map/all_gather | solution.py:60
  1011.0 497.3 %reduce-scatter.21.cloned.1.call-start = ((), (), s32[]{:S(2)}) async-start(), calls=%async_computation.24 | async-start | bytes 4456448 | tf_op jit(solution)/shard_map/reduce_scatter | solution.py:433
  1028.4 546.1 %reduce-scatter.15.cloned.1.call-start = ((), (), s32[]{:S(2)}) async-start(), calls=%async_computation.20 | async-start | bytes 7864320 | tf_op jit(solution)/shard_map/reduce_scatter | solution.py:359
  1483.4 7.6 collective-permute-start.1
  1507.4 128.4 %reduce-scatter.19.cloned.1.call-start = ((), (), s32[]{:S(2)}) async-start(), calls=%async_computation.23 | async-start | bytes 1114112 | tf_op jit(solution)/shard_map/reduce_scatter | solution.py:430
  1520.0 185.1 %reduce-scatter.17.cloned.1.call-start = ((), (), s32[]{:S(2)}) async-start(), calls=%async_computation.22 | async-start | bytes 3342336 | tf_op jit(solution)/shard_map/reduce_scatter | solution.py:427
  1574.3 264.9 %all-reduce.6.cloned.1.call-start = ((), (), s32[]{:S(2)}) async-start(), calls=%async_computation.21 | async-start | bytes 1966080 | tf_op jit(solution)/shard_map/psum | solution.py:410
  1629.2 211.3 %copy-start.36 = (f32[14336]{0:T(1024)S(1)}, f32[14336]{0:T(1024)}, u32[]{:S(2)}) copy-start(f32[14336]{0:T(1024)} %param.33) | copy-start | bytes 172036
  1629.2 211.3 %slice-start.13 = ((f32[14336]{0:T(1024)}), f32[8192]{0:T(1024)S(1)}, s32[]{:S(2)}) async-start(f32[14336]{0:T(1024)} %copy-done.37), calls=%async_computation.39 | async-start | bytes 65536 | tf_op jit(solution)/shard_map/slice | solution.py:411
  1629.2 211.3 %copy-start.47 = (f32[14336]{0:T(1024)S(1)}, f32[14336]{0:T(1024)}, u32[]{:S(2)}) copy-start(f32[14336]{0:T(1024)} %param.45) | copy-start | bytes 172036
  1629.2 212.0 %copy-start.16 = (f32[64,6144]{1,0:T(8,128)S(1)}, f32[64,6144]{1,0:T(8,128)}, u32[]{:S(2)}) copy-start(f32[64,6144]{1,0:T(8,128)} %param.32) | copy-start | bytes 4718596
  1629.3 212.0 %copy-start.49 = (bf16[40,64]{1,0:T(8,128)(2,1)S(1)}, bf16[40,64]{1,0:T(8,128)(2,1)}, u32[]{:S(2)}) copy-start(bf16[40,64]{1,0:T(8,128)(2,1)} %param.26) | copy-start | bytes 15364
  1630.8 209.7 %copy-start.48 = (f32[14336]{0:T(1024)S(1)}, f32[14336]{0:T(1024)}, u32[]{:S(2)}) copy-start(f32[14336]{0:T(1024)} %param.39) | copy-start | bytes 172036
  (82 other events, 1307.4 us)
Sparse Core Ops, SparseCore 0:
  12.0 95.8 all-reduce.3
  131.9 67.5 all-gather.8
  202.2 45.1 all-gather.10
  250.0 36.7 all-gather.12
  415.4 64.5 reduce-scatter.8
  482.7 50.5 all-gather.16
  535.5 67.0 all-gather.14
  604.8 68.5 all-gather.20
  690.3 72.7 reduce-scatter.22
  765.7 49.5 all-gather.18
  860.9 64.1 reduce-scatter.12
  928.0 65.6 reduce-scatter.10
  1011.1 68.5 all-gather.22
  1083.4 72.3 reduce-scatter.20
  1507.6 66.8 reduce-scatter.14
  1578.5 57.3 reduce-scatter.18
  1640.0 65.1 reduce-scatter.16
  1711.6 127.5 all-reduce.5
where the time goes:
time: 1870 us; the launch traced here: 1860 us
  waiting for transfers between devices  907 us (49%)
  matrix products  421 us (23%)
  local copies, waits for them, and re-layouts  261 us (14%)
  other arithmetic  204 us (11%)
  blocking collectives  40.2 us (2%)
    psum x1, waiting for transfers between devices, on_device(): lax.psum((mod_grad_all, bias_part), ('dp', 'tensor'))  132 us
    all_gather x2, waiting for transfers between devices, attn_rows(): return lax.all_gather(values, 'tensor', axis=0, tiled=True)  117 us
    all_gather x2, waiting for transfers between devices, mlp_rows(): return lax.all_gather(values, 'tensor', axis=0, tiled=True)  116 us
    reduce_scatter x2, waiting for transfers between devices, mlp_total(): lax.psum_scatter(values.astype(jnp.bfloat16), 'tensor', scatter_dimension...  110 us
    psum x1, waiting for transfers between devices, on_device(): modulation = lax.psum(ada_part, 'dp') + bias_all[4 * D + FF:]  91.8 us
    reduce_scatter x1, waiting for transfers between devices, on_device(): lax.psum_scatter(down_wgrad.astype(jnp.bfloat16), 'dp', scatter_dimension...  72.8 us
    dot_general x5, matrix products, block_step(): jnp.einsum('qhd,khd->hqk', grad_block, block_values, preferred_element_ty...  72.2 us
    reduce_scatter x1, waiting for transfers between devices, on_device(): lax.psum_scatter(qkv_wgrad.astype(jnp.bfloat16), 'dp', scatter_dimension=...  67.5 us
  transfers between devices with their start and end apart: 20, of which 15 were waited for; matrix products, arithmetic and copies ran while one was open for 40% of the time, Pallas kernels for 0%

commit v1 on v0

v1 whole, which is shorter than its diff:
```python
import math

import jax
import jax.numpy as jnp
import numpy as np
from jax import lax
from jax.experimental import pallas as pl
from jax.experimental.pallas import tpu as pltpu
from jax.sharding import PartitionSpec as P

D = 1024
HD = 64
FF = 4096
L = 1024
STEP = 10
LANES = 128
VMEM_BYTES = 48 * 1024 * 1024


eps_norm = 1e-06
beta_one = 0.9
beta_two = 0.95
adam_eps = 1e-08
decay_rate = 0.01
highest = lax.Precision.HIGHEST
both = ("dp", "tensor")


def halo_plan(device_count, row_count):
    by_size = {}
    for dst in range(device_count):
        low = dst * row_count // L * L
        high = -(-(dst + 1) * row_count // L) * L
        for src in range(low // row_count, -(-high // row_count)):
            start = max(low, src * row_count)
            stop = min(high, (src + 1) * row_count)
            if src != dst and start < stop:
                piece = (src, dst, start - src * row_count, start - low)
                by_size.setdefault(stop - start, []).append(piece)
    rounds = []
    for size in sorted(by_size, reverse=True):
        left = by_size[size]
        while left:
            taken, later, sources, targets = [], [], set(), set()
            for piece in left:
                if piece[0] in sources or piece[1] in targets:
                    later.append(piece)
                else:
                    taken.append(piece)
                    sources.add(piece[0])
                    targets.add(piece[1])
            rounds.append((size, taken))
            left = later
    return rounds


def window_latents(device_count, row_count):
    widths = [
        -(-(i + 1) * row_count // L) - i * row_count // L for i in range(device_count)
    ]
    return max(widths)


def look_up(table, index):
    return lax.dynamic_index_in_dim(jnp.asarray(np.array(table, np.int32)), index, 0, False)


def norm_parts(values):
    center = values - jnp.mean(values, axis=-1, keepdims=True)
    spread = jnp.mean(center * center, axis=-1, keepdims=True)
    inverse = lax.rsqrt(spread + eps_norm)
    return (center * inverse, inverse)


def norm_back(normed, inverse, cotangent):
    mean_grad = jnp.mean(cotangent, axis=-1, keepdims=True)
    mean_dot = jnp.mean(cotangent * normed, axis=-1, keepdims=True)
    return inverse * (cotangent - mean_grad - normed * mean_dot)


def gelu_tanh(values):
    return jax.nn.gelu(values, approximate=True)


def adam_update(weight, gradient, first_old, second, step_rate):
    first_new = beta_one * first_old + (1.0 - beta_one) * gradient
    second_new = beta_two * second + (1.0 - beta_two) * gradient * gradient
    first_hat = first_new / (1.0 - beta_one**STEP)
    second_hat = second_new / (1.0 - beta_two**STEP)
    weight_new = weight - step_rate * (
        first_hat / (jnp.sqrt(second_hat) + adam_eps) + decay_rate * weight
    )
    return (first_new, second_new, weight_new)


def dot_nt(left, right):
    return lax.dot_general(
        left, right, (((1,), (1,)), ((), ())), preferred_element_type=jnp.float32
    )


def dot_nn(left, right):
    return lax.dot_general(
        left, right, (((1,), (0,)), ((), ())), preferred_element_type=jnp.float32
    )


def dot_tn(left, right):
    return lax.dot_general(
        left, right, (((0,), (0,)), ((), ())), preferred_element_type=jnp.float32
    )


def head_masks():
    lane = lax.broadcasted_iota(jnp.int32, (1, LANES), 1)
    low_half = (lane < HD).astype(jnp.bfloat16)
    return (low_half, (lane >= HD).astype(jnp.bfloat16))


def forward_kernel(start_ref, query_ref, key_ref, value_ref, heads_ref, log_ref):
    masks = head_masks()

    @pl.loop(0, query_ref.shape[1] // LANES)
    def pair_step(pair):
        cols = pl.ds(pl.multiple_of(pair * LANES, LANES), LANES)
        query = query_ref[:, cols] * jnp.bfloat16(HD**-0.5)
        key = key_ref[:, cols]
        value_turned = value_ref[:, cols].T
        outs = []
        for half in range(2):
            scores = dot_nt(key, query * masks[half])
            row_max = jnp.max(scores, axis=0, keepdims=True)
            weights = jnp.exp(scores - row_max)
            row_sum = jnp.sum(weights, axis=0, keepdims=True)
            out = dot_nn(
                value_turned[half * HD : (half + 1) * HD], weights.astype(jnp.bfloat16)
            )
            outs.append(out / row_sum)
            log_ref[0, 0, pl.ds(2 * pair + half, 1), :] = row_max + jnp.log(row_sum)
        heads_ref[:, cols] = jnp.concatenate(outs, axis=0).T.astype(jnp.bfloat16)


def backward_kernel(
    start_ref, query_ref, key_ref, value_ref, grad_ref, log_ref, out_ref, key_acc, value_acc
):
    step = pl.program_id(1)
    block_rows, width = query_ref.shape
    block = start_ref[0] + step
    latent = block * block_rows // L
    rows = pl.ds(pl.multiple_of(latent * L, L), L)
    own = pl.ds(pl.multiple_of(block * block_rows, block_rows), block_rows)
    masks = head_masks()

    @pl.when(step == 0)
    def clear():
        key_acc[...] = jnp.zeros_like(key_acc)
        value_acc[...] = jnp.zeros_like(value_acc)
        out_ref[:, :width] = jnp.zeros((out_ref.shape[0], width), out_ref.dtype)

    @pl.loop(0, width // LANES)
    def pair_step(pair):
        cols = pl.ds(pl.multiple_of(pair * LANES, LANES), LANES)
        query = query_ref[:, cols] * jnp.bfloat16(HD**-0.5)
        grad = grad_ref[:, cols]
        key = key_ref[:, cols]
        value = value_ref[:, cols]
        key_turned = key.T
        probs, score_grads, query_grads = [], [], []
        for half in range(2):
            scores = dot_nt(key, query * masks[half])
            prob = jnp.exp(scores - log_ref[0, 0, pl.ds(2 * pair + half, 1), :])
            weighted = prob * dot_nt(value, grad * masks[half])
            row_dot = jnp.sum(weighted, axis=0, keepdims=True)
            score_grad = (weighted - prob * row_dot).astype(jnp.bfloat16)
            query_grads.append(
                dot_nn(key_turned[half * HD : (half + 1) * HD], score_grad)
            )
            probs.append(prob.astype(jnp.bfloat16))
            score_grads.append(score_grad)
        queries = [query * mask for mask in masks]
        grads = [grad * mask for mask in masks]
        if block_rows % LANES == 0:
            probs, score_grads = (
                [jnp.concatenate(probs, axis=1)],
                [jnp.concatenate(score_grads, axis=1)],
            )
            queries, grads = (
                [jnp.concatenate(queries, axis=0)],
                [jnp.concatenate(grads, axis=0)],
            )
        value_acc[rows, cols] += sum(dot_nn(a, b) for a, b in zip(probs, grads))
        key_acc[rows, cols] += sum(dot_nn(a, b) for a, b in zip(score_grads, queries))
        turned = jnp.concatenate(query_grads, axis=0).T * HD**-0.5
        out_ref[own, cols] = turned.astype(jnp.bfloat16)

    @pl.when(step == pl.num_programs(1) - 1)
    def finish():
        out_ref[:, width : 2 * width] = key_acc[...].astype(jnp.bfloat16)
        out_ref[:, 2 * width :] = value_acc[...].astype(jnp.bfloat16)


def qkv_specs(block_rows, width):
    return [
        pl.BlockSpec((block_rows, width), lambda h, b, start: (start[0] + b, 3 * h)),
        pl.BlockSpec(
            (L, width), lambda h, b, start: ((start[0] + b) * block_rows // L, 3 * h + 1)
        ),
        pl.BlockSpec(
            (L, width), lambda h, b, start: ((start[0] + b) * block_rows // L, 3 * h + 2)
        ),
    ]


def attend_forward(qkv_ext, start_block, block_rows, block_count, chunks):
    width = D // chunks
    chunk_heads = width // HD
    cost = 4 * block_rows * block_count * L * D
    return pl.pallas_call(
        forward_kernel,
        grid_spec=pltpu.PrefetchScalarGridSpec(
            num_scalar_prefetch=1,
            grid=(chunks, block_count),
            in_specs=qkv_specs(block_rows, width),
            out_specs=[
                pl.BlockSpec((block_rows, width), lambda h, b, start: (b, h)),
                pl.BlockSpec(
                    (1, 1, chunk_heads, block_rows), lambda h, b, start: (h, b, 0, 0)
                ),
            ],
        ),
        out_shape=[
            jax.ShapeDtypeStruct((block_rows * block_count, D), jnp.bfloat16),
            jax.ShapeDtypeStruct((chunks, block_count, chunk_heads, block_rows), jnp.float32),
        ],
        compiler_params=pltpu.CompilerParams(vmem_limit_bytes=VMEM_BYTES),
        cost_estimate=pl.CostEstimate(
            flops=4 * cost, bytes_accessed=qkv_ext.size * 4, transcendentals=cost // 4 // HD
        ),
        name="attend_forward",
    )(start_block, qkv_ext, qkv_ext, qkv_ext)


def attend_backward(qkv_ext, heads_grad, log_totals, start_block, block_rows, block_count, chunks):
    width = D // chunks
    chunk_heads = width // HD
    ext_rows = qkv_ext.shape[0]
    cost = 10 * block_rows * block_count * L * D
    return pl.pallas_call(
        backward_kernel,
        grid_spec=pltpu.PrefetchScalarGridSpec(
            num_scalar_prefetch=1,
            grid=(chunks, block_count),
            in_specs=qkv_specs(block_rows, width)
            + [
                pl.BlockSpec((block_rows, width), lambda h, b, start: (b, h)),
                pl.BlockSpec(
                    (1, 1, chunk_heads, block_rows), lambda h, b, start: (h, b, 0, 0)
                ),
            ],
            out_specs=pl.BlockSpec((ext_rows, 3 * width), lambda h, b, start: (0, h)),
            scratch_shapes=[
                pltpu.VMEM((ext_rows, width), jnp.float32),
                pltpu.VMEM((ext_rows, width), jnp.float32),
            ],
        ),
        out_shape=jax.ShapeDtypeStruct((ext_rows, 3 * D), jnp.bfloat16),
        compiler_params=pltpu.CompilerParams(vmem_limit_bytes=VMEM_BYTES),
        cost_estimate=pl.CostEstimate(
            flops=4 * cost, bytes_accessed=qkv_ext.size * 6, transcendentals=cost // 10 // HD
        ),
        name="attend_backward",
    )(start_block, qkv_ext, qkv_ext, qkv_ext, heads_grad, log_totals)


def gather_columns(shard):
    tensor_count = lax.axis_size("tensor")
    whole = lax.all_gather(shard, both, axis=0, tiled=False)
    whole = whole.reshape(-1, tensor_count, *shard.shape)
    return whole.transpose(0, 2, 1, 3).reshape(D, tensor_count * shard.shape[1])


def scatter_columns(grad):
    tensor_count = lax.axis_size("tensor")
    dp_count = lax.axis_size("dp")
    columns = grad.shape[1] // tensor_count
    parts = grad.reshape(dp_count, D // dp_count, tensor_count, columns).transpose(0, 2, 1, 3)
    parts = parts.reshape(dp_count * tensor_count, D // dp_count, columns)
    summed = lax.psum_scatter(parts, both, scatter_dimension=0, tiled=False)
    return summed.astype(jnp.float32)


def on_device(
    tokens_in,
    condition,
    out_grad,
    qkv_weight,
    out_weight,
    up_weight,
    down_weight,
    ada_weight,
    bias_all,
    qkv_first,
    out_first,
    up_first,
    down_first,
    ada_first,
    bias_first,
    qkv_second,
    out_second,
    up_second,
    down_second,
    ada_second,
    bias_second,
):
    tensor_count = lax.axis_size("tensor")
    dp_count = lax.axis_size("dp")
    device_count = dp_count * tensor_count
    dp_index = lax.axis_index("dp")
    device = dp_index * tensor_count + lax.axis_index("tensor")
    row_count = tokens_in.shape[0]
    latent_count = condition.shape[0]
    width = D // tensor_count
    block_rows = math.gcd(row_count, L)
    block_count = row_count // block_rows
    rounds = halo_plan(device_count, row_count)
    window = window_latents(device_count, row_count)
    dp_window = window_latents(dp_count, row_count * tensor_count)
    first_latents = [i * row_count // L for i in range(device_count)]
    dp_latents = [i * row_count * tensor_count // L for i in range(dp_count)]
    first_latent = look_up(first_latents, device)
    start_block = look_up(
        [i * row_count % L // block_rows for i in range(device_count)], device
    )

    qkv_whole = gather_columns(qkv_weight.astype(jnp.bfloat16).reshape(-1, 3 * width))
    out_whole = gather_columns(out_weight.astype(jnp.bfloat16).T)
    up_whole = gather_columns(up_weight.astype(jnp.bfloat16))
    down_whole = gather_columns(down_weight.astype(jnp.bfloat16).T)

    cond_value = condition.astype(jnp.float32)
    silu_low = jax.nn.silu(cond_value).astype(jnp.bfloat16)
    ada_low = ada_weight.astype(jnp.bfloat16)
    picked = [
        min(first + w, latent_count - 1) for first in dp_latents for w in range(dp_window)
    ]
    silu_picked = jnp.stack([silu_low[latent] for latent in picked])
    ada_part = dot_nn(silu_picked, ada_low).reshape(dp_count, dp_window, 6 * D)
    ada_parts = lax.all_to_all(ada_part, "dp", split_axis=0, concat_axis=0, tiled=True)
    mod_dp = jnp.sum(ada_parts, axis=0) + bias_all[4 * D + FF :]
    mod_dp = jnp.concatenate([mod_dp, jnp.zeros((window, 6 * D), jnp.float32)])
    mod_window = lax.dynamic_slice_in_dim(
        mod_dp, first_latent - look_up(dp_latents, dp_index), window, 0
    )
    block_latent = (start_block + jnp.arange(block_count, dtype=jnp.int32)) * block_rows // L
    latent_pick = (
        block_latent[None, :] == jnp.arange(window, dtype=jnp.int32)[:, None]
    ).astype(jnp.float32)
    mod_blocks = jnp.sum(latent_pick[:, :, None] * mod_window[:, None, :], axis=0)
    mod_blocks = mod_blocks.reshape(block_count, 1, 6 * D)
    shift_attn, scale_attn, gate_attn, shift_mlp, scale_mlp, gate_mlp = (
        mod_blocks[:, :, i * D : (i + 1) * D] for i in range(6)
    )

    def in_blocks(values):
        return values.reshape(block_count, block_rows, -1)

    def in_rows(values):
        return values.reshape(row_count, -1)

    def latent_sums(values):
        return jnp.sum(latent_pick[:, :, None] * jnp.sum(values, axis=1)[None], axis=1)

    tokens = in_blocks(tokens_in)
    cotangent = in_blocks(out_grad)
    norm_attn, inverse_attn = norm_parts(tokens)
    attn_input = (norm_attn * (1.0 + scale_attn) + shift_attn).astype(jnp.bfloat16)

    attn_ext = jnp.zeros((window * L // block_rows, block_rows, D), jnp.bfloat16)
    places = []
    for size, pieces in rounds:
        source = [0] * device_count
        target = [i * row_count % L // block_rows for i in range(device_count)]
        for src, dst, src_row, dst_row in pieces:
            source[src] = src_row // block_rows
            target[dst] = dst_row // block_rows
        places.append((look_up(source, device), look_up(target, device)))
    for (size, pieces), (source, target) in zip(rounds, places):
        sent = lax.dynamic_slice_in_dim(attn_input, source, size // block_rows, 0)
        got = lax.ppermute(sent, both, [(piece[0], piece[1]) for piece in pieces])
        attn_ext = lax.dynamic_update_slice_in_dim(attn_ext, got, target, 0)
    attn_ext = lax.dynamic_update_slice_in_dim(attn_ext, attn_input, start_block, 0)
    attn_ext = attn_ext.reshape(window * L, D)

    bias_chunks = jnp.stack(
        [
            bias_all[:D].reshape(tensor_count, width),
            jnp.zeros((tensor_count, width), jnp.float32),
            bias_all[D : 2 * D].reshape(tensor_count, width),
        ],
        axis=1,
    ).reshape(3 * D)
    qkv_ext = (dot_nn(attn_ext, qkv_whole) + bias_chunks).astype(jnp.bfloat16)
    starts = start_block.reshape(1)
    head_low, log_totals = attend_forward(
        qkv_ext, starts, block_rows, block_count, tensor_count
    )
    attn_value = in_blocks(dot_nt(head_low, out_whole) + bias_all[2 * D : 3 * D])
    residual_mid = tokens + gate_attn * attn_value
    norm_mlp, inverse_mlp = norm_parts(residual_mid)
    mlp_low = in_rows((norm_mlp * (1.0 + scale_mlp) + shift_mlp).astype(jnp.bfloat16))
    mlp_grad = in_rows((cotangent * gate_mlp).astype(jnp.bfloat16))

    up_value = dot_nn(mlp_low, up_whole) + bias_all[3 * D : 3 * D + FF]
    hidden_low = gelu_tanh(up_value).astype(jnp.bfloat16)
    mlp_value = in_blocks(dot_nt(hidden_low, down_whole) + bias_all[3 * D + FF : 4 * D + FF])
    hidden_grad = dot_nn(mlp_grad, down_whole)
    unused, gelu_pull = jax.vjp(gelu_tanh, up_value)
    up_grad = gelu_pull(hidden_grad)[0].astype(jnp.bfloat16)
    down_wgrad = dot_tn(mlp_grad, hidden_low).astype(jnp.bfloat16)
    up_wgrad = dot_tn(mlp_low, up_grad).astype(jnp.bfloat16)
    mlp_norm_grad = in_blocks(dot_nt(up_grad, up_whole))
    block_out = in_rows(residual_mid + gate_mlp * mlp_value)
    mid_grad = cotangent + norm_back(norm_mlp, inverse_mlp, mlp_norm_grad * (1.0 + scale_mlp))
    attn_grad = in_rows((mid_grad * gate_attn).astype(jnp.bfloat16))
    out_wgrad = dot_tn(attn_grad, head_low).astype(jnp.bfloat16)
    heads_grad = dot_nn(attn_grad, out_whole).astype(jnp.bfloat16)

    early = jnp.concatenate(
        [
            jnp.sum(attn_grad.astype(jnp.float32), axis=0),
            jnp.sum(up_grad.astype(jnp.float32), axis=0),
            jnp.sum(mlp_grad.astype(jnp.float32), axis=0),
            latent_sums(mid_grad * attn_value).reshape(-1),
            latent_sums(mlp_norm_grad).reshape(-1),
            latent_sums(mlp_norm_grad * norm_mlp).reshape(-1),
            latent_sums(cotangent * mlp_value).reshape(-1),
        ]
    )
    early_all = lax.all_gather(early.reshape(-1, LANES), both, axis=0, tiled=False)
    early_all = early_all.reshape(device_count, -1)

    qkv_grad = attend_backward(
        qkv_ext, heads_grad, log_totals, starts, block_rows, block_count, tensor_count
    )
    qkv_wgrad = dot_tn(attn_ext, qkv_grad).astype(jnp.bfloat16)
    norm_grad_ext = dot_nt(qkv_grad, qkv_whole).reshape(-1, block_rows, D)
    attn_norm_grad = lax.dynamic_slice_in_dim(norm_grad_ext, start_block, block_count, 0)
    for (size, pieces), (source, target) in zip(rounds, places):
        count = size // block_rows
        sent = lax.dynamic_slice_in_dim(norm_grad_ext, target, count, 0).astype(jnp.bfloat16)
        got = lax.ppermute(sent, both, [(piece[1], piece[0]) for piece in pieces])
        old = lax.dynamic_slice_in_dim(attn_norm_grad, source, count, 0)
        attn_norm_grad = lax.dynamic_update_slice_in_dim(
            attn_norm_grad, old + got.astype(jnp.float32), source, 0
        )
    tokens_grad = in_rows(
        mid_grad + norm_back(norm_attn, inverse_attn, attn_norm_grad * (1.0 + scale_attn))
    )
    qkv_sums = jnp.sum(qkv_grad.astype(jnp.float32), axis=0).reshape(tensor_count, 3, width)
    late = jnp.concatenate(
        [
            qkv_sums[:, 0].reshape(-1),
            qkv_sums[:, 2].reshape(-1),
            latent_sums(attn_norm_grad).reshape(-1),
            latent_sums(attn_norm_grad * norm_attn).reshape(-1),
        ]
    )
    late_all = lax.all_gather(late.reshape(-1, LANES), both, axis=0, tiled=False)
    late_all = late_all.reshape(device_count, -1)

    spread = np.zeros((latent_count, device_count, window), np.float32)
    for i, first in enumerate(first_latents):
        for w in range(window):
            if first + w < latent_count:
                spread[first + w, i, w] = 1.0
    spread = jnp.asarray(spread.reshape(latent_count, -1))

    def latent_totals(gathered):
        terms = gathered.reshape(device_count * window, D)
        return jnp.dot(spread, terms, precision=highest, preferred_element_type=jnp.float32)

    early_bias = 2 * D + FF
    mod_grads = [
        latent_totals(late_all[:, 2 * D + i * window * D : 2 * D + (i + 1) * window * D])
        for i in range(2)
    ] + [
        latent_totals(
            early_all[:, early_bias + i * window * D : early_bias + (i + 1) * window * D]
        )
        for i in range(4)
    ]
    mod_grad = jnp.concatenate(mod_grads, axis=1)
    bias_grad = jnp.concatenate(
        [
            jnp.sum(late_all[:, : 2 * D], axis=0),
            jnp.sum(early_all[:, :early_bias], axis=0),
            jnp.sum(mod_grad, axis=0),
        ]
    )
    ada_wgrad = jnp.dot(
        silu_low.astype(jnp.float32).T,
        mod_grad,
        precision=highest,
        preferred_element_type=jnp.float32,
    )
    cond_inner = jnp.dot(
        mod_grad,
        ada_low.astype(jnp.float32).T,
        precision=highest,
        preferred_element_type=jnp.float32,
    )
    unused, silu_pull = jax.vjp(jax.nn.silu, cond_value)
    condition_grad = silu_pull(cond_inner)[0]
    down_summed = scatter_columns(down_wgrad).T
    up_summed = scatter_columns(up_wgrad)
    out_summed = scatter_columns(out_wgrad).T
    qkv_summed = scatter_columns(qkv_wgrad).reshape(qkv_weight.shape)
    qkv_new = adam_update(qkv_weight, qkv_summed, qkv_first, qkv_second, 3.0 / math.sqrt(D))
    out_new = adam_update(out_weight, out_summed, out_first, out_second, 3.0 / math.sqrt(D // 4))
    up_new = adam_update(up_weight, up_summed, up_first, up_second, 3.0 / math.sqrt(D))
    down_new = adam_update(down_weight, down_summed, down_first, down_second, 3.0 / math.sqrt(FF))
    ada_new = adam_update(ada_weight, ada_wgrad, ada_first, ada_second, 3.0 / math.sqrt(D))
    bias_new = adam_update(bias_all, bias_grad, bias_first, bias_second, 0.9)
    return (
        block_out,
        tokens_grad,
        condition_grad,
        *qkv_new,
        *out_new,
        *up_new,
        *down_new,
        *ada_new,
        *bias_new,
    )


def solution(mesh):
    weights = (
        P("dp", None, "tensor"),
        P("tensor", "dp"),
        P("dp", "tensor"),
        P("tensor", "dp"),
        P("dp", None),
        P(),
    )
    tokens = P(both, None)
    return jax.shard_map(
        on_device,
        mesh=mesh,
        in_specs=(tokens, P(None, "dp"), tokens, *weights, *weights, *weights),
        out_specs=(tokens, tokens, P(None, "dp"))
        + tuple(spec for spec in weights for unused in range(3)),
        check_vma=False,
    )
```

time: 1870 us -> 1390 us (0.74)
  waiting for transfers between devices: 907 us -> 578 us
  matrix products: 421 us -> 215 us
  Pallas kernels: 0 us -> 159 us
  other arithmetic: 204 us -> 70.2 us
  blocking collectives: 40.2 us -> 72.5 us
  local copies, waits for them, and re-layouts: 261 us -> 233 us
  starting transfers between devices: 1.17 us -> 26 us
    all_gather x8 -> x5, waiting for transfers between devices: 366 us -> 90.3 us  [the longest x4 90.3 us: gather_columns(): whole = lax.all_gather(shard, both, axis=0, tiled=False)]
    psum x2 -> x0, waiting for transfers between devices: 223 us -> none  [the longest x1 132 us: on_device(): lax.psum((mod_grad_all, bias_part), ('dp', 'tensor'))]
    dot_general x50 -> x19, matrix products: 412 us -> 206 us  [the longest x5 71.2 us: dot_nn(): lax.dot_general(left, right, (((1,), (0,)), ((), ())), preferred_element_...]
    pallas_call x0 -> x2, Pallas kernels: none -> 159 us  [the longest x1 90.3 us: attend_backward(): pl.pallas_call(backward_kernel, grid_spec=pltpu.PrefetchScalarGridSpec(nu...]
    reduce_scatter x8 -> x4, waiting for transfers between devices: 317 us -> 451 us  [scatter_columns(): summed = lax.psum_scatter(parts, both, scatter_dimension=0, tiled=False)]
    reshape x1 -> x18, local copies, waits for them, and re-layouts: 4.61 us -> 128 us  [the longest x5 54.2 us: scatter_columns(): grad.reshape(dp_count, D // dp_count, tensor_count, columns)]
    dynamic_slice x48 -> x14, local copies, waits for them, and re-layouts: 91 us -> 10.6 us  [the longest x9 5.28 us: look_up(): lax.dynamic_index_in_dim(jnp.asarray(np.array(table, np.int32)), index, 0...]
    all_gather x0 -> x1, blocking collectives: none -> 72.5 us  [on_device(): lax.all_gather(late.reshape(-1, LANES), both, axis=0, tiled=False)]
  transfers between devices with their start and end apart: 20 -> 16, of which waited for: 15 -> 7; matrix products, arithmetic and copies ran while one was open for 40% -> 20% of each run, Pallas kernels for 0% -> 5%
where the time goes in v1:
time: 1390 us; the launch traced here: 1380 us
  waiting for transfers between devices  578 us (42%)
  local copies, waits for them, and re-layouts  233 us (17%)
  matrix products  215 us (15%)
  Pallas kernels  159 us (11%)
  blocking collectives  72.5 us (5%)
  other arithmetic  70.2 us (5%)
  between operations  30.1 us (2%)
  starting transfers between devices  26 us (2%)
    reduce_scatter x4, waiting for transfers between devices, scatter_columns(): summed = lax.psum_scatter(parts, both, scatter_dimension=0, tiled=False)  451 us
    all_gather x4, waiting for transfers between devices, gather_columns(): whole = lax.all_gather(shard, both, axis=0, tiled=False)  90.3 us
    pallas_call x1, Pallas kernels, attend_backward(): pl.pallas_call(backward_kernel, grid_spec=pltpu.PrefetchScalarGridSpec(nu...  90.3 us
    all_gather x1, blocking collectives, on_device(): lax.all_gather(late.reshape(-1, LANES), both, axis=0, tiled=False)  72.5 us
    dot_general x5, matrix products, dot_nn(): lax.dot_general(left, right, (((1,), (0,)), ((), ())), preferred_element_...  71.2 us
    pallas_call x1, Pallas kernels, attend_forward(): pl.pallas_call(forward_kernel, grid_spec=pltpu.PrefetchScalarGridSpec(num...  68.5 us
    dot_general x4, matrix products, dot_nt(): lax.dot_general(left, right, (((1,), (1,)), ((), ())), preferred_element_...  64.8 us
    dot_general x4, matrix products, dot_tn(): lax.dot_general(left, right, (((0,), (0,)), ((), ())), preferred_element_...  60.1 us
  transfers between devices with their start and end apart: 16, of which 7 were waited for; matrix products, arithmetic and copies ran while one was open for 20% of the time, Pallas kernels for 5%

profile of v1, /device:TPU:0, one launch (start us, length us, event | category | flops | bytes accessed | tf_op | source)
XLA Modules:
  0.0 1382.6 jit_solution(440706975901103655)
XLA Ops:
  37.2 22.8 %all-to-all-done = f32[16,3,6144]{2,1,0:T(4,128)S(1)} async-done(((f32[16,3,6144]{2,1,0:T(4,128)}), f32[16,3,6144]{2,1,0:T(4,128)S(1)}, u32[]{:S(2)}, u32[]{:S(2)}) %all-to-all-start) | async-done | bytes 1179680 | tf_op jit(solution)/shard_map/all_to_all | solution.py:348
  114.6 41.2 %all-gather.9.cloned.1.call-done = bf16[32,64,1536]{2,1,0:T(8,128)(2,1)} async-done(((bf16[1,64,1536]{2,1,0:T(8,128)(2,1)}), bf16[32,64,1536]{2,1,0:T(8,128)(2,1)}) %all-gather.9.cloned.1.call-update) | async-done | bytes 6291472 | tf_op jit(solution)/shard_map/all_gather | solution.py:277
  155.8 11.8 copy.105
  173.2 19.3 %add_convert_fusion.query_ref.key_ref.value_ref = bf16[2048,3072]{1,0:T(8,128)(2,1)} fusion(bf16[2048,1024]{1,0:T(8,128)(2,1)} %bitcast.14, bf16[1024,3072]{1,0:T(8,128)(2,1)} %bitcast.244, f32[3072]{0:T(1024)S(1)} %add.326), kind=kOutput, calls=%fused_computation.3 | convolution fusion | flops 12897484800 | bytes 23080960 | tf_op jit(solution)/shard_map/dot_general | solution.py:103
  192.5 68.5 %attend_forward.1 = (bf16[1280,1024]{1,0:T(8,128)(2,1)S(1)}, f32[2,5,8,256]{3,2,1,0:T(8,128)S(1)}) custom-call(s32[1]{0:T(128)} %dynamic_slice.65.start_ref, bf16[2048,3072]{1,0:T(8,128)(2,1)} %add_convert_fusion.query_ref.key_ref.value_ref, bf16[2048,3072]{1,0:T(8,128)(2,1)} %add_convert_fusion.query_ref.key_ref.value_ref, ...), custom_call_target="tpu_custom_call" | custom-call | flops 21474836480 | bytes 25165824 | tf_op jit(solution)/shard_map/attend_forward/pallas_call | solution.py:218
  272.4 16.3 %copy.146 = bf16[16,2,64,2048]{3,1,2,0:T(2,128)(2,1)} copy(bf16[16,2,64,2048]{3,2,1,0:T(8,128)(2,1)} %bitcast.231) | data formatting | bytes 16777216 | tf_op jit(solution)/shard_map/reshape | solution.py:278
  288.7 12.2 copy.118
  300.9 18.0 %fusion.57 = f32[1280,4096]{1,0:T(8,128)} fusion(bf16[1280,1024]{1,0:T(8,128)(2,1)S(1)} %copy-done.10, bf16[1024,4096]{1,0:T(8,128)(2,1)} %bitcast.233), kind=kOutput, calls=%fused_computation.168 | convolution fusion | flops 10737418240 | bytes 31981568 | tf_op jit(solution)/shard_map/dot_general | solution.py:103
  318.9 17.9 %convolution_convert_fusion = bf16[1024,4096]{1,0:T(8,128)(2,1)} fusion(bf16[1280,1024]{1,0:T(8,128)(2,1)S(1)} %copy-done.8, f32[1280,4096]{1,0:T(8,128)} %fusion.57, f32[4096]{0:T(1024)S(1)} %slice.182), kind=kOutput, calls=%fused_computation.15 | convolution fusion | flops 10794041344 | bytes 31997952 | tf_op jit(solution)/shard_map/dot_general | solution.py:109
  336.8 14.6 %reshape.373 = bf16[16,64,2,2048]{3,2,1,0:T(2,128)(2,1)} reshape(bf16[1024,4096]{1,0:T(8,128)(2,1)} %convolution_convert_fusion) | data formatting | bytes 16777216 | tf_op jit(solution)/shard_map/reshape | solution.py:286
  351.4 10.6 copy.115
  362.0 181.8 %reduce-scatter.11.cloned.1.call-done = bf16[1,64,2048]{2,1,0:T(8,128)(2,1)} async-done(((bf16[32,64,2048]{2,1,0:T(8,128)(2,1)}), bf16[1,64,2048]{2,1,0:T(8,128)(2,1)}) %reduce-scatter.11.cloned.1.call-update) | async-done | bytes 262160 | tf_op jit(solution)/shard_map/reduce_scatter | solution.py:288
  546.6 14.9 %reshape.386 = bf16[1024,3072,1]{1,0,2:T(8,128)(2,1)} reshape(bf16[16,64,2,1536]{3,2,1,0:T(2,128)(2,1)} %copy-done.3) | data formatting | bytes 12582912 | tf_op jit(solution)/shard_map/reshape | solution.py:279
  561.5 14.5 %reshape.385 = bf16[1024,4096,1]{1,0,2:T(8,128)(2,1)} reshape(bf16[16,64,2,2048]{3,2,1,0:T(2,128)(2,1)} %bitcast.212) | data formatting | bytes 16777216 | tf_op jit(solution)/shard_map/reshape | solution.py:279
  576.0 49.1 %all-gather.17.cloned.1.call-done = bf16[2048,2048]{1,0:T(8,128)(2,1)} async-done(((bf16[64,2048]{1,0:T(8,128)(2,1)}), bf16[2048,2048]{1,0:T(8,128)(2,1)}) %all-gather.17.cloned.1.call-update) | async-done | bytes 8388624 | tf_op jit(solution)/shard_map/all_gather | solution.py:277
  625.1 16.3 %copy.108 = bf16[16,2,64,2048]{3,1,2,0:T(2,128)(2,1)} copy(bf16[16,2,64,2048]{3,2,1,0:T(8,128)(2,1)} %bitcast.232) | data formatting | bytes 16777216 | tf_op jit(solution)/shard_map/reshape | solution.py:278
  641.4 12.2 copy.119
  653.6 29.1 %convert_reduce_fusion.1 = (f32[4096]{0:T(1024)S(1)}, bf16[1280,4096]{1,0:T(8,128)(2,1)}) fusion(f32[1280,4096]{1,0:T(8,128)} %fusion.57, f32[4096]{0:T(1024)S(1)} %slice.182, bf16[1280,1024]{1,0:T(8,128)(2,1)S(1)} %copy-done.8, bf16[1024,4096]{1,0:T(8,128)(2,1)} %bitcast.219), kind=kOutput, calls=%fused_computation.11 | convolution fusion | flops 10858000384 | bytes 42500096 | tf_op jit(solution)/shard_map/dot_general | solution.py:103
  682.7 20.6 %fusion.7 = (f32[1280,1024]{1,0:T(8,128)}, f32[1280,1024]{1,0:T(8,128)}) fusion(f32[1280,1024]{1,0:T(8,128)S(1)} %bitcast.210, f32[5,1024]{1,0:T(8,128)S(1)} %copy-done.21, f32[1024]{0:T(1024)S(1)} %copy-done.35, bf16[1024,4096]{1,0:T(8,128)(2,1)} %bitcast.220, f32[1280,4096]{1,0:T(8,128)} %fusion.57, f32[4096]{0:T(1024)S(1)} %slice.182), kind=kOutput, calls=%fused_computation.18 | convolution fusion | flops 10793779200 | bytes 45129728 | tf_op jit(solution)/shard_map/dot_general | solution.py:97
  703.3 21.7 %multiply_reduce_fusion.1 = (f32[5,1024]{1,0:T(8,128)S(1)}, f32[5,256]{1,0:T(8,128)S(1)}, f32[5,256]{1,0:T(8,128)S(1)}, f32[5,1024]{1,0:T(8,128)S(1)}, f32[5,256,1024]{2,1,0:T(8,128)}, /*index=5*/f32[5,256,1024]{2,1,0:T(8,128)}) fusion(f32[5,1024]{1,0:T(8,128)S(1)} %get-tuple-element.145, f32[5,256]{1,0:T(8,128)S(1)} %rsqrt.26, f32[5,256]{1,0:T(8,128)S(1)} %div.147, ...), kind=kOutput, calls=%fused_computation.26 | convolution fusion | flops 10751823872 | bytes 39948288 | tf_op jit(solution)/shard_map/dot_general | solution.py:97
  725.0 11.0 convert_reduce_fusion.3
  739.2 90.3 %attend_backward.1 = bf16[2048,3072]{1,0:T(8,128)(2,1)} custom-call(s32[1]{0:T(128)} %dynamic_slice.65.start_ref, bf16[2048,3072]{1,0:T(8,128)(2,1)} %add_convert_fusion.query_ref.key_ref.value_ref, bf16[2048,3072]{1,0:T(8,128)(2,1)} %add_convert_fusion.query_ref.key_ref.value_ref, bf16[2048,3072]{1,0:T(8,128)(2,1)} %add_convert_fusion.query_ref.key_ref.value_ref, ...), custom_call_target="tpu_custom_call" | custom-call | flops 53687091200 | bytes 37748736 | tf_op jit(solution)/shard_map/attend_backward/pallas_call | solution.py:248
  829.5 16.4 %fusion.58 = f32[8,256,1024]{2,1,0:T(8,128)S(1)} fusion(bf16[8,256,3072]{2,1,0:T(8,128)(2,1)} %bitcast.230, bf16[1024,3072,1]{1,0,2:T(8,128)(2,1)S(1)} %bitcast.243), kind=kOutput, calls=%fused_computation.169 | convolution fusion | flops 12884901888 | bytes 27262976 | tf_op jit(solution)/shard_map/dot_general | solution.py:97
  876.0 13.1 collective-permute-done.3
  902.2 18.7 %convolution_convert_fusion.2 = bf16[1024,3072]{1,0:T(8,128)(2,1)} fusion(bf16[2048,1024]{1,0:T(8,128)(2,1)} %bitcast.14, bf16[2048,3072]{1,0:T(8,128)(2,1)} %attend_backward.1), kind=kOutput, calls=%fused_computation.17 | convolution fusion | flops 12888047616 | bytes 23068672 | tf_op jit(solution)/shard_map/dot_general | solution.py:109
  920.9 14.9 %reshape.367 = bf16[16,64,2,1536]{3,2,1,0:T(2,128)(2,1)} reshape(bf16[1024,3072]{1,0:T(8,128)(2,1)} %convolution_convert_fusion.2) | data formatting | bytes 12582912 | tf_op jit(solution)/shard_map/reshape | solution.py:286
  944.5 17.6 %convolution_convert_fusion.1 = bf16[1024,4096]{1,0:T(8,128)(2,1)} fusion(bf16[1280,1024]{1,0:T(8,128)(2,1)S(1)} %copy-done.11, bf16[1280,4096]{1,0:T(8,128)(2,1)} %get-tuple-element.123), kind=kOutput, calls=%fused_computation.16 | convolution fusion | flops 10741612544 | bytes 21495808 | tf_op jit(solution)/shard_map/dot_general | solution.py:109
  962.1 14.5 %reshape.371 = bf16[16,64,2,2048]{3,2,1,0:T(2,128)(2,1)} reshape(bf16[1024,4096]{1,0:T(8,128)(2,1)} %convolution_convert_fusion.1) | data formatting | bytes 16777216 | tf_op jit(solution)/shard_map/reshape | solution.py:286
  976.6 10.6 copy.114
  993.8 72.5 %all_gather.34 = f32[32,48,128]{2,1,0:T(8,128)S(1)} all-gather(f32[1,48,128]{2,1,0:T(8,128)S(1)} %maximum_bitcast_fusion), channel_id=1, replica_groups=mesh['dp'=16,'tensor'=2] {'dp','tensor'}, dimensions={0}, use_global_device_ids=true | all-gather | bytes 811008 | tf_op jit(solution)/shard_map/all_gather | solution.py:468
  1100.2 88.4 %reduce-scatter.5.cloned.1.call-done = bf16[1,64,1536]{2,1,0:T(8,128)(2,1)} async-done(((bf16[32,64,1536]{2,1,0:T(8,128)(2,1)}), bf16[1,64,1536]{2,1,0:T(8,128)(2,1)}) %reduce-scatter.5.cloned.1.call-update) | async-done | bytes 196624 | tf_op jit(solution)/shard_map/reduce_scatter | solution.py:288
  1192.2 181.1 %reduce-scatter.9.cloned.1.call-done = bf16[1,64,2048]{2,1,0:T(8,128)(2,1)} async-done(((bf16[32,64,2048]{2,1,0:T(8,128)(2,1)}), bf16[1,64,2048]{2,1,0:T(8,128)(2,1)}) %reduce-scatter.9.cloned.1.call-update) | async-done | bytes 262160 | tf_op jit(solution)/shard_map/reduce_scatter | solution.py:288
  (276 shorter events, 190.1 us)
Async XLA Ops:
  7.2 103.0 %all-gather.13.cloned.1.call-start = ((), (), s32[]{:S(2)}) async-start(), calls=%async_computation.11 | async-start | bytes 2162688 | tf_op jit(solution)/shard_map/all_gather | solution.py:277
  8.8 147.0 %all-gather.9.cloned.1.call-start = ((), (), s32[]{:S(2)}) async-start(), calls=%async_computation.5 | async-start | bytes 6488064 | tf_op jit(solution)/shard_map/all_gather | solution.py:277
  11.1 261.4 %all-gather.15.cloned.1.call-start = ((), (), s32[]{:S(2)}) async-start(), calls=%async_computation.12 | async-start | bytes 8650752 | tf_op jit(solution)/shard_map/all_gather | solution.py:277
  17.3 42.6 %all-to-all-start = ((f32[16,3,6144]{2,1,0:T(4,128)}), f32[16,3,6144]{2,1,0:T(4,128)S(1)}, u32[]{:S(2)}, u32[]{:S(2)}) async-start(f32[16,3,6144]{2,1,0:T(4,128)} %reshape.335), calls=%async_computation | async-start | bytes 3145728 | tf_op jit(solution)/shard_map/all_to_all | solution.py:348
  24.7 519.0 %reduce-scatter.11.cloned.1.call-start = ((), (), s32[]{:S(2)}) async-start(), calls=%async_computation.10 | async-start | bytes 8650752 | tf_op jit(solution)/shard_map/reduce_scatter | solution.py:288
  32.6 74.5 %copy-start.24 = (f32[5,256]{1,0:T(8,128)}, f32[5,256]{1,0:T(8,128)S(1)}, u32[]{:S(2)}) copy-start(f32[5,256]{1,0:T(8,128)S(1)} %div.142) | copy-start | bytes 15364
  35.8 71.3 %copy-start.26 = (f32[5,256]{1,0:T(8,128)}, f32[5,256]{1,0:T(8,128)S(1)}, u32[]{:S(2)}) copy-start(f32[5,256]{1,0:T(8,128)S(1)} %rsqrt.24) | copy-start | bytes 15364
  60.8 46.3 %copy-start.14 = (f32[5,1024]{1,0:T(8,128)}, f32[5,1024]{1,0:T(8,128)S(1)}, u32[]{:S(2)}) copy-start(f32[5,1024]{1,0:T(8,128)S(1)} %get-tuple-element.147) | copy-start | bytes 61444
  65.5 33.0 %collective-permute-start = (bf16[3,256,1024]{2,1,0:T(8,128)(2,1)}, bf16[3,256,1024]{2,1,0:T(8,128)(2,1)}, u32[]{:S(2)}, u32[]{:S(2)}) collective-permute-start(bf16[3,256,1024]{2,1,0:T(8,128)(2,1)} %constant_dynamic-slice_fusion.3), channel_id=1, source_target_pairs={{1,0},{2,3},{5,4},{6,7},{9,8},{10,11},{13,12},{14,15},{17,16},{18,... | collective-permute-start | bytes 4718600 | tf_op jit(solution)/shard_map/ppermute | solution.py:389
  70.4 33.6 %collective-permute-start.1 = (bf16[2,256,1024]{2,1,0:T(8,128)(2,1)}, bf16[2,256,1024]{2,1,0:T(8,128)(2,1)}, u32[]{:S(2)}, u32[]{:S(2)}) collective-permute-start(bf16[2,256,1024]{2,1,0:T(8,128)(2,1)} %constant_dynamic-slice_fusion.2), channel_id=1, source_target_pairs={{2,1},{1,2},{6,5},{5,6},{10,9},{9,10},{14,13},{13,14},{18,17},{17,... | collective-permute-start | bytes 3145736 | tf_op jit(solution)/shard_map/ppermute | solution.py:389
  74.6 31.6 %collective-permute-start.2 = (bf16[1,256,1024]{2,1,0:T(8,128)(2,1)S(1)}, bf16[1,256,1024]{2,1,0:T(8,128)(2,1)S(1)}, u32[]{:S(2)}, u32[]{:S(2)}) collective-permute-start(bf16[1,256,1024]{2,1,0:T(8,128)(2,1)S(1)} %constant_dynamic-slice_fusion.1), channel_id=1, source_target_pairs={{0,1},{3,2},{4,5},{7,6},{8,9},{11,10},{12,13},{15,14},{16,17},{19,... | collective-permute-start | bytes 1572872 | tf_op jit(solution)/shard_map/ppermute | solution.py:389
  114.6 146.5 %copy-start.5 = (bf16[128,8,2,512]{3,1,2,0:T(8,128)(2,1)}, bf16[128,8,2,512]{3,1,2,0:T(8,128)(2,1)S(1)}, u32[]{:S(2)}) copy-start(bf16[128,8,2,512]{3,1,2,0:T(8,128)(2,1)S(1)} %copy.117) | copy-start | bytes 6291460
  167.7 93.4 %slice-start.2 = ((s8[5242880]{0:T(1024)(128)(4,1)}), s8[4194304]{0:T(1024)(128)(4,1)S(1)}, s32[]{:S(2)}) async-start(s8[5242880]{0:T(1024)(128)(4,1)} %bitcast.203), calls=%async_computation.16 | async-start | bytes 8388608
  173.2 87.9 %slice-start.3 = ((s8[5242880]{0:T(1024)(128)(4,1)}), s8[1048576]{0:T(1024)(128)(4,1)S(1)}, s32[]{:S(2)}) async-start(s8[5242880]{0:T(1024)(128)(4,1)} %bitcast.203), calls=%async_computation.17 | async-start | bytes 2097152
  361.9 181.8 %copy-start.17 = (f32[2048,64]{0,1:T(8,128)S(1)}, f32[2048,64]{0,1:T(8,128)}, u32[]{:S(2)}) copy-start(f32[2048,64]{0,1:T(8,128)} %param.37) | copy-start | bytes 1572868
  362.0 263.2 %all-gather.17.cloned.1.call-start = ((), (), s32[]{:S(2)}) async-start(), calls=%async_computation.13 | async-start | bytes 8650752 | tf_op jit(solution)/shard_map/all_gather | solution.py:277
  546.5 522.1 %reduce-scatter.7.cloned.1.call-start = ((), (), s32[]{:S(2)}) async-start(), calls=%async_computation.8 | async-start | bytes 2162688 | tf_op jit(solution)/shard_map/reduce_scatter | solution.py:288
  736.1 93.4 %slice-start.12 = ((s8[6291456]{0:T(1024)(128)(4,1)}), s8[4194304]{0:T(1024)(128)(4,1)S(1)}, s32[]{:S(2)}) async-start(s8[6291456]{0:T(1024)(128)(4,1)} %bitcast.242), calls=%async_computation.26 | async-start | bytes 8388608
  739.2 90.3 %slice-start.13 = ((s8[6291456]{0:T(1024)(128)(4,1)}), s8[2097152]{0:T(1024)(128)(4,1)S(1)}, s32[]{:S(2)}) async-start(s8[6291456]{0:T(1024)(128)(4,1)} %bitcast.242), calls=%async_computation.27 | async-start | bytes 4194304
  850.5 38.6 %collective-permute-start.3 = (bf16[3,256,1024]{2,1,0:T(8,128)(2,1)}, bf16[3,256,1024]{2,1,0:T(8,128)(2,1)}, u32[]{:S(2)}, u32[]{:S(2)}) collective-permute-start(bf16[3,256,1024]{2,1,0:T(8,128)(2,1)} %dynamic-slice_convert_fusion), channel_id=1, source_target_pairs={{0,1},{3,2},{4,5},{7,6},{8,9},{11,10},{12,13},{15,14},{16,17},{19,... | collective-permute-start | bytes 4718600 | tf_op jit(solution)/shard_map/ppermute | solution.py:451
  857.7 34.6 %collective-permute-start.4 = (bf16[2,256,1024]{2,1,0:T(8,128)(2,1)}, bf16[2,256,1024]{2,1,0:T(8,128)(2,1)}, u32[]{:S(2)}, u32[]{:S(2)}) collective-permute-start(bf16[2,256,1024]{2,1,0:T(8,128)(2,1)} %dynamic-slice_convert_fusion.1), channel_id=1, source_target_pairs={{1,2},{2,1},{5,6},{6,5},{9,10},{10,9},{13,14},{14,13},{17,18},{18,... | collective-permute-start | bytes 3145736 | tf_op jit(solution)/shard_map/ppermute | solution.py:451
  866.6 27.7 %collective-permute-start.5 = (bf16[1,256,1024]{2,1,0:T(8,128)(2,1)S(1)}, bf16[1,256,1024]{2,1,0:T(8,128)(2,1)S(1)}, u32[]{:S(2)}, u32[]{:S(2)}) collective-permute-start(bf16[1,256,1024]{2,1,0:T(8,128)(2,1)S(1)} %dynamic-slice_convert_fusion.2), channel_id=1, source_target_pairs={{1,0},{2,3},{5,4},{6,7},{9,8},{10,11},{13,12},{14,15},{17,16},{18,... | collective-permute-start | bytes 1572872 | tf_op jit(solution)/shard_map/ppermute | solution.py:451
  873.0 197.4 %all-gather.11.cloned.1.call-start = ((), (), s32[]{:S(2)}) async-start(), calls=%async_computation.6 | async-start | bytes 1892352 | tf_op jit(solution)/shard_map/all_gather | solution.py:439
  902.2 286.4 %reduce-scatter.5.cloned.1.call-start = ((), (), s32[]{:S(2)}) async-start(), calls=%async_computation.7 | async-start | bytes 6488064 | tf_op jit(solution)/shard_map/reduce_scatter | solution.py:288
  942.8 430.5 %reduce-scatter.9.cloned.1.call-start = ((), (), s32[]{:S(2)}) async-start(), calls=%async_computation.9 | async-start | bytes 8650752 | tf_op jit(solution)/shard_map/reduce_scatter | solution.py:288
  987.2 79.5 %copy-start.16 = (f32[40,64]{1,0:T(8,128)S(1)}, f32[40,64]{1,0:T(8,128)}, u32[]{:S(2)}) copy-start(f32[40,64]{1,0:T(8,128)} %constant.211.clone) | copy-start | bytes 30724
  993.8 74.9 %copy-start.18 = (f32[512,64]{0,1:T(8,128)S(1)}, f32[512,64]{0,1:T(8,128)}, u32[]{:S(2)}) copy-start(f32[512,64]{0,1:T(8,128)} %param.35) | copy-start | bytes 393220
  993.8 74.9 %copy-start.28 = (f32[512,64]{0,1:T(8,128)S(1)}, f32[512,64]{0,1:T(8,128)}, u32[]{:S(2)}) copy-start(f32[512,64]{0,1:T(8,128)} %param.47) | copy-start | bytes 393220
  993.8 74.9 %copy-start.29 = (f32[512,64]{0,1:T(8,128)S(1)}, f32[512,64]{0,1:T(8,128)}, u32[]{:S(2)}) copy-start(f32[512,64]{0,1:T(8,128)} %param.41) | copy-start | bytes 393220
  1093.5 96.3 %copy-start.13 = (f32[64,3,512]{2,0,1:T(8,128)S(1)}, f32[64,3,512]{2,0,1:T(8,128)}, u32[]{:S(2)}) copy-start(f32[64,3,512]{2,0,1:T(8,128)} %param.34) | copy-start | bytes 1179652
  1093.5 96.3 %copy-start.19 = (f32[64,3,512]{2,0,1:T(8,128)S(1)}, f32[64,3,512]{2,0,1:T(8,128)}, u32[]{:S(2)}) copy-start(f32[64,3,512]{2,0,1:T(8,128)} %param.46) | copy-start | bytes 1179652
  1093.5 279.7 %copy-start.12 = (f32[64,2048]{1,0:T(8,128)S(1)}, f32[64,2048]{1,0:T(8,128)}, u32[]{:S(2)}) copy-start(f32[64,2048]{1,0:T(8,128)} %param.36) | copy-start | bytes 1572868
  (44 other events, 587.0 us)
Sparse Core Ops, SparseCore 0:
  11.7 71.0 all-gather.12
  86.2 69.5 all-gather.8
  159.5 76.1 all-gather.14
  362.1 181.6 reduce-scatter.10
  547.3 77.8 all-gather.16
  873.1 136.6 reduce-scatter.6
  1013.7 53.9 all-gather.10
  1074.2 114.2 reduce-scatter.4
  1190.9 182.3 reduce-scatter.8

commit v2 on v1

v2 whole, which is shorter than its diff:
```python
import math

import jax
import jax.numpy as jnp
import numpy as np
from jax import lax
from jax.experimental import pallas as pl
from jax.experimental.pallas import tpu as pltpu
from jax.sharding import PartitionSpec as P

D = 1024
HD = 64
FF = 4096
L = 1024
STEP = 10
LANES = 128
VMEM_BYTES = 48 * 1024 * 1024


eps_norm = 1e-06
beta_one = 0.9
beta_two = 0.95
adam_eps = 1e-08
decay_rate = 0.01
highest = lax.Precision.HIGHEST
both = ("dp", "tensor")


def halo_plan(device_count, row_count):
    by_size = {}
    for dst in range(device_count):
        low = dst * row_count // L * L
        high = -(-(dst + 1) * row_count // L) * L
        for src in range(low // row_count, -(-high // row_count)):
            start = max(low, src * row_count)
            stop = min(high, (src + 1) * row_count)
            if src != dst and start < stop:
                piece = (src, dst, start - src * row_count, start - low)
                by_size.setdefault(stop - start, []).append(piece)
    rounds = []
    for size in sorted(by_size, reverse=True):
        left = by_size[size]
        while left:
            taken, later, sources, targets = [], [], set(), set()
            for piece in left:
                if piece[0] in sources or piece[1] in targets:
                    later.append(piece)
                else:
                    taken.append(piece)
                    sources.add(piece[0])
                    targets.add(piece[1])
            rounds.append((size, taken))
            left = later
    return rounds


def window_latents(device_count, row_count):
    widths = [
        -(-(i + 1) * row_count // L) - i * row_count // L for i in range(device_count)
    ]
    return max(widths)


def look_up(table, index):
    return lax.dynamic_index_in_dim(jnp.asarray(np.array(table, np.int32)), index, 0, False)


def norm_parts(values):
    center = values - jnp.mean(values, axis=-1, keepdims=True)
    spread = jnp.mean(center * center, axis=-1, keepdims=True)
    inverse = lax.rsqrt(spread + eps_norm)
    return (center * inverse, inverse)


def norm_back(normed, inverse, cotangent):
    mean_grad = jnp.mean(cotangent, axis=-1, keepdims=True)
    mean_dot = jnp.mean(cotangent * normed, axis=-1, keepdims=True)
    return inverse * (cotangent - mean_grad - normed * mean_dot)


def gelu_tanh(values):
    return jax.nn.gelu(values, approximate=True)


def adam_update(weight, gradient, first_old, second, step_rate):
    first_new = beta_one * first_old + (1.0 - beta_one) * gradient
    second_new = beta_two * second + (1.0 - beta_two) * gradient * gradient
    first_hat = first_new / (1.0 - beta_one**STEP)
    second_hat = second_new / (1.0 - beta_two**STEP)
    weight_new = weight - step_rate * (
        first_hat / (jnp.sqrt(second_hat) + adam_eps) + decay_rate * weight
    )
    return (first_new, second_new, weight_new)


def dot_nt(left, right):
    return lax.dot_general(
        left, right, (((1,), (1,)), ((), ())), preferred_element_type=jnp.float32
    )


def dot_nn(left, right):
    return lax.dot_general(
        left, right, (((1,), (0,)), ((), ())), preferred_element_type=jnp.float32
    )


def dot_tn(left, right):
    return lax.dot_general(
        left, right, (((0,), (0,)), ((), ())), preferred_element_type=jnp.float32
    )


def head_masks():
    lane = lax.broadcasted_iota(jnp.int32, (1, LANES), 1)
    low_half = (lane < HD).astype(jnp.bfloat16)
    return (low_half, (lane >= HD).astype(jnp.bfloat16))


def forward_kernel(start_ref, query_ref, key_ref, value_ref, heads_ref, log_ref):
    masks = head_masks()
    pairs = query_ref.shape[1] // LANES
    group = 2 if pairs % 2 == 0 else 1

    @pl.loop(0, pairs // group)
    def group_step(step):
        scores, turned = [], []
        for i in range(group):
            cols = pl.ds(pl.multiple_of((step * group + i) * LANES, LANES), LANES)
            query = query_ref[:, cols] * jnp.bfloat16(HD**-0.5)
            scores += [dot_nt(key_ref[:, cols], query * mask) for mask in masks]
            turned.append(value_ref[:, cols].T)
        for i in range(group):
            pair = step * group + i
            outs = []
            for half in range(2):
                score = scores[2 * i + half]
                row_max = jnp.max(score, axis=0, keepdims=True)
                weights = jnp.exp(score - row_max)
                row_sum = jnp.sum(weights, axis=0, keepdims=True)
                out = dot_nn(
                    turned[i][half * HD : (half + 1) * HD], weights.astype(jnp.bfloat16)
                )
                outs.append(out / row_sum)
                log_ref[0, pl.ds(2 * pair + half, 1), :] = row_max + jnp.log(row_sum)
            cols = pl.ds(pl.multiple_of(pair * LANES, LANES), LANES)
            heads_ref[:, cols] = jnp.concatenate(outs, axis=0).T.astype(jnp.bfloat16)


def backward_kernel(
    start_ref,
    query_ref,
    key_ref,
    value_ref,
    heads_ref,
    grad_ref,
    log_ref,
    out_ref,
    key_acc,
    value_acc,
):
    step = pl.program_id(0)
    block_rows, width = query_ref.shape
    block = start_ref[0] + step
    latent = block * block_rows // L
    own = pl.ds(pl.multiple_of(block * block_rows, block_rows), block_rows)
    masks = head_masks()
    key_rows = L // 2

    @pl.when(step == 0)
    def clear():
        key_acc[...] = jnp.zeros_like(key_acc)
        value_acc[...] = jnp.zeros_like(value_acc)
        out_ref[:, :width] = jnp.zeros((out_ref.shape[0], width), out_ref.dtype)

    @pl.loop(0, width // LANES)
    def pair_step(pair):
        cols = pl.ds(pl.multiple_of(pair * LANES, LANES), LANES)
        query = query_ref[:, cols] * jnp.bfloat16(HD**-0.5)
        grad = grad_ref[:, cols]
        dots = (grad.astype(jnp.float32) * heads_ref[:, cols].astype(jnp.float32)).T
        key_turned = key_ref[:, cols].T
        queries = [query * mask for mask in masks]
        grads = [grad * mask for mask in masks]
        logs = [log_ref[0, pl.ds(2 * pair + half, 1), :] for half in range(2)]
        row_dots = [
            jnp.sum(dots[half * HD : (half + 1) * HD], axis=0, keepdims=True) for half in range(2)
        ]
        joined = block_rows % LANES == 0
        if joined:
            queries, grads = (
                [jnp.concatenate(queries, axis=0)],
                [jnp.concatenate(grads, axis=0)],
            )
            logs, row_dots = (
                [jnp.concatenate(logs, axis=1)],
                [jnp.concatenate(row_dots, axis=1)],
            )
        query_grads = [0.0, 0.0]
        for start in range(0, L, key_rows):
            key = key_ref[start : start + key_rows, cols]
            value = value_ref[start : start + key_rows, cols]
            value_part = key_part = 0.0
            for i in range(len(queries)):
                prob = jnp.exp(dot_nt(key, queries[i]) - logs[i])
                prob_grad = dot_nt(value, grads[i])
                score_grad = (prob * (prob_grad - row_dots[i])).astype(jnp.bfloat16)
                value_part += dot_nn(prob.astype(jnp.bfloat16), grads[i])
                key_part += dot_nn(score_grad, queries[i])
                for half in range(2) if joined else (i,):
                    mine = score_grad
                    if joined:
                        mine = score_grad[:, half * block_rows : (half + 1) * block_rows]
                    turned = key_turned[half * HD : (half + 1) * HD, start : start + key_rows]
                    query_grads[half] += dot_nn(turned, mine)
            rows = pl.ds(pl.multiple_of(latent * L + start, key_rows), key_rows)
            value_acc[rows, cols] += value_part
            key_acc[rows, cols] += key_part
        turned = jnp.concatenate(query_grads, axis=0).T * HD**-0.5
        out_ref[own, cols] = turned.astype(jnp.bfloat16)

    @pl.when(step == pl.num_programs(0) - 1)
    def finish():
        out_ref[:, width : 2 * width] = key_acc[...].astype(jnp.bfloat16)
        out_ref[:, 2 * width :] = value_acc[...].astype(jnp.bfloat16)


def qkv_specs(block_rows, width):
    return [
        pl.BlockSpec((block_rows, width), lambda b, start: (start[0] + b, 0)),
        pl.BlockSpec((L, width), lambda b, start: ((start[0] + b) * block_rows // L, 1)),
        pl.BlockSpec((L, width), lambda b, start: ((start[0] + b) * block_rows // L, 2)),
    ]


def attend_forward(qkv_ext, start_block, block_rows, block_count):
    width = qkv_ext.shape[1] // 3
    heads = width // HD
    cost = 4 * block_rows * block_count * L * width
    return pl.pallas_call(
        forward_kernel,
        grid_spec=pltpu.PrefetchScalarGridSpec(
            num_scalar_prefetch=1,
            grid=(block_count,),
            in_specs=qkv_specs(block_rows, width),
            out_specs=[
                pl.BlockSpec((block_rows, width), lambda b, start: (b, 0)),
                pl.BlockSpec((1, heads, block_rows), lambda b, start: (b, 0, 0)),
            ],
        ),
        out_shape=[
            jax.ShapeDtypeStruct((block_rows * block_count, width), jnp.bfloat16),
            jax.ShapeDtypeStruct((block_count, heads, block_rows), jnp.float32),
        ],
        compiler_params=pltpu.CompilerParams(vmem_limit_bytes=VMEM_BYTES),
        cost_estimate=pl.CostEstimate(
            flops=4 * cost, bytes_accessed=qkv_ext.size * 4, transcendentals=cost // 4 // HD
        ),
        name="attend_forward",
    )(start_block, qkv_ext, qkv_ext, qkv_ext)


def attend_backward(
    qkv_ext, heads_low, heads_grad, log_totals, start_block, block_rows, block_count
):
    ext_rows, width = qkv_ext.shape[0], qkv_ext.shape[1] // 3
    heads = width // HD
    cost = 10 * block_rows * block_count * L * width
    return pl.pallas_call(
        backward_kernel,
        grid_spec=pltpu.PrefetchScalarGridSpec(
            num_scalar_prefetch=1,
            grid=(block_count,),
            in_specs=qkv_specs(block_rows, width)
            + [
                pl.BlockSpec((block_rows, width), lambda b, start: (b, 0)),
                pl.BlockSpec((block_rows, width), lambda b, start: (b, 0)),
                pl.BlockSpec((1, heads, block_rows), lambda b, start: (b, 0, 0)),
            ],
            out_specs=pl.BlockSpec((ext_rows, 3 * width), lambda b, start: (0, 0)),
            scratch_shapes=[
                pltpu.VMEM((ext_rows, width), jnp.float32),
                pltpu.VMEM((ext_rows, width), jnp.float32),
            ],
        ),
        out_shape=jax.ShapeDtypeStruct((ext_rows, 3 * width), jnp.bfloat16),
        compiler_params=pltpu.CompilerParams(vmem_limit_bytes=VMEM_BYTES),
        cost_estimate=pl.CostEstimate(
            flops=4 * cost, bytes_accessed=qkv_ext.size * 6, transcendentals=cost // 10 // HD
        ),
        name="attend_backward",
    )(start_block, qkv_ext, qkv_ext, qkv_ext, heads_low, heads_grad, log_totals)


def axis_bits():
    dp_bits = lax.axis_size("dp").bit_length() - 1
    tensor_bits = lax.axis_size("tensor").bit_length() - 1
    z_bits = [("dp", bit) for bit in (dp_bits - 1, dp_bits - 2)]
    x_bits = [("dp", bit) for bit in range(dp_bits - 3, 0, -1)]
    y_bits = [("tensor", bit) for bit in range(tensor_bits - 1, -1, -1)]
    return z_bits, x_bits, y_bits


def own_bit(place):
    return lax.axis_index(place[0]) >> place[1] & 1


def swap(values, place):
    axis, bit = place
    route = [(i, i ^ 1 << bit) for i in range(lax.axis_size(axis))]
    return lax.ppermute(values, axis, route)


def add_low(kept, got):
    return (kept.astype(jnp.float32) + got.astype(jnp.float32)).astype(jnp.bfloat16)


def pick_half(values, axis, bit):
    return lax.dynamic_index_in_dim(values, bit, axis, False)


class SumChain:
    def __init__(self, groups):
        dp_count = lax.axis_size("dp")
        rows, columns = D // dp_count, groups[0][0].shape[1]
        z_bits, x_bits, y_bits = axis_bits()
        parts = [part.reshape(dp_count // 2, 2, rows, columns) for group in groups for part in group]
        places = ["group"] + y_bits + z_bits + x_bits
        self.shape = (len(groups),) + (2,) * (len(places) - 1) + (rows, columns)
        self.parts = parts
        self.places = places
        self.stages = [[("dp", 0)]]
        self.stages += [list(both) for both in zip(x_bits + y_bits, y_bits + x_bits)]
        self.stages += [[z_bits[0]], [z_bits[1]]]
        self.z_bits = z_bits
        self.stage = 0

    def done(self):
        return self.stage == len(self.stages)

    def sends(self):
        stage = self.stages[self.stage]
        if self.stage == 0:
            bit = own_bit(stage[0])
            self.kept = [pick_half(part, 1, bit) for part in self.parts]
            return [pick_half(part, 1, 1 - bit) for part in self.parts]
        if self.stage == len(self.stages) - 2:
            upper = own_bit(stage[0]) == 1
            first, second = self.halves
            self.kept = [jnp.where(upper, second, first)]
            return [jnp.where(upper, first, second)]
        sent, self.kept = [], []
        for i, place in enumerate(stage):
            axis, bit = self.labels[i].index(place), own_bit(place)
            sent.append(pick_half(self.halves[i], axis, 1 - bit))
            self.kept.append(pick_half(self.halves[i], axis, bit))
            self.labels[i] = [label for label in self.labels[i] if label != place]
        return sent

    def swap(self, sent):
        places = self.stages[self.stage]
        if self.stage == 0:
            places = places * len(sent)
        return [swap(values, place) for values, place in zip(sent, places)]

    def receive(self, got):
        self.stage += 1
        if self.stage == 1:
            self.kept, got = [jnp.stack(self.kept)], [jnp.stack(got)]
        if self.done():
            self.result = self.kept[0].astype(jnp.float32) + got[0].astype(jnp.float32)
            return
        totals = [add_low(kept, part) for kept, part in zip(self.kept, got)]
        if self.stage == 1:
            total = totals[0].reshape(self.shape)
            high = self.places.index(self.z_bits[0])
            rest = [place for place in self.places if place != self.z_bits[0]]
            totals = [lax.index_in_dim(total, i, high, False) for i in range(2)]
            self.labels = [rest, rest]
        elif self.stage == len(self.stages) - 1:
            self.labels = [["group", self.z_bits[1]]]
        self.halves = totals


class GatherChain:
    def __init__(self, values):
        z_bits, x_bits, y_bits = axis_bits()
        self.values, self.order = values[None], np.zeros((1,), np.int64)
        self.stages = z_bits + x_bits + y_bits + [("dp", 0)]
        self.stage = 0

    def done(self):
        return self.stage == len(self.stages)

    def sends(self):
        return [self.values]

    def swap(self, sent):
        return [swap(sent[0], self.stages[self.stage])]

    def receive(self, got):
        place = self.stages[self.stage]
        upper = own_bit(place) == 1
        self.values = jnp.concatenate(
            [jnp.where(upper, got[0], self.values), jnp.where(upper, self.values, got[0])]
        )
        weight = (lax.axis_size("tensor") if place[0] == "dp" else 1) << place[1]
        self.order = np.concatenate([self.order, self.order + weight])
        self.stage += 1


class Received:
    def __init__(self, values):
        self.values, self.got = values, None

    def done(self):
        return self.got is not None

    def sends(self):
        return self.values

    def swap(self, sent):
        return sent

    def receive(self, got):
        self.got = got


def advance(chains):
    chains = [chain for chain in chains if not chain.done()]
    got = lax.optimization_barrier([chain.swap(chain.sends()) for chain in chains])
    for chain, values in zip(chains, got):
        chain.receive(values)


def beside(chains, work, operand):
    chains = [chain for chain in chains if not chain.done()]
    operand, sent = lax.optimization_barrier((operand, [chain.sends() for chain in chains]))
    got = [chain.swap(values) for chain, values in zip(chains, sent)]
    result, got = lax.optimization_barrier((work(operand), got))
    for chain, values in zip(chains, got):
        chain.receive(values)
    return result


def gather_rows(shard):
    whole = lax.all_gather(shard, ("tensor", "dp"), axis=0, tiled=True)
    tensor_count = lax.axis_size("tensor")
    return whole.reshape(tensor_count, D, shard.shape[1])


def on_device(
    tokens_in,
    condition,
    out_grad,
    qkv_weight,
    out_weight,
    up_weight,
    down_weight,
    ada_weight,
    bias_all,
    qkv_first,
    out_first,
    up_first,
    down_first,
    ada_first,
    bias_first,
    qkv_second,
    out_second,
    up_second,
    down_second,
    ada_second,
    bias_second,
):
    tensor_count = lax.axis_size("tensor")
    dp_count = lax.axis_size("dp")
    device_count = dp_count * tensor_count
    dp_index = lax.axis_index("dp")
    device = dp_index * tensor_count + lax.axis_index("tensor")
    row_count = tokens_in.shape[0]
    latent_count = condition.shape[0]
    width = D // tensor_count
    block_rows = math.gcd(row_count, L)
    block_count = row_count // block_rows
    rounds = halo_plan(device_count, row_count)
    window = window_latents(device_count, row_count)
    dp_window = window_latents(dp_count, row_count * tensor_count)
    first_latents = [i * row_count // L for i in range(device_count)]
    dp_latents = [i * row_count * tensor_count // L for i in range(dp_count)]
    first_latent = look_up(first_latents, device)
    start_block = look_up(
        [i * row_count % L // block_rows for i in range(device_count)], device
    )

    hidden = FF // tensor_count
    chunks = range(tensor_count)
    attn_shard = jnp.concatenate(
        [
            qkv_weight.astype(jnp.bfloat16).reshape(-1, 3 * width),
            out_weight.astype(jnp.bfloat16).T,
        ],
        axis=1,
    )
    attn_whole = gather_rows(attn_shard)
    qkv_whole = [attn_whole[h, :, : 3 * width] for h in chunks]
    out_whole = [attn_whole[h, :, 3 * width :] for h in chunks]
    mlp_shard = jnp.concatenate(
        [up_weight.astype(jnp.bfloat16), down_weight.astype(jnp.bfloat16).T], axis=1
    )
    mlp_whole = gather_rows(mlp_shard)
    up_whole = [mlp_whole[h, :, :hidden] for h in chunks]
    down_whole = [mlp_whole[h, :, hidden:] for h in chunks]

    cond_value = condition.astype(jnp.float32)
    silu_low = jax.nn.silu(cond_value).astype(jnp.bfloat16)
    ada_low = ada_weight.astype(jnp.bfloat16)
    picked = [min(first, latent_count - dp_window) for first in dp_latents]
    silu_picked = jnp.concatenate([silu_low[first : first + dp_window] for first in picked])
    ada_part = dot_nn(silu_picked, ada_low).reshape(dp_count, dp_window, 6 * D)

    def in_blocks(values):
        return values.reshape(block_count, block_rows, -1)

    def in_rows(values):
        return values.reshape(row_count, -1)

    tokens = in_blocks(tokens_in)
    cotangent = in_blocks(out_grad)
    norm_attn, inverse_attn = norm_parts(tokens)
    ada_part, norm_low = lax.optimization_barrier((ada_part, norm_attn.astype(jnp.bfloat16)))
    norm_ext = jnp.zeros((window * L // block_rows, block_rows, D), jnp.bfloat16)
    places = []
    for size, pieces in rounds:
        source = [0] * device_count
        target = [i * row_count % L // block_rows for i in range(device_count)]
        for src, dst, src_row, dst_row in pieces:
            source[src] = src_row // block_rows
            target[dst] = dst_row // block_rows
        places.append((look_up(source, device), look_up(target, device)))
    for (size, pieces), (source, target) in zip(rounds, places):
        sent = lax.dynamic_slice_in_dim(norm_low, source, size // block_rows, 0)
        got = lax.ppermute(sent, both, [(piece[0], piece[1]) for piece in pieces])
        norm_ext = lax.dynamic_update_slice_in_dim(norm_ext, got, target, 0)
    norm_ext = lax.dynamic_update_slice_in_dim(norm_ext, norm_low, start_block, 0)

    ada_parts = lax.all_to_all(ada_part, "dp", split_axis=0, concat_axis=0, tiled=True)
    mod_dp = jnp.sum(ada_parts, axis=0) + bias_all[4 * D + FF :]
    mod_dp = jnp.concatenate([mod_dp, jnp.zeros((window, 6 * D), jnp.float32)])
    mod_window = lax.dynamic_slice_in_dim(
        mod_dp, first_latent - look_up(picked, dp_index), window, 0
    )
    block_latent = (start_block + jnp.arange(block_count, dtype=jnp.int32)) * block_rows // L
    latent_pick = (
        block_latent[None, :] == jnp.arange(window, dtype=jnp.int32)[:, None]
    ).astype(jnp.float32)
    mod_blocks = jnp.sum(latent_pick[:, :, None] * mod_window[:, None, :], axis=0)
    mod_blocks = mod_blocks.reshape(block_count, 1, 6 * D)
    shift_attn, scale_attn, gate_attn, shift_mlp, scale_mlp, gate_mlp = (
        mod_blocks[:, :, i * D : (i + 1) * D] for i in range(6)
    )

    def latent_sums(values):
        return jnp.sum(latent_pick[:, :, None] * jnp.sum(values, axis=1)[None], axis=1)

    norm_ext = norm_ext.reshape(window, L, D)
    attn_ext = (
        norm_ext.astype(jnp.float32) * (1.0 + mod_window[:, None, D : 2 * D])
        + mod_window[:, None, :D]
    ).astype(jnp.bfloat16)
    attn_own = (norm_attn * (1.0 + scale_attn) + shift_attn).astype(jnp.bfloat16)
    attn_ext = lax.dynamic_update_slice_in_dim(
        attn_ext.reshape(-1, block_rows, D), attn_own, start_block, 0
    ).reshape(window * L, D)

    starts = start_block.reshape(1)
    qkv_ext, head_low, log_totals = [], [], []
    for h in chunks:
        own = slice(h * width, (h + 1) * width)
        bias = jnp.concatenate(
            [bias_all[:D][own], jnp.zeros((width,), jnp.float32), bias_all[D : 2 * D][own]]
        )
        qkv_ext.append((dot_nn(attn_ext, qkv_whole[h]) + bias).astype(jnp.bfloat16))
        heads, logs = attend_forward(qkv_ext[h], starts, block_rows, block_count)
        head_low.append(heads)
        log_totals.append(logs)
    attn_value = sum(dot_nt(head_low[h], out_whole[h]) for h in chunks)
    attn_value = in_blocks(attn_value + bias_all[2 * D : 3 * D])
    residual_mid = tokens + gate_attn * attn_value
    norm_mlp, inverse_mlp = norm_parts(residual_mid)
    mlp_low = in_rows((norm_mlp * (1.0 + scale_mlp) + shift_mlp).astype(jnp.bfloat16))
    mlp_grad = in_rows((cotangent * gate_mlp).astype(jnp.bfloat16))

    up_values = [
        dot_nn(mlp_low, up_whole[h]) + bias_all[3 * D + h * hidden : 3 * D + (h + 1) * hidden]
        for h in chunks
    ]
    hidden_low = [gelu_tanh(up_value).astype(jnp.bfloat16) for up_value in up_values]
    down_sum = SumChain([[dot_tn(mlp_grad, part).astype(jnp.bfloat16) for part in hidden_low]])

    def up_backward(grad):
        grads, sums = [], []
        for h in chunks:
            unused, gelu_pull = jax.vjp(gelu_tanh, up_values[h])
            part = gelu_pull(dot_nn(grad, down_whole[h]))[0].astype(jnp.bfloat16)
            grads.append(part)
            sums.append(jnp.sum(part.astype(jnp.float32), axis=0))
        return grads, sums

    up_grad, up_sums = beside([down_sum], up_backward, mlp_grad)
    up_wgrad = [dot_tn(mlp_low, part).astype(jnp.bfloat16) for part in up_grad]
    up_sum = SumChain([up_wgrad])
    mlp_value = sum(dot_nt(hidden_low[h], down_whole[h]) for h in chunks)
    mlp_value = in_blocks(mlp_value + bias_all[3 * D + FF : 4 * D + FF])
    block_out = in_rows(residual_mid + gate_mlp * mlp_value)

    def mid_backward(parts):
        norm_grad = in_blocks(sum(dot_nt(parts[h], up_whole[h]) for h in chunks))
        grad = cotangent + norm_back(norm_mlp, inverse_mlp, norm_grad * (1.0 + scale_mlp))
        low = in_rows((grad * gate_attn).astype(jnp.bfloat16))
        return low, grad, norm_grad, jnp.sum(low.astype(jnp.float32), axis=0)

    attn_grad, mid_grad, mlp_norm_grad, attn_grad_sum = beside(
        [down_sum, up_sum], mid_backward, up_grad
    )
    early = jnp.concatenate(
        [attn_grad_sum]
        + up_sums
        + [
            jnp.sum(mlp_grad.astype(jnp.float32), axis=0),
            latent_sums(mid_grad * attn_value).reshape(-1),
            latent_sums(mlp_norm_grad).reshape(-1),
            latent_sums(mlp_norm_grad * norm_mlp).reshape(-1),
            latent_sums(cotangent * mlp_value).reshape(-1),
        ]
    )
    heads_grad = [dot_nn(attn_grad, part).astype(jnp.bfloat16) for part in out_whole]
    early, heads_grad = lax.optimization_barrier((early, heads_grad))
    early_all = lax.all_gather(early.reshape(-1, LANES), both, axis=0, tiled=False)
    out_wgrad = jnp.stack([dot_tn(attn_grad, part) for part in head_low])
    out_summed = lax.psum_scatter(
        out_wgrad.reshape(device_count, D // dp_count, width),
        ("tensor", "dp"),
        scatter_dimension=0,
        tiled=False,
    ).T

    qkv_grad = []
    for h in chunks:
        qkv_grad.append(
            beside(
                [down_sum, up_sum],
                lambda grad: attend_backward(
                    qkv_ext[h], head_low[h], grad, log_totals[h], starts, block_rows, block_count
                ),
                heads_grad[h],
            )
        )
    early_all, qkv_grad = lax.optimization_barrier((early_all, qkv_grad))
    early_all = early_all.reshape(device_count, -1)
    norm_grad_ext, norm_ext = beside(
        [down_sum, up_sum],
        lambda parts: (sum(dot_nt(parts[0][h], qkv_whole[h]) for h in chunks), parts[1]),
        (qkv_grad, norm_ext),
    )

    qkv_sums = [jnp.sum(part.astype(jnp.float32), axis=0) for part in qkv_grad]
    by_latent = norm_grad_ext.reshape(window, L, D)
    late = jnp.concatenate(
        [part[:width] for part in qkv_sums]
        + [part[2 * width :] for part in qkv_sums]
        + [
            jnp.sum(by_latent, axis=1).reshape(-1),
            jnp.sum(by_latent * norm_ext.astype(jnp.float32), axis=1).reshape(-1),
        ]
    )
    late_sums = GatherChain(late.reshape(-1, LANES))
    norm_grad_ext = norm_grad_ext.reshape(-1, block_rows, D)
    sent = [
        lax.dynamic_slice_in_dim(norm_grad_ext, target, size // block_rows, 0).astype(jnp.bfloat16)
        for (size, pieces), (source, target) in zip(rounds, places)
    ]
    qkv_grad, sent = lax.optimization_barrier((qkv_grad, sent))
    returned = Received(
        [
            lax.ppermute(part, both, [(piece[1], piece[0]) for piece in pieces])
            for part, (size, pieces) in zip(sent, rounds)
        ]
    )
    qkv_wgrad = beside(
        [late_sums, down_sum, up_sum],
        lambda parts: [dot_tn(attn_ext, part).astype(jnp.bfloat16) for part in parts],
        qkv_grad,
    )
    qkv_sum = SumChain([qkv_wgrad])
    chains = [qkv_sum, late_sums, down_sum, up_sum]
    advance(chains + [returned])
    attn_norm_grad = lax.dynamic_slice_in_dim(norm_grad_ext, start_block, block_count, 0)
    for (size, pieces), (source, target), got in zip(rounds, places, returned.got):
        old = lax.dynamic_slice_in_dim(attn_norm_grad, source, size // block_rows, 0)
        attn_norm_grad = lax.dynamic_update_slice_in_dim(
            attn_norm_grad, old + got.astype(jnp.float32), source, 0
        )
    tokens_grad = in_rows(
        mid_grad + norm_back(norm_attn, inverse_attn, attn_norm_grad * (1.0 + scale_attn))
    )
    while not all(chain.done() for chain in chains):
        advance(chains)
    late_all, order = late_sums.values.reshape(device_count, -1), late_sums.order

    spread = np.zeros((latent_count, device_count, window), np.float32)
    for i, first in enumerate(first_latents):
        for w in range(window):
            if first + w < latent_count:
                spread[first + w, i, w] = 1.0

    def latent_totals(gathered, devices):
        terms = gathered.reshape(device_count * window, D)
        picks = jnp.asarray(spread[:, devices].reshape(latent_count, -1))
        return jnp.dot(picks, terms, precision=highest, preferred_element_type=jnp.float32)

    early_bias = 2 * D + FF
    step = window * D
    mod_grads = [
        latent_totals(late_all[:, 2 * D + i * step : 2 * D + (i + 1) * step], order)
        for i in range(2)
    ] + [
        latent_totals(
            early_all[:, early_bias + i * step : early_bias + (i + 1) * step],
            np.arange(device_count),
        )
        for i in range(4)
    ]
    mod_grad = jnp.concatenate(mod_grads, axis=1)
    bias_grad = jnp.concatenate(
        [
            jnp.sum(late_all[:, : 2 * D], axis=0),
            jnp.sum(early_all[:, :early_bias], axis=0),
            jnp.sum(mod_grad, axis=0),
        ]
    )
    ada_wgrad = jnp.dot(
        silu_low.astype(jnp.float32).T,
        mod_grad,
        precision=highest,
        preferred_element_type=jnp.float32,
    )
    cond_inner = jnp.dot(
        mod_grad,
        ada_low.astype(jnp.float32).T,
        precision=highest,
        preferred_element_type=jnp.float32,
    )
    unused, silu_pull = jax.vjp(jax.nn.silu, cond_value)
    condition_grad = silu_pull(cond_inner)[0]
    qkv_summed = qkv_sum.result[0].reshape(qkv_weight.shape)
    up_summed = up_sum.result[0]
    down_summed = down_sum.result[0].T
    qkv_new = adam_update(qkv_weight, qkv_summed, qkv_first, qkv_second, 3.0 / math.sqrt(D))
    out_new = adam_update(out_weight, out_summed, out_first, out_second, 3.0 / math.sqrt(D // 4))
    up_new = adam_update(up_weight, up_summed, up_first, up_second, 3.0 / math.sqrt(D))
    down_new = adam_update(down_weight, down_summed, down_first, down_second, 3.0 / math.sqrt(FF))
    ada_new = adam_update(ada_weight, ada_wgrad, ada_first, ada_second, 3.0 / math.sqrt(D))
    bias_new = adam_update(bias_all, bias_grad, bias_first, bias_second, 0.9)
    return (
        block_out,
        tokens_grad,
        condition_grad,
        *qkv_new,
        *out_new,
        *up_new,
        *down_new,
        *ada_new,
        *bias_new,
    )


def solution(mesh):
    weights = (
        P("dp", None, "tensor"),
        P("tensor", "dp"),
        P("dp", "tensor"),
        P("tensor", "dp"),
        P("dp", None),
        P(),
    )
    tokens = P(both, None)
    return jax.shard_map(
        on_device,
        mesh=mesh,
        in_specs=(tokens, P(None, "dp"), tokens, *weights, *weights, *weights),
        out_specs=(tokens, tokens, P(None, "dp"))
        + tuple(spec for spec in weights for unused in range(3)),
        check_vma=False,
    )
```

time: 1390 us -> 722 us (0.52)
  waiting for transfers between devices: 578 us -> 120 us
  local copies, waits for them, and re-layouts: 233 us -> 71.1 us
  blocking collectives: 72.5 us -> 0 us
  Pallas kernels: 159 us -> 116 us
  other arithmetic: 70.2 us -> 102 us
  starting transfers between devices: 26 us -> 47 us
    reduce_scatter x4 -> x1, waiting for transfers between devices: 451 us -> 0.01 us  [on_device(): lax.psum_scatter(out_wgrad.reshape(device_count, D // dp_count, width), (...]
    reshape x11 -> x1, local copies, waits for them, and re-layouts: 120 us -> 0.01 us  [on_device(): qkv_weight.astype(jnp.bfloat16).reshape(-1, 3 * width)]
    all_gather x1 -> x0, blocking collectives: 72.5 us -> none  [on_device(): lax.all_gather(late.reshape(-1, LANES), both, axis=0, tiled=False)]
    ppermute x3 -> x32, waiting for transfers between devices: 13.1 us -> 70.2 us  [the longest x29 45.7 us: swap(): return lax.ppermute(values, axis, route)]
    all_gather x4 -> x2, waiting for transfers between devices: 90.3 us -> 47.5 us  [gather_rows(): whole = lax.all_gather(shard, ('tensor', 'dp'), axis=0, tiled=True)]
    transpose x4 -> x0, local copies, waits for them, and re-layouts: 34.7 us -> none  [the longest x3 22.9 us: scatter_columns(): grad.reshape(dp_count, D // dp_count, tensor_count, columns)]
    pallas_call x1 -> x2, Pallas kernels: 68.5 us -> 41.2 us  [attend_forward(): pl.pallas_call(forward_kernel, grid_spec=pltpu.PrefetchScalarGridSpec(num...]
    unnamed x132 -> x236, local copies, waits for them, and re-layouts: 40.4 us -> 14.1 us
  transfers between devices with their start and end apart: 16 -> 40, of which waited for: 7 -> 10; matrix products, arithmetic and copies ran while one was open for 20% -> 42% of each run, Pallas kernels for 5% -> 16%
where the time goes in v2:
time: 722 us; the launch traced here: 715 us
  matrix products  228 us (32%)
  waiting for transfers between devices  120 us (17%)
  Pallas kernels  116 us (16%)
  other arithmetic  102 us (14%)
  local copies, waits for them, and re-layouts  71.1 us (10%)
  starting transfers between devices  47 us (7%)
  between operations  31.3 us (4%)
    dot_general x9, matrix products, dot_nn(): lax.dot_general(left, right, (((1,), (0,)), ((), ())), preferred_element_...  84.8 us
    dot_general x8, matrix products, dot_nt(): lax.dot_general(left, right, (((1,), (1,)), ((), ())), preferred_element_...  80.7 us
    pallas_call x2, Pallas kernels, attend_backward(): pl.pallas_call(backward_kernel, grid_spec=pltpu.PrefetchScalarGridSpec(nu...  74.9 us
    dot_general x8, matrix products, dot_tn(): lax.dot_general(left, right, (((0,), (0,)), ((), ())), preferred_element_...  48.6 us
    all_gather x2, waiting for transfers between devices, gather_rows(): whole = lax.all_gather(shard, ('tensor', 'dp'), axis=0, tiled=True)  47.5 us
    ppermute x29, waiting for transfers between devices, swap(): return lax.ppermute(values, axis, route)  45.7 us
    pallas_call x2, Pallas kernels, attend_forward(): pl.pallas_call(forward_kernel, grid_spec=pltpu.PrefetchScalarGridSpec(num...  41.2 us
    ppermute x3, waiting for transfers between devices, on_device(): lax.ppermute(part, both, [(piece[1], piece[0]) for piece in pieces])  24.5 us
  transfers between devices with their start and end apart: 40, of which 10 were waited for; matrix products, arithmetic and copies ran while one was open for 42% of the time, Pallas kernels for 16%

profile of v2, /device:TPU:0, one launch (start us, length us, event | category | flops | bytes accessed | tf_op | source)
XLA Modules:
  0.0 715.3 jit_solution(4539876412099975242)
XLA Ops:
  24.8 7.4 %all-to-all-start = ((f32[16,3,6144]{2,1,0:T(4,128)}), f32[16,3,6144]{2,1,0:T(4,128)}, u32[]{:S(2)}, u32[]{:S(2)}) async-start(f32[16,3,6144]{2,1,0:T(4,128)} %reshape.779), calls=%async_computation | async-start | bytes 3145728 | tf_op jit(solution)/shard_map/all_to_all | solution.py:546
  90.1 18.3 %all-gather.4.cloned.1.call-done = bf16[2048,2048]{1,0:T(8,128)(2,1)} async-done(((bf16[64,2048]{1,0:T(8,128)(2,1)}), bf16[2048,2048]{1,0:T(8,128)(2,1)}) %all-gather.4.cloned.1.call-update) | async-done | bytes 8388624 | tf_op jit(solution)/shard_map/all_gather | solution.py:447
  108.3 11.3 %add_convert_fusion.1.query_ref.key_ref.value_ref = bf16[2048,1536]{1,0:T(8,128)(2,1)} fusion(bf16[2048,1024]{1,0:T(8,128)(2,1)} %bitcast.14, f32[1536]{0:T(1024)S(1)} %get-tuple-element.363, bf16[2,1024,2048]{2,1,0:T(8,128)(2,1)} %bitcast.453), kind=kOutput, calls=%fused_computation.7 | convolution fusion | flops 6448742400 | bytes 13637632 | tf_op jit(solution)/shard_map/dot_general | solution.py:103
  119.6 20.5 %attend_forward.2 = (bf16[1280,512]{1,0:T(8,128)(2,1)S(1)}, f32[5,8,256]{2,1,0:T(8,128)S(1)}) custom-call(s32[1]{0:T(128)} %dynamic_slice.203.start_ref, bf16[2048,1536]{1,0:T(8,128)(2,1)} %add_convert_fusion.1.query_ref.key_ref.value_ref, bf16[2048,1536]{1,0:T(8,128)(2,1)} %add_convert_fusion.1.query_ref.key_ref.value_ref, ...), custom_call_target="tpu_custom_call" | custom-call | flops 10737418240 | bytes 12582912 | tf_op jit(solution)/shard_map/attend_forward/pallas_call | solution.py:240
  143.5 11.5 %add_convert_fusion.query_ref.key_ref.value_ref = bf16[2048,1536]{1,0:T(8,128)(2,1)} fusion(bf16[2048,1024]{1,0:T(8,128)(2,1)} %bitcast.14, f32[1536]{0:T(1024)S(1)} %get-tuple-element.362, bf16[2,1024,2048]{2,1,0:T(8,128)(2,1)} %bitcast.455), kind=kOutput, calls=%fused_computation.6 | convolution fusion | flops 6448742400 | bytes 13637632 | tf_op jit(solution)/shard_map/dot_general | solution.py:103
  155.0 20.7 %attend_forward.3 = (bf16[1280,512]{1,0:T(8,128)(2,1)S(1)}, f32[5,8,256]{2,1,0:T(8,128)S(1)}) custom-call(s32[1]{0:T(128)} %dynamic_slice.203.start_ref, bf16[2048,1536]{1,0:T(8,128)(2,1)} %add_convert_fusion.query_ref.key_ref.value_ref, bf16[2048,1536]{1,0:T(8,128)(2,1)} %add_convert_fusion.query_ref.key_ref.value_ref, ...), custom_call_target="tpu_custom_call" | custom-call | flops 10737418240 | bytes 12582912 | tf_op jit(solution)/shard_map/attend_forward/pallas_call | solution.py:240
  175.7 7.9 %fusion.82 = (f32[1280]{0:T(1024)S(1)}, f32[1280,1024]{1,0:T(8,128)}, f32[1280,1024]{1,0:T(8,128)}) fusion(f32[1280,1024]{1,0:T(8,128)S(1)} %bitcast.389, f32[5,1024]{1,0:T(8,128)S(1)} %get-tuple-element.338, f32[1024]{0:T(1024)S(1)} %get-tuple-element.346, f32[1280,1024]{1,0:T(8,128)S(1)} %fusion.42, ...), kind=kOutput, calls=%fused_computation.294 | convolution fusion | flops 1348729600 | bytes 23360512 | tf_op jit(solution)/shard_map/dot_general | solution.py:97
  188.0 8.2 %convert_reduce_fusion.4 = (f32[1024]{0:T(1024)}, bf16[1280,1024]{1,0:T(8,128)(2,1)}, bf16[1280,1024]{1,0:T(8,128)(2,1)S(1)}) fusion(f32[1280,1024]{1,0:T(8,128)} %param.38, f32[5,1024]{1,0:T(8,128)S(1)} %get-tuple-element.333, f32[5,1024]{1,0:T(8,128)S(1)} %get-tuple-element.334, f32[5,1024]{1,0:T(8,128)S(1)} %get-tuple-element.335, ...), kind=kLoop, calls=%fused_computation.50 | loop fusion | flops 11795456 | bytes 15804416 | tf_op jit(solution)/shard_map/reduce_sum | solution.py:629
  196.2 29.3 %all-gather.6.cloned.1.call-done = bf16[2048,4096]{1,0:T(8,128)(2,1)} async-done(((bf16[64,4096]{1,0:T(8,128)(2,1)}), bf16[2048,4096]{1,0:T(8,128)(2,1)}) %all-gather.6.cloned.1.call-update) | async-done | bytes 16777232 | tf_op jit(solution)/shard_map/all_gather | solution.py:447
  225.5 7.4 %fusion.26 = f32[1280,2048]{1,0:T(8,128)S(1)} fusion(bf16[1280,1024]{1,0:T(8,128)(2,1)S(1)} %get-tuple-element.371, bf16[2,1024,4096]{2,1,0:T(8,128)(2,1)} %bitcast.436), kind=kOutput, calls=%fused_computation.83 | convolution fusion | flops 5368709120 | bytes 17301504 | tf_op jit(solution)/shard_map/dot_general | solution.py:103
  232.9 13.6 %fusion.23 = f32[1280,2048]{1,0:T(8,128)} fusion(bf16[1280,1024]{1,0:T(8,128)(2,1)S(1)} %get-tuple-element.371, bf16[2,1024,4096]{2,1,0:T(8,128)(2,1)} %bitcast.437), kind=kOutput, calls=%fused_computation.80 | convolution fusion | flops 5368709120 | bytes 17301504 | tf_op jit(solution)/shard_map/dot_general | solution.py:103
  246.5 6.4 convolution_convert_fusion.4
  252.9 9.1 %convolution_convert_fusion.5 = bf16[1024,2048]{1,0:T(8,128)(2,1)S(1)} fusion(bf16[1280,1024]{1,0:T(8,128)(2,1)S(1)} %copy-done.30, f32[1280,2048]{1,0:T(8,128)} %fusion.23, f32[2048]{0:T(1024)S(1)} %get-tuple-element.344), kind=kOutput, calls=%fused_computation.78 | convolution fusion | flops 5397020672 | bytes 17309696 | tf_op jit(solution)/shard_map/dot_general | solution.py:109
  264.9 17.6 %convert_reduce_fusion.3 = (f32[2048]{0:T(1024)}, bf16[1280,2048]{1,0:T(8,128)(2,1)}) fusion(f32[1280,2048]{1,0:T(8,128)} %fusion.23, f32[2048]{0:T(1024)S(1)} %get-tuple-element.344, bf16[1280,1024]{1,0:T(8,128)(2,1)S(1)} %copy-done.30, bf16[2,1024,4096]{2,1,0:T(8,128)(2,1)} %bitcast.438), kind=kOutput, calls=%fused_computation.23 | convolution fusion | flops 5429000192 | bytes 22560768 | tf_op jit(solution)/shard_map/dot_general | solution.py:103
  282.5 14.8 %convert_reduce_fusion.2 = (f32[2048]{0:T(1024)}, bf16[1280,2048]{1,0:T(8,128)(2,1)S(1)}) fusion(f32[1280,2048]{1,0:T(8,128)S(1)} %fusion.26, f32[2048]{0:T(1024)S(1)} %get-tuple-element.343, bf16[1280,1024]{1,0:T(8,128)(2,1)S(1)} %copy-done.31, bf16[2,1024,4096]{2,1,0:T(8,128)(2,1)} %bitcast.439), kind=kOutput, calls=%fused_computation.22 | convolution fusion | flops 5429000192 | bytes 22560768 | tf_op jit(solution)/shard_map/dot_general | solution.py:103
  297.3 12.2 %fusion.25 = f32[1280,1024]{1,0:T(8,128)} fusion(bf16[2,1024,4096]{2,1,0:T(8,128)(2,1)} %bitcast.440, f32[1280,2048]{1,0:T(8,128)} %fusion.23, f32[2048]{0:T(1024)S(1)} %get-tuple-element.344), kind=kOutput, calls=%fused_computation.82 | convolution fusion | flops 5394923520 | bytes 19931136 | tf_op jit(solution)/shard_map/dot_general | solution.py:97
  315.9 6.3 convolution_convert_fusion.3
  335.1 9.1 %fusion.22 = f32[1280,1024]{1,0:T(8,128)S(1)} fusion(bf16[1280,2048]{1,0:T(8,128)(2,1)} %get-tuple-element.121, bf16[2,1024,4096]{2,1,0:T(8,128)(2,1)} %bitcast.441), kind=kOutput, calls=%fused_computation.79 | convolution fusion | flops 5368709120 | bytes 14680064 | tf_op jit(solution)/shard_map/dot_general | solution.py:97
  344.3 10.7 %fusion.21 = (f32[1280]{0:T(1024)S(1)}, f32[1280]{0:T(1024)S(1)}, f32[1280,1024]{1,0:T(8,128)}) fusion(f32[5,1024]{1,0:T(8,128)S(1)} %get-tuple-element.335, f32[1280]{0:T(1024)S(1)} %copy-done.62, f32[1280,1024]{1,0:T(8,128)S(1)} %bitcast.398, f32[1280]{0:T(1024)S(1)} %copy-done.52, f32[1280,1024]{1,0:T(8,128)S(1)} %fusion.22, ...), kind=kOutput, calls=%fused_computation.62 | convolution fusion | flops 5377882112 | bytes 25206784 | tf_op jit(solution)/shard_map/dot_general | solution.py:97
  357.1 18.3 %convert_reduce_fusion.5 = (f32[1024]{0:T(1024)S(1)}, bf16[1280,1024]{1,0:T(8,128)(2,1)S(1)}, f32[1280,1024]{1,0:T(8,128)}, f32[1280,1024]{1,0:T(8,128)S(1)}) fusion(f32[5,1024]{1,0:T(8,128)S(1)} %copy-done.39, f32[1280,1024]{1,0:T(8,128)} %param.38, f32[1280]{0:T(1024)S(1)} %broadcast_multiply_fusion.2, f32[1280,1024]{1,0:T(8,128)} %get-tuple-element.298, ...), kind=kOutput, calls=%fused_computation.51 | convolution fusion | flops 5415894016 | bytes 48857088 | tf_op jit(solution)/shard_map/dot_general | solution.py:97
  375.4 8.0 %multiply_reduce_fusion.1 = (f32[5,1024]{1,0:T(8,128)S(1)}, f32[5,256,1024]{2,1,0:T(8,128)S(1)}) fusion(f32[5,256,1024]{2,1,0:T(8,128)} %bitcast.408, f32[5,256,1024]{2,1,0:T(8,128)S(1)} %bitcast.413, f32[5,256]{1,0:T(8,128)S(1)} %div.154, f32[5,256]{1,0:T(8,128)S(1)} %copy-done.64, f32[5,256,1024]{2,1,0:T(8,128)} %bitcast.384, ...), kind=kLoop, calls=%fused_computation.47 | loop fusion | flops 15723520 | bytes 31539200 | tf_op jit(solution)/shard_map/reduce_sum | solution.py:563
  418.1 37.6 %attend_backward.2 = bf16[2048,1536]{1,0:T(8,128)(2,1)} custom-call(s32[1]{0:T(128)} %dynamic_slice.203.start_ref, bf16[2048,1536]{1,0:T(8,128)(2,1)} %add_convert_fusion.1.query_ref.key_ref.value_ref, bf16[2048,1536]{1,0:T(8,128)(2,1)} %add_convert_fusion.1.query_ref.key_ref.value_ref, bf16[2048,1536]{1,0:T(8,128)(2,1)} %add_convert_fusion.1.query_ref.key_ref.value_ref, ...), custom_call_target="tpu_custom_call" | custom-call | flops 26843545600 | bytes 18874368 | tf_op jit(solution)/shard_map/attend_backward/pallas_call | solution.py:269
  471.0 37.4 %attend_backward.3 = bf16[2048,1536]{1,0:T(8,128)(2,1)} custom-call(s32[1]{0:T(128)} %dynamic_slice.203.start_ref, bf16[2048,1536]{1,0:T(8,128)(2,1)} %add_convert_fusion.query_ref.key_ref.value_ref, bf16[2048,1536]{1,0:T(8,128)(2,1)} %add_convert_fusion.query_ref.key_ref.value_ref, bf16[2048,1536]{1,0:T(8,128)(2,1)} %add_convert_fusion.query_ref.key_ref.value_ref, ...), custom_call_target="tpu_custom_call" | custom-call | flops 26843545600 | bytes 18874368 | tf_op jit(solution)/shard_map/attend_backward/pallas_call | solution.py:269
  522.1 8.6 %fusion.29 = f32[2048,1024]{1,0:T(8,128)S(1)} fusion(bf16[2048,1536]{1,0:T(8,128)(2,1)S(1)} %bitcast.422, bf16[2,1024,2048]{2,1,0:T(8,128)(2,1)} %bitcast.459), kind=kOutput, calls=%fused_computation.92 | convolution fusion | flops 6442450944 | bytes 17825792 | tf_op jit(solution)/shard_map/dot_general | solution.py:97
  530.7 10.6 %convolution_add_fusion.1 = f32[2048,1024]{1,0:T(8,128)} fusion(f32[2048,1024]{1,0:T(8,128)S(1)} %fusion.29, bf16[2048,1536]{1,0:T(8,128)(2,1)S(1)} %bitcast.426, bf16[2,1024,2048]{2,1,0:T(8,128)(2,1)} %bitcast.460), kind=kOutput, calls=%fused_computation.72 | convolution fusion | flops 6444548096 | bytes 26214400 | tf_op jit(solution)/shard_map/dot_general | solution.py:97
  563.8 8.9 %convolution_convert_fusion.1 = bf16[1024,1536]{1,0:T(8,128)(2,1)S(1)} fusion(bf16[2048,1024]{1,0:T(8,128)(2,1)} %bitcast.14, bf16[2048,1536]{1,0:T(8,128)(2,1)S(1)} %bitcast.424), kind=kOutput, calls=%fused_computation.74 | convolution fusion | flops 6444023808 | bytes 13631488 | tf_op jit(solution)/shard_map/dot_general | solution.py:109
  576.0 8.7 %convolution_convert_fusion = bf16[1024,1536]{1,0:T(8,128)(2,1)S(1)} fusion(bf16[2048,1024]{1,0:T(8,128)(2,1)} %bitcast.14, bf16[2048,1536]{1,0:T(8,128)(2,1)S(1)} %bitcast.428), kind=kOutput, calls=%fused_computation.73 | convolution fusion | flops 6444023808 | bytes 13631488 | tf_op jit(solution)/shard_map/dot_general | solution.py:109
  601.8 22.6 %collective-permute-done.25 = bf16[1,256,1024]{2,1,0:T(8,128)(2,1)S(1)} collective-permute-done((bf16[1,256,1024]{2,1,0:T(8,128)(2,1)S(1)}, bf16[1,256,1024]{2,1,0:T(8,128)(2,1)S(1)}, u32[]{:S(2)}, u32[]{:S(2)}) %collective-permute-start.25) | collective-permute-done | bytes 524320 | tf_op jit(solution)/shard_map/ppermute | solution.py:685
  636.7 13.0 %collective-permute-done.26 = bf16[1,2,2,64,1536]{4,3,2,1,0:T(8,128)(2,1)S(1)} collective-permute-done((bf16[1,2,2,64,1536]{4,3,2,1,0:T(8,128)(2,1)S(1)}, bf16[1,2,2,64,1536]{4,3,2,1,0:T(8,128)(2,1)S(1)}, u32[]{:S(2)}, u32[]{:S(2)}) %collective-permute-start.26) | collective-permute-done | bytes 786464 | tf_op jit(solution)/shard_map/ppermute | solution.py:311
  652.9 12.7 %collective-permute-done.31 = f32[8,48,128]{2,1,0:T(8,128)S(1)} collective-permute-done((f32[8,48,128]{2,1,0:T(8,128)S(1)}, f32[8,48,128]{2,1,0:T(8,128)S(1)}, u32[]{:S(2)}, u32[]{:S(2)}) %collective-permute-start.31) | collective-permute-done | bytes 196640 | tf_op jit(solution)/shard_map/ppermute | solution.py:311
  669.4 15.5 %collective-permute-done.32 = bf16[1,2,64,1536]{3,2,1,0:T(8,128)(2,1)S(1)} collective-permute-done((bf16[1,2,64,1536]{3,2,1,0:T(8,128)(2,1)S(1)}, bf16[1,2,64,1536]{3,2,1,0:T(8,128)(2,1)S(1)}, u32[]{:S(2)}, u32[]{:S(2)}) %collective-permute-start.32) | collective-permute-done | bytes 393248 | tf_op jit(solution)/shard_map/ppermute | solution.py:311
  695.3 6.1 multiply_subtract_fusion
  (490 shorter events, 233.8 us)
Async XLA Ops:
  7.2 101.1 %all-gather.4.cloned.1.call-start = ((), (), s32[]{:S(2)}) async-start(), calls=%async_computation.2 | async-start | bytes 8650752 | tf_op jit(solution)/shard_map/all_gather | solution.py:447
  10.0 215.5 %all-gather.6.cloned.1.call-start = ((), (), s32[]{:S(2)}) async-start(), calls=%async_computation.3 | async-start | bytes 17301504 | tf_op jit(solution)/shard_map/all_gather | solution.py:447
  24.8 53.5 %all-to-all-start = ((f32[16,3,6144]{2,1,0:T(4,128)}), f32[16,3,6144]{2,1,0:T(4,128)}, u32[]{:S(2)}, u32[]{:S(2)}) async-start(f32[16,3,6144]{2,1,0:T(4,128)} %reshape.779), calls=%async_computation | async-start | bytes 3145728 | tf_op jit(solution)/shard_map/all_to_all | solution.py:546
  32.3 479.9 %all-gather.8.cloned.1.call-start = ((), (), s32[]{:S(2)}) async-start(), calls=%async_computation.4 | async-start | bytes 1892352 | tf_op jit(solution)/shard_map/all_gather | solution.py:638
  36.1 32.0 %collective-permute-start = (bf16[3,256,1024]{2,1,0:T(8,128)(2,1)}, bf16[3,256,1024]{2,1,0:T(8,128)(2,1)}, u32[]{:S(2)}, u32[]{:S(2)}) collective-permute-start(bf16[3,256,1024]{2,1,0:T(8,128)(2,1)} %constant_dynamic-slice_fusion.9), channel_id=1, source_target_pairs={{1,0},{2,3},{5,4},{6,7},{9,8},{10,11},{13,12},{14,15},{17,16},{18,... | collective-permute-start | bytes 4718600 | tf_op jit(solution)/shard_map/ppermute | solution.py:542
  40.8 34.9 %collective-permute-start.2 = (bf16[1,256,1024]{2,1,0:T(8,128)(2,1)}, bf16[1,256,1024]{2,1,0:T(8,128)(2,1)S(1)}, u32[]{:S(2)}, u32[]{:S(2)}) collective-permute-start(bf16[1,256,1024]{2,1,0:T(8,128)(2,1)} %constant_dynamic-slice_fusion.7), channel_id=1, source_target_pairs={{0,1},{3,2},{4,5},{7,6},{8,9},{11,10},{12,13},{15,14},{16,17},{19,... | collective-permute-start | bytes 1572872 | tf_op jit(solution)/shard_map/ppermute | solution.py:542
  50.1 23.3 %collective-permute-start.1 = (bf16[2,256,1024]{2,1,0:T(8,128)(2,1)}, bf16[2,256,1024]{2,1,0:T(8,128)(2,1)}, u32[]{:S(2)}, u32[]{:S(2)}) collective-permute-start(bf16[2,256,1024]{2,1,0:T(8,128)(2,1)} %constant_dynamic-slice_fusion.8), channel_id=1, source_target_pairs={{2,1},{1,2},{6,5},{5,6},{10,9},{9,10},{14,13},{13,14},{18,17},{17,... | collective-permute-start | bytes 3145736 | tf_op jit(solution)/shard_map/ppermute | solution.py:542
  264.4 45.1 %collective-permute-start.3 = (bf16[8,64,2048]{2,1,0:T(8,128)(2,1)}, bf16[8,64,2048]{2,1,0:T(8,128)(2,1)}, u32[]{:S(2)}, u32[]{:S(2)}) collective-permute-start(bf16[8,64,2048]{2,1,0:T(8,128)(2,1)} %get-tuple-element.115), channel_id=1, source_target_pairs={{0,2},{2,0},{4,6},{6,4},{8,10},{10,8},{12,14},{14,12},{16,18},{18,... | collective-permute-start | bytes 6291464 | tf_op jit(solution)/shard_map/ppermute | solution.py:311
  264.6 44.9 %collective-permute-start.4 = (bf16[8,64,2048]{2,1,0:T(8,128)(2,1)S(1)}, bf16[8,64,2048]{2,1,0:T(8,128)(2,1)}, u32[]{:S(2)}, u32[]{:S(2)}) collective-permute-start(bf16[8,64,2048]{2,1,0:T(8,128)(2,1)S(1)} %get-tuple-element.116), channel_id=1, source_target_pairs={{0,2},{2,0},{4,6},{6,4},{8,10},{10,8},{12,14},{14,12},{16,18},{18,... | collective-permute-start | bytes 6291464 | tf_op jit(solution)/shard_map/ppermute | solution.py:311
  334.5 48.9 %collective-permute-start.7 = (bf16[8,64,2048]{2,1,0:T(8,128)(2,1)}, bf16[8,64,2048]{2,1,0:T(8,128)(2,1)}, u32[]{:S(2)}, u32[]{:S(2)}) collective-permute-start(bf16[8,64,2048]{2,1,0:T(8,128)(2,1)} %get-tuple-element.125), channel_id=1, source_target_pairs={{0,2},{2,0},{4,6},{6,4},{8,10},{10,8},{12,14},{14,12},{16,18},{18,... | collective-permute-start | bytes 6291464 | tf_op jit(solution)/shard_map/ppermute | solution.py:311
  334.8 48.6 %collective-permute-start.8 = (bf16[8,64,2048]{2,1,0:T(8,128)(2,1)}, bf16[8,64,2048]{2,1,0:T(8,128)(2,1)}, u32[]{:S(2)}, u32[]{:S(2)}) collective-permute-start(bf16[8,64,2048]{2,1,0:T(8,128)(2,1)} %get-tuple-element.126), channel_id=1, source_target_pairs={{0,2},{2,0},{4,6},{6,4},{8,10},{10,8},{12,14},{14,12},{16,18},{18,... | collective-permute-start | bytes 6291464 | tf_op jit(solution)/shard_map/ppermute | solution.py:311
  355.0 28.4 %collective-permute-start.5 = (bf16[1,2,2,64,2048]{4,3,2,1,0:T(8,128)(2,1)}, bf16[1,2,2,64,2048]{4,3,2,1,0:T(8,128)(2,1)}, u32[]{:S(2)}, u32[]{:S(2)}) collective-permute-start(bf16[1,2,2,64,2048]{4,3,2,1,0:T(8,128)(2,1)} %dynamic-slice_bitcast_fusion.9), channel_id=1, source_target_pairs={{0,4},{2,6},{4,0},{6,2},{8,12},{10,14},{12,8},{14,10},{16,20},{18,... | collective-permute-start | bytes 3145736 | tf_op jit(solution)/shard_map/ppermute | solution.py:311
  356.3 27.1 %collective-permute-start.6 = (bf16[1,2,2,64,2048]{4,3,2,1,0:T(8,128)(2,1)S(1)}, bf16[1,2,2,64,2048]{4,3,2,1,0:T(8,128)(2,1)}, u32[]{:S(2)}, u32[]{:S(2)}) collective-permute-start(bf16[1,2,2,64,2048]{4,3,2,1,0:T(8,128)(2,1)S(1)} %dynamic-slice_bitcast_fusion.8), channel_id=1, source_target_pairs={{0,1},{1,0},{2,3},{3,2},{4,5},{5,4},{6,7},{7,6},{8,9},{9,8},{10,11... | collective-permute-start | bytes 3145736 | tf_op jit(solution)/shard_map/ppermute | solution.py:311
  413.9 292.6 %reduce-scatter.2.cloned.1.call-start = ((), (), s32[]{:S(2)}) async-start(), calls=%async_computation.5 | async-start | bytes 4325376 | tf_op jit(solution)/shard_map/reduce_scatter | solution.py:640
  413.9 47.3 %collective-permute-start.9 = (bf16[1,2,64,2048]{3,2,1,0:T(8,128)(2,1)}, bf16[1,2,64,2048]{3,2,1,0:T(8,128)(2,1)}, u32[]{:S(2)}, u32[]{:S(2)}) collective-permute-start(bf16[1,2,64,2048]{3,2,1,0:T(8,128)(2,1)} %dynamic-slice_bitcast_fusion.15), channel_id=1, source_target_pairs={{0,1},{1,0},{2,3},{3,2},{4,5},{5,4},{6,7},{7,6},{8,9},{9,8},{10,11... | collective-permute-start | bytes 1572872 | tf_op jit(solution)/shard_map/ppermute | solution.py:311
  415.3 46.0 %collective-permute-start.10 = (bf16[1,2,64,2048]{3,2,1,0:T(8,128)(2,1)}, bf16[1,2,64,2048]{3,2,1,0:T(8,128)(2,1)}, u32[]{:S(2)}, u32[]{:S(2)}) collective-permute-start(bf16[1,2,64,2048]{3,2,1,0:T(8,128)(2,1)} %dynamic-slice_bitcast_fusion.14), channel_id=1, source_target_pairs={{0,4},{2,6},{4,0},{6,2},{8,12},{10,14},{12,8},{14,10},{16,20},{18,... | collective-permute-start | bytes 1572872 | tf_op jit(solution)/shard_map/ppermute | solution.py:311
  416.1 45.2 %collective-permute-start.11 = (bf16[1,2,2,64,2048]{4,3,2,1,0:T(8,128)(2,1)}, bf16[1,2,2,64,2048]{4,3,2,1,0:T(8,128)(2,1)}, u32[]{:S(2)}, u32[]{:S(2)}) collective-permute-start(bf16[1,2,2,64,2048]{4,3,2,1,0:T(8,128)(2,1)} %dynamic-slice_bitcast_fusion.7), channel_id=1, source_target_pairs={{0,4},{2,6},{4,0},{6,2},{8,12},{10,14},{12,8},{14,10},{16,20},{18,... | collective-permute-start | bytes 3145736 | tf_op jit(solution)/shard_map/ppermute | solution.py:311
  417.3 44.0 %collective-permute-start.12 = (bf16[1,2,2,64,2048]{4,3,1,2,0:T(8,128)(2,1)}, bf16[1,2,2,64,2048]{4,3,1,2,0:T(8,128)(2,1)}, u32[]{:S(2)}, u32[]{:S(2)}) collective-permute-start(bf16[1,2,2,64,2048]{4,3,1,2,0:T(8,128)(2,1)} %dynamic-slice_bitcast_fusion.6), channel_id=1, source_target_pairs={{0,1},{1,0},{2,3},{3,2},{4,5},{5,4},{6,7},{7,6},{8,9},{9,8},{10,11... | collective-permute-start | bytes 3145736 | tf_op jit(solution)/shard_map/ppermute | solution.py:311
  467.5 41.0 %collective-permute-start.13 = (bf16[1,2,64,2048]{3,2,1,0:T(8,128)(2,1)S(1)}, bf16[1,2,64,2048]{3,2,1,0:T(8,128)(2,1)S(1)}, u32[]{:S(2)}, u32[]{:S(2)}) collective-permute-start(bf16[1,2,64,2048]{3,2,1,0:T(8,128)(2,1)S(1)} %broadcast_select_fusion.1), channel_id=1, source_target_pairs={{0,16},{2,18},{4,20},{6,22},{8,24},{10,26},{12,28},{14,30},{16,0},... | collective-permute-start | bytes 1572872 | tf_op jit(solution)/shard_map/ppermute | solution.py:311
  469.1 39.4 %collective-permute-start.14 = (bf16[1,2,64,2048]{3,2,1,0:T(8,128)(2,1)S(1)}, bf16[1,2,64,2048]{3,2,1,0:T(8,128)(2,1)S(1)}, u32[]{:S(2)}, u32[]{:S(2)}) collective-permute-start(bf16[1,2,64,2048]{3,2,1,0:T(8,128)(2,1)S(1)} %dynamic-slice_bitcast_fusion.13), channel_id=1, source_target_pairs={{0,1},{1,0},{2,3},{3,2},{4,5},{5,4},{6,7},{7,6},{8,9},{9,8},{10,11... | collective-permute-start | bytes 1572872 | tf_op jit(solution)/shard_map/ppermute | solution.py:311
  470.3 38.1 %collective-permute-start.15 = (bf16[1,2,64,2048]{3,2,1,0:T(8,128)(2,1)S(1)}, bf16[1,2,64,2048]{3,2,1,0:T(8,128)(2,1)S(1)}, u32[]{:S(2)}, u32[]{:S(2)}) collective-permute-start(bf16[1,2,64,2048]{3,2,1,0:T(8,128)(2,1)S(1)} %dynamic-slice_bitcast_fusion.12), channel_id=1, source_target_pairs={{0,4},{2,6},{4,0},{6,2},{8,12},{10,14},{12,8},{14,10},{16,20},{18,... | collective-permute-start | bytes 1572872 | tf_op jit(solution)/shard_map/ppermute | solution.py:311
  520.2 27.4 %collective-permute-start.16 = (bf16[1,64,2048]{2,1,0:T(8,128)(2,1)}, bf16[1,64,2048]{2,1,0:T(8,128)(2,1)}, u32[]{:S(2)}, u32[]{:S(2)}) collective-permute-start(bf16[1,64,2048]{2,1,0:T(8,128)(2,1)} %dynamic-slice_bitcast_fusion.19), channel_id=1, source_target_pairs={{0,8},{2,10},{4,12},{6,14},{8,0},{10,2},{12,4},{14,6},{16,24},{18,... | collective-permute-start | bytes 786440 | tf_op jit(solution)/shard_map/ppermute | solution.py:311
  520.7 27.8 %collective-permute-start.17 = (bf16[1,2,64,2048]{3,2,1,0:T(8,128)(2,1)}, bf16[1,2,64,2048]{3,2,1,0:T(8,128)(2,1)}, u32[]{:S(2)}, u32[]{:S(2)}) collective-permute-start(bf16[1,2,64,2048]{3,2,1,0:T(8,128)(2,1)} %broadcast_select_fusion), channel_id=1, source_target_pairs={{0,16},{2,18},{4,20},{6,22},{8,24},{10,26},{12,28},{14,30},{16,0},... | collective-permute-start | bytes 1572872 | tf_op jit(solution)/shard_map/ppermute | solution.py:311
  584.7 39.7 %collective-permute-start.24 = (bf16[2,256,1024]{2,1,0:T(8,128)(2,1)}, bf16[2,256,1024]{2,1,0:T(8,128)(2,1)S(1)}, u32[]{:S(2)}, u32[]{:S(2)}) collective-permute-start(bf16[2,256,1024]{2,1,0:T(8,128)(2,1)} %dynamic-slice_convert_fusion.1), channel_id=1, source_target_pairs={{1,2},{2,1},{5,6},{6,5},{9,10},{10,9},{13,14},{14,13},{17,18},{18,... | collective-permute-start | bytes 3145736 | tf_op jit(solution)/shard_map/ppermute | solution.py:685
  585.5 40.9 %collective-permute-start.23 = (bf16[3,256,1024]{2,1,0:T(8,128)(2,1)S(1)}, bf16[3,256,1024]{2,1,0:T(8,128)(2,1)S(1)}, u32[]{:S(2)}, u32[]{:S(2)}) collective-permute-start(bf16[3,256,1024]{2,1,0:T(8,128)(2,1)S(1)} %copy-done.36), channel_id=1, source_target_pairs={{0,1},{3,2},{4,5},{7,6},{8,9},{11,10},{12,13},{15,14},{16,17},{19,... | collective-permute-start | bytes 4718600 | tf_op jit(solution)/shard_map/ppermute | solution.py:685
  591.4 34.9 %collective-permute-start.21 = (bf16[8,64,1536]{2,1,0:T(8,128)(2,1)S(1)}, bf16[8,64,1536]{2,1,0:T(8,128)(2,1)S(1)}, u32[]{:S(2)}, u32[]{:S(2)}) collective-permute-start(bf16[8,64,1536]{2,1,0:T(8,128)(2,1)S(1)} %get-tuple-element.319), channel_id=1, source_target_pairs={{0,2},{2,0},{4,6},{6,4},{8,10},{10,8},{12,14},{14,12},{16,18},{18,... | collective-permute-start | bytes 4718600 | tf_op jit(solution)/shard_map/ppermute | solution.py:311
  591.5 34.8 %collective-permute-start.20 = (bf16[8,64,1536]{2,1,0:T(8,128)(2,1)S(1)}, bf16[8,64,1536]{2,1,0:T(8,128)(2,1)S(1)}, u32[]{:S(2)}, u32[]{:S(2)}) collective-permute-start(bf16[8,64,1536]{2,1,0:T(8,128)(2,1)S(1)} %get-tuple-element.317), channel_id=1, source_target_pairs={{0,2},{2,0},{4,6},{6,4},{8,10},{10,8},{12,14},{14,12},{16,18},{18,... | collective-permute-start | bytes 4718600 | tf_op jit(solution)/shard_map/ppermute | solution.py:311
  598.8 25.6 %collective-permute-start.25 = (bf16[1,256,1024]{2,1,0:T(8,128)(2,1)S(1)}, bf16[1,256,1024]{2,1,0:T(8,128)(2,1)S(1)}, u32[]{:S(2)}, u32[]{:S(2)}) collective-permute-start(bf16[1,256,1024]{2,1,0:T(8,128)(2,1)S(1)} %copy-done.43), channel_id=1, source_target_pairs={{1,0},{2,3},{5,4},{6,7},{9,8},{10,11},{13,12},{14,15},{17,16},{18,... | collective-permute-start | bytes 1572872 | tf_op jit(solution)/shard_map/ppermute | solution.py:685
  627.7 22.1 %collective-permute-start.26 = (bf16[1,2,2,64,1536]{4,3,2,1,0:T(8,128)(2,1)S(1)}, bf16[1,2,2,64,1536]{4,3,2,1,0:T(8,128)(2,1)S(1)}, u32[]{:S(2)}, u32[]{:S(2)}) collective-permute-start(bf16[1,2,2,64,1536]{4,3,2,1,0:T(8,128)(2,1)S(1)} %dynamic-slice_bitcast_fusion.11), channel_id=1, source_target_pairs={{0,4},{2,6},{4,0},{6,2},{8,12},{10,14},{12,8},{14,10},{16,20},{18,... | collective-permute-start | bytes 2359304 | tf_op jit(solution)/shard_map/ppermute | solution.py:311
  629.8 20.0 %collective-permute-start.27 = (bf16[1,2,2,64,1536]{4,3,2,1,0:T(8,128)(2,1)S(1)}, bf16[1,2,2,64,1536]{4,3,2,1,0:T(8,128)(2,1)S(1)}, u32[]{:S(2)}, u32[]{:S(2)}) collective-permute-start(bf16[1,2,2,64,1536]{4,3,2,1,0:T(8,128)(2,1)S(1)} %dynamic-slice_bitcast_fusion.10), channel_id=1, source_target_pairs={{0,1},{1,0},{2,3},{3,2},{4,5},{5,4},{6,7},{7,6},{8,9},{9,8},{10,11... | collective-permute-start | bytes 2359304 | tf_op jit(solution)/shard_map/ppermute | solution.py:311
  665.9 19.1 %collective-permute-start.32 = (bf16[1,2,64,1536]{3,2,1,0:T(8,128)(2,1)S(1)}, bf16[1,2,64,1536]{3,2,1,0:T(8,128)(2,1)S(1)}, u32[]{:S(2)}, u32[]{:S(2)}) collective-permute-start(bf16[1,2,64,1536]{3,2,1,0:T(8,128)(2,1)S(1)} %broadcast_select_fusion.2), channel_id=1, source_target_pairs={{0,16},{2,18},{4,20},{6,22},{8,24},{10,26},{12,28},{14,30},{16,0},... | collective-permute-start | bytes 1179656 | tf_op jit(solution)/shard_map/ppermute | solution.py:311
  666.0 19.0 %collective-permute-start.33 = (f32[16,48,128]{2,1,0:T(8,128)S(1)}, f32[16,48,128]{2,1,0:T(8,128)S(1)}, u32[]{:S(2)}, u32[]{:S(2)}) collective-permute-start(f32[16,48,128]{2,1,0:T(8,128)S(1)} %pad_maximum_fusion.5), channel_id=1, source_target_pairs={{0,2},{2,0},{4,6},{6,4},{8,10},{10,8},{12,14},{14,12},{16,18},{18,... | collective-permute-start | bytes 1179656 | tf_op jit(solution)/shard_map/ppermute | solution.py:311
  (120 other events, 2018.9 us)
Sparse Core Ops, SparseCore 0:
  11.4 96.8 all-gather.3
  111.7 113.7 all-gather.5
  414.0 55.5 all-gather.7
  471.7 143.0 reduce-scatter.1

commit v3 on v2

--- a/solution.py
+++ b/solution.py
@@ -655,8 +655,7 @@
                 heads_grad[h],
             )
         )
-    early_all, qkv_grad = lax.optimization_barrier((early_all, qkv_grad))
-    early_all = early_all.reshape(device_count, -1)
+    early_all = Received([early_all])
     norm_grad_ext, norm_ext = beside(
         [down_sum, up_sum],
         lambda parts: (sum(dot_nt(parts[0][h], qkv_whole[h]) for h in chunks), parts[1]),
@@ -680,22 +679,31 @@
         for (size, pieces), (source, target) in zip(rounds, places)
     ]
     qkv_grad, sent = lax.optimization_barrier((qkv_grad, sent))
-    returned = Received(
-        [
-            lax.ppermute(part, both, [(piece[1], piece[0]) for piece in pieces])
-            for part, (size, pieces) in zip(sent, rounds)
-        ]
-    )
-    qkv_wgrad = beside(
-        [late_sums, down_sum, up_sum],
-        lambda parts: [dot_tn(attn_ext, part).astype(jnp.bfloat16) for part in parts],
-        qkv_grad,
-    )
+    got = [
+        lax.ppermute(part, both, [(piece[1], piece[0]) for piece in pieces])
+        for part, (size, pieces) in zip(sent, rounds)
+    ]
+    large_rounds = len(rounds) * 2 // 3
+    later_got, first_got = Received(got[:large_rounds]), got[large_rounds:]
+
+    def qkv_backward(parts):
+        return [dot_tn(attn_ext, part).astype(jnp.bfloat16) for part in parts]
+
+    half = (tensor_count + 1) // 2
+    first_wgrad = beside([late_sums], qkv_backward, qkv_grad[:half])
+    first_wgrad, first_got, rest = lax.optimization_barrier(
+        (first_wgrad, first_got, qkv_grad[half:])
+    )
+    qkv_wgrad = first_wgrad + beside([late_sums, down_sum, up_sum], qkv_backward, rest)
     qkv_sum = SumChain([qkv_wgrad])
     chains = [qkv_sum, late_sums, down_sum, up_sum]
-    advance(chains + [returned])
+    advance(chains + [later_got])
+    advance(chains + [early_all])
+    early_all = early_all.got[0].reshape(device_count, -1)
     attn_norm_grad = lax.dynamic_slice_in_dim(norm_grad_ext, start_block, block_count, 0)
-    for (size, pieces), (source, target), got in zip(rounds, places, returned.got):
+    for (size, pieces), (source, target), got in zip(
+        rounds, places, list(later_got.got) + list(first_got)
+    ):
         old = lax.dynamic_slice_in_dim(attn_norm_grad, source, size // block_rows, 0)
         attn_norm_grad = lax.dynamic_update_slice_in_dim(
             attn_norm_grad, old + got.astype(jnp.float32), source, 0

time: 722 us -> 698 us (0.967)
  waiting for transfers between devices: 120 us -> 81.4 us
  matrix products: 228 us -> 242 us
    ppermute x29, waiting for transfers between devices: 45.7 us -> 25.2 us  [swap(): return lax.ppermute(values, axis, route)]
    ppermute x3, waiting for transfers between devices: 24.5 us -> 6.07 us  [on_device(): lax.ppermute(part, both, [(piece[1], piece[0]) for piece in pieces])]
    convert_element_type x3, local copies, waits for them, and re-layouts: 8.51 us -> 0.47 us  [on_device(): lax.dynamic_slice_in_dim(norm_grad_ext, target, size // block_rows, 0)]
  transfers between devices with their start and end apart: 40 -> 40, of which waited for: 10 -> 12; matrix products, arithmetic and copies ran while one was open for 42% -> 45% of each run, Pallas kernels for 16% -> 17%
where the time goes in v3:
time: 698 us; the launch traced here: 691 us
  matrix products  242 us (35%)
  Pallas kernels  116 us (17%)
  other arithmetic  106 us (15%)
  waiting for transfers between devices  81.4 us (12%)
  local copies, waits for them, and re-layouts  64.1 us (9%)
  starting transfers between devices  49.6 us (7%)
  between operations  31.2 us (4%)
    dot_general x8, matrix products, dot_nt(): lax.dot_general(left, right, (((1,), (1,)), ((), ())), preferred_element_...  87.5 us
    dot_general x9, matrix products, dot_nn(): lax.dot_general(left, right, (((1,), (0,)), ((), ())), preferred_element_...  83.8 us
    pallas_call x2, Pallas kernels, attend_backward(): pl.pallas_call(backward_kernel, grid_spec=pltpu.PrefetchScalarGridSpec(nu...  75.1 us
    dot_general x8, matrix products, dot_tn(): lax.dot_general(left, right, (((0,), (0,)), ((), ())), preferred_element_...  50.4 us
    all_gather x2, waiting for transfers between devices, gather_rows(): whole = lax.all_gather(shard, ('tensor', 'dp'), axis=0, tiled=True)  47.7 us
    pallas_call x2, Pallas kernels, attend_forward(): pl.pallas_call(forward_kernel, grid_spec=pltpu.PrefetchScalarGridSpec(num...  41.4 us
    ppermute x29, starting transfers between devices, swap(): return lax.ppermute(values, axis, route)  25.5 us
    ppermute x29, waiting for transfers between devices, swap(): return lax.ppermute(values, axis, route)  25.2 us
  transfers between devices with their start and end apart: 40, of which 12 were waited for; matrix products, arithmetic and copies ran while one was open for 45% of the time, Pallas kernels for 17%

profile of v3, /device:TPU:0, one launch (start us, length us, event | category | flops | bytes accessed | tf_op | source)
XLA Modules:
  0.0 690.6 jit_solution(236080103286252191)
XLA Ops:
  24.8 7.4 %all-to-all-start = ((f32[16,3,6144]{2,1,0:T(4,128)}), f32[16,3,6144]{2,1,0:T(4,128)}, u32[]{:S(2)}, u32[]{:S(2)}) async-start(f32[16,3,6144]{2,1,0:T(4,128)} %reshape.779), calls=%async_computation | async-start | bytes 3145728 | tf_op jit(solution)/shard_map/all_to_all | solution.py:546
  81.2 5.8 add_convert_fusion.4
  89.8 18.5 %all-gather.4.cloned.1.call-done = bf16[2048,2048]{1,0:T(8,128)(2,1)} async-done(((bf16[64,2048]{1,0:T(8,128)(2,1)}), bf16[2048,2048]{1,0:T(8,128)(2,1)}) %all-gather.4.cloned.1.call-update) | async-done | bytes 8388624 | tf_op jit(solution)/shard_map/all_gather | solution.py:447
  108.3 11.4 %add_convert_fusion.1.query_ref.key_ref.value_ref = bf16[2048,1536]{1,0:T(8,128)(2,1)} fusion(bf16[2048,1024]{1,0:T(8,128)(2,1)} %bitcast.14, f32[1536]{0:T(1024)S(1)} %get-tuple-element.363, bf16[2,1024,2048]{2,1,0:T(8,128)(2,1)} %bitcast.447), kind=kOutput, calls=%fused_computation.7 | convolution fusion | flops 6448742400 | bytes 13637632 | tf_op jit(solution)/shard_map/dot_general | solution.py:103
  119.7 20.5 %attend_forward.2 = (bf16[1280,512]{1,0:T(8,128)(2,1)S(1)}, f32[5,8,256]{2,1,0:T(8,128)S(1)}) custom-call(s32[1]{0:T(128)} %dynamic_slice.203.start_ref, bf16[2048,1536]{1,0:T(8,128)(2,1)} %add_convert_fusion.1.query_ref.key_ref.value_ref, bf16[2048,1536]{1,0:T(8,128)(2,1)} %add_convert_fusion.1.query_ref.key_ref.value_ref, ...), custom_call_target="tpu_custom_call" | custom-call | flops 10737418240 | bytes 12582912 | tf_op jit(solution)/shard_map/attend_forward/pallas_call | solution.py:240
  143.6 11.4 %add_convert_fusion.query_ref.key_ref.value_ref = bf16[2048,1536]{1,0:T(8,128)(2,1)} fusion(bf16[2048,1024]{1,0:T(8,128)(2,1)} %bitcast.14, f32[1536]{0:T(1024)S(1)} %get-tuple-element.362, bf16[2,1024,2048]{2,1,0:T(8,128)(2,1)} %bitcast.449), kind=kOutput, calls=%fused_computation.6 | convolution fusion | flops 6448742400 | bytes 13637632 | tf_op jit(solution)/shard_map/dot_general | solution.py:103
  154.9 20.9 %attend_forward.3 = (bf16[1280,512]{1,0:T(8,128)(2,1)S(1)}, f32[5,8,256]{2,1,0:T(8,128)S(1)}) custom-call(s32[1]{0:T(128)} %dynamic_slice.203.start_ref, bf16[2048,1536]{1,0:T(8,128)(2,1)} %add_convert_fusion.query_ref.key_ref.value_ref, bf16[2048,1536]{1,0:T(8,128)(2,1)} %add_convert_fusion.query_ref.key_ref.value_ref, ...), custom_call_target="tpu_custom_call" | custom-call | flops 10737418240 | bytes 12582912 | tf_op jit(solution)/shard_map/attend_forward/pallas_call | solution.py:240
  175.9 7.9 %fusion.82 = (f32[1280]{0:T(1024)S(1)}, f32[1280,1024]{1,0:T(8,128)}, f32[1280,1024]{1,0:T(8,128)}) fusion(f32[1280,1024]{1,0:T(8,128)S(1)} %bitcast.389, f32[5,1024]{1,0:T(8,128)S(1)} %get-tuple-element.338, f32[1024]{0:T(1024)S(1)} %get-tuple-element.346, f32[1280,1024]{1,0:T(8,128)S(1)} %fusion.42, ...), kind=kOutput, calls=%fused_computation.294 | convolution fusion | flops 1348729600 | bytes 23360512 | tf_op jit(solution)/shard_map/dot_general | solution.py:97
  188.2 8.2 %convert_reduce_fusion.4 = (f32[1024]{0:T(1024)}, bf16[1280,1024]{1,0:T(8,128)(2,1)}, bf16[1280,1024]{1,0:T(8,128)(2,1)S(1)}) fusion(f32[1280,1024]{1,0:T(8,128)} %param.38, f32[5,1024]{1,0:T(8,128)S(1)} %get-tuple-element.333, f32[5,1024]{1,0:T(8,128)S(1)} %get-tuple-element.334, f32[5,1024]{1,0:T(8,128)S(1)} %get-tuple-element.335, ...), kind=kLoop, calls=%fused_computation.50 | loop fusion | flops 11795456 | bytes 15804416 | tf_op jit(solution)/shard_map/reduce_sum | solution.py:629
  196.4 29.2 %all-gather.6.cloned.1.call-done = bf16[2048,4096]{1,0:T(8,128)(2,1)} async-done(((bf16[64,4096]{1,0:T(8,128)(2,1)}), bf16[2048,4096]{1,0:T(8,128)(2,1)}) %all-gather.6.cloned.1.call-update) | async-done | bytes 16777232 | tf_op jit(solution)/shard_map/all_gather | solution.py:447
  225.6 7.4 %fusion.26 = f32[1280,2048]{1,0:T(8,128)S(1)} fusion(bf16[1280,1024]{1,0:T(8,128)(2,1)S(1)} %get-tuple-element.371, bf16[2,1024,4096]{2,1,0:T(8,128)(2,1)} %bitcast.430), kind=kOutput, calls=%fused_computation.83 | convolution fusion | flops 5368709120 | bytes 17301504 | tf_op jit(solution)/shard_map/dot_general | solution.py:103
  233.1 13.6 %fusion.23 = f32[1280,2048]{1,0:T(8,128)} fusion(bf16[1280,1024]{1,0:T(8,128)(2,1)S(1)} %get-tuple-element.371, bf16[2,1024,4096]{2,1,0:T(8,128)(2,1)} %bitcast.431), kind=kOutput, calls=%fused_computation.80 | convolution fusion | flops 5368709120 | bytes 17301504 | tf_op jit(solution)/shard_map/dot_general | solution.py:103
  246.7 6.4 convolution_convert_fusion.4
  253.1 9.1 %convolution_convert_fusion.5 = bf16[1024,2048]{1,0:T(8,128)(2,1)S(1)} fusion(bf16[1280,1024]{1,0:T(8,128)(2,1)S(1)} %copy-done.27, f32[1280,2048]{1,0:T(8,128)} %fusion.23, f32[2048]{0:T(1024)S(1)} %get-tuple-element.344), kind=kOutput, calls=%fused_computation.78 | convolution fusion | flops 5397020672 | bytes 17309696 | tf_op jit(solution)/shard_map/dot_general | solution.py:109
  264.9 17.6 %convert_reduce_fusion.3 = (f32[2048]{0:T(1024)}, bf16[1280,2048]{1,0:T(8,128)(2,1)}) fusion(f32[1280,2048]{1,0:T(8,128)} %fusion.23, f32[2048]{0:T(1024)S(1)} %get-tuple-element.344, bf16[1280,1024]{1,0:T(8,128)(2,1)S(1)} %copy-done.27, bf16[2,1024,4096]{2,1,0:T(8,128)(2,1)} %bitcast.432), kind=kOutput, calls=%fused_computation.23 | convolution fusion | flops 5429000192 | bytes 22560768 | tf_op jit(solution)/shard_map/dot_general | solution.py:103
  282.6 14.6 %convert_reduce_fusion.2 = (f32[2048]{0:T(1024)}, bf16[1280,2048]{1,0:T(8,128)(2,1)S(1)}) fusion(f32[1280,2048]{1,0:T(8,128)S(1)} %fusion.26, f32[2048]{0:T(1024)S(1)} %get-tuple-element.343, bf16[1280,1024]{1,0:T(8,128)(2,1)S(1)} %copy-done.28, bf16[2,1024,4096]{2,1,0:T(8,128)(2,1)} %bitcast.433), kind=kOutput, calls=%fused_computation.22 | convolution fusion | flops 5429000192 | bytes 22560768 | tf_op jit(solution)/shard_map/dot_general | solution.py:103
  297.1 12.2 %fusion.25 = f32[1280,1024]{1,0:T(8,128)} fusion(bf16[2,1024,4096]{2,1,0:T(8,128)(2,1)} %bitcast.434, f32[1280,2048]{1,0:T(8,128)} %fusion.23, f32[2048]{0:T(1024)S(1)} %get-tuple-element.344), kind=kOutput, calls=%fused_computation.82 | convolution fusion | flops 5394923520 | bytes 19931136 | tf_op jit(solution)/shard_map/dot_general | solution.py:97
  315.7 6.5 convolution_convert_fusion.3
  324.7 6.0 convolution_convert_fusion.2
  335.1 9.1 %fusion.22 = f32[1280,1024]{1,0:T(8,128)S(1)} fusion(bf16[1280,2048]{1,0:T(8,128)(2,1)} %get-tuple-element.121, bf16[2,1024,4096]{2,1,0:T(8,128)(2,1)} %bitcast.435), kind=kOutput, calls=%fused_computation.79 | convolution fusion | flops 5368709120 | bytes 14680064 | tf_op jit(solution)/shard_map/dot_general | solution.py:97
  344.3 10.7 %fusion.21 = (f32[1280]{0:T(1024)S(1)}, f32[1280]{0:T(1024)S(1)}, f32[1280,1024]{1,0:T(8,128)}) fusion(f32[5,1024]{1,0:T(8,128)S(1)} %get-tuple-element.335, f32[1280]{0:T(1024)S(1)} %copy-done.57, f32[1280,1024]{1,0:T(8,128)S(1)} %bitcast.398, f32[1280]{0:T(1024)S(1)} %copy-done.47, f32[1280,1024]{1,0:T(8,128)S(1)} %fusion.22, ...), kind=kOutput, calls=%fused_computation.62 | convolution fusion | flops 5377882112 | bytes 25206784 | tf_op jit(solution)/shard_map/dot_general | solution.py:97
  357.1 18.3 %convert_reduce_fusion.5 = (f32[1024]{0:T(1024)S(1)}, bf16[1280,1024]{1,0:T(8,128)(2,1)S(1)}, f32[1280,1024]{1,0:T(8,128)}, f32[1280,1024]{1,0:T(8,128)S(1)}) fusion(f32[5,1024]{1,0:T(8,128)S(1)} %copy-done.35, f32[1280,1024]{1,0:T(8,128)} %param.38, f32[1280]{0:T(1024)S(1)} %broadcast_multiply_fusion.2, f32[1280,1024]{1,0:T(8,128)} %get-tuple-element.298, ...), kind=kOutput, calls=%fused_computation.51 | convolution fusion | flops 5415894016 | bytes 48857088 | tf_op jit(solution)/shard_map/dot_general | solution.py:97
  375.4 8.0 %multiply_reduce_fusion.1 = (f32[5,1024]{1,0:T(8,128)S(1)}, f32[5,256,1024]{2,1,0:T(8,128)S(1)}) fusion(f32[5,256,1024]{2,1,0:T(8,128)} %bitcast.408, f32[5,256,1024]{2,1,0:T(8,128)S(1)} %bitcast.413, f32[5,256]{1,0:T(8,128)S(1)} %div.154, f32[5,256]{1,0:T(8,128)S(1)} %copy-done.61, f32[5,256,1024]{2,1,0:T(8,128)} %bitcast.384, ...), kind=kLoop, calls=%fused_computation.47 | loop fusion | flops 15723520 | bytes 31539200 | tf_op jit(solution)/shard_map/reduce_sum | solution.py:563
  417.4 37.5 %attend_backward.2 = bf16[2048,1536]{1,0:T(8,128)(2,1)} custom-call(s32[1]{0:T(128)} %dynamic_slice.203.start_ref, bf16[2048,1536]{1,0:T(8,128)(2,1)} %add_convert_fusion.1.query_ref.key_ref.value_ref, bf16[2048,1536]{1,0:T(8,128)(2,1)} %add_convert_fusion.1.query_ref.key_ref.value_ref, bf16[2048,1536]{1,0:T(8,128)(2,1)} %add_convert_fusion.1.query_ref.key_ref.value_ref, ...), custom_call_target="tpu_custom_call" | custom-call | flops 26843545600 | bytes 18874368 | tf_op jit(solution)/shard_map/attend_backward/pallas_call | solution.py:269
  469.7 37.6 %attend_backward.3 = bf16[2048,1536]{1,0:T(8,128)(2,1)} custom-call(s32[1]{0:T(128)} %dynamic_slice.203.start_ref, bf16[2048,1536]{1,0:T(8,128)(2,1)} %add_convert_fusion.query_ref.key_ref.value_ref, bf16[2048,1536]{1,0:T(8,128)(2,1)} %add_convert_fusion.query_ref.key_ref.value_ref, bf16[2048,1536]{1,0:T(8,128)(2,1)} %add_convert_fusion.query_ref.key_ref.value_ref, ...), custom_call_target="tpu_custom_call" | custom-call | flops 26843545600 | bytes 18874368 | tf_op jit(solution)/shard_map/attend_backward/pallas_call | solution.py:269
  513.6 11.0 %fusion.29 = f32[2048,1024]{1,0:T(8,128)} fusion(bf16[2048,1536]{1,0:T(8,128)(2,1)S(1)} %bitcast.422, bf16[2,1024,2048]{2,1,0:T(8,128)(2,1)} %bitcast.453), kind=kOutput, calls=%fused_computation.92 | convolution fusion | flops 6442450944 | bytes 17825792 | tf_op jit(solution)/shard_map/dot_general | solution.py:97
  524.6 15.1 %convolution_add_fusion.1 = f32[2048,1024]{1,0:T(8,128)S(1)} fusion(f32[2048,1024]{1,0:T(8,128)} %fusion.29, bf16[2048,1536]{1,0:T(8,128)(2,1)} %attend_backward.3, bf16[2,1024,2048]{2,1,0:T(8,128)(2,1)} %bitcast.454), kind=kOutput, calls=%fused_computation.72 | convolution fusion | flops 6444548096 | bytes 26214400 | tf_op jit(solution)/shard_map/dot_general | solution.py:97
  545.2 8.8 %convolution_convert_fusion.1 = bf16[1024,1536]{1,0:T(8,128)(2,1)S(1)} fusion(bf16[2048,1024]{1,0:T(8,128)(2,1)} %bitcast.14, bf16[2048,1536]{1,0:T(8,128)(2,1)S(1)} %bitcast.422), kind=kOutput, calls=%fused_computation.74 | convolution fusion | flops 6444023808 | bytes 13631488 | tf_op jit(solution)/shard_map/dot_general | solution.py:109
  557.9 5.9 collective-permute-start.25
  569.5 10.5 %convolution_convert_fusion = bf16[1024,1536]{1,0:T(8,128)(2,1)S(1)} fusion(bf16[2048,1024]{1,0:T(8,128)(2,1)} %bitcast.14, bf16[2048,1536]{1,0:T(8,128)(2,1)} %attend_backward.3), kind=kOutput, calls=%fused_computation.73 | convolution fusion | flops 6444023808 | bytes 13631488 | tf_op jit(solution)/shard_map/dot_general | solution.py:109
  609.9 12.4 %collective-permute-done.27 = bf16[1,2,2,64,1536]{4,3,2,1,0:T(8,128)(2,1)} collective-permute-done((bf16[1,2,2,64,1536]{4,3,2,1,0:T(8,128)(2,1)}, bf16[1,2,2,64,1536]{4,3,2,1,0:T(8,128)(2,1)}, u32[]{:S(2)}, u32[]{:S(2)}) %collective-permute-start.27) | collective-permute-done | bytes 786464 | tf_op jit(solution)/shard_map/ppermute | solution.py:311
  663.4 6.4 multiply_subtract_fusion
  (471 shorter events, 233.8 us)
Async XLA Ops:
  7.2 101.1 %all-gather.4.cloned.1.call-start = ((), (), s32[]{:S(2)}) async-start(), calls=%async_computation.2 | async-start | bytes 8650752 | tf_op jit(solution)/shard_map/all_gather | solution.py:447
  10.0 215.7 %all-gather.6.cloned.1.call-start = ((), (), s32[]{:S(2)}) async-start(), calls=%async_computation.3 | async-start | bytes 17301504 | tf_op jit(solution)/shard_map/all_gather | solution.py:447
  24.8 53.5 %all-to-all-start = ((f32[16,3,6144]{2,1,0:T(4,128)}), f32[16,3,6144]{2,1,0:T(4,128)}, u32[]{:S(2)}, u32[]{:S(2)}) async-start(f32[16,3,6144]{2,1,0:T(4,128)} %reshape.779), calls=%async_computation | async-start | bytes 3145728 | tf_op jit(solution)/shard_map/all_to_all | solution.py:546
  32.3 577.6 %all-gather.8.cloned.1.call-start = ((), (), s32[]{:S(2)}) async-start(), calls=%async_computation.4 | async-start | bytes 1892352 | tf_op jit(solution)/shard_map/all_gather | solution.py:638
  36.1 32.0 %collective-permute-start = (bf16[3,256,1024]{2,1,0:T(8,128)(2,1)}, bf16[3,256,1024]{2,1,0:T(8,128)(2,1)}, u32[]{:S(2)}, u32[]{:S(2)}) collective-permute-start(bf16[3,256,1024]{2,1,0:T(8,128)(2,1)} %constant_dynamic-slice_fusion.9), channel_id=1, source_target_pairs={{1,0},{2,3},{5,4},{6,7},{9,8},{10,11},{13,12},{14,15},{17,16},{18,... | collective-permute-start | bytes 4718600 | tf_op jit(solution)/shard_map/ppermute | solution.py:542
  40.8 34.9 %collective-permute-start.2 = (bf16[1,256,1024]{2,1,0:T(8,128)(2,1)}, bf16[1,256,1024]{2,1,0:T(8,128)(2,1)S(1)}, u32[]{:S(2)}, u32[]{:S(2)}) collective-permute-start(bf16[1,256,1024]{2,1,0:T(8,128)(2,1)} %constant_dynamic-slice_fusion.7), channel_id=1, source_target_pairs={{0,1},{3,2},{4,5},{7,6},{8,9},{11,10},{12,13},{15,14},{16,17},{19,... | collective-permute-start | bytes 1572872 | tf_op jit(solution)/shard_map/ppermute | solution.py:542
  50.1 23.3 %collective-permute-start.1 = (bf16[2,256,1024]{2,1,0:T(8,128)(2,1)}, bf16[2,256,1024]{2,1,0:T(8,128)(2,1)}, u32[]{:S(2)}, u32[]{:S(2)}) collective-permute-start(bf16[2,256,1024]{2,1,0:T(8,128)(2,1)} %constant_dynamic-slice_fusion.8), channel_id=1, source_target_pairs={{2,1},{1,2},{6,5},{5,6},{10,9},{9,10},{14,13},{13,14},{18,17},{17,... | collective-permute-start | bytes 3145736 | tf_op jit(solution)/shard_map/ppermute | solution.py:542
  264.4 44.9 %collective-permute-start.3 = (bf16[8,64,2048]{2,1,0:T(8,128)(2,1)}, bf16[8,64,2048]{2,1,0:T(8,128)(2,1)}, u32[]{:S(2)}, u32[]{:S(2)}) collective-permute-start(bf16[8,64,2048]{2,1,0:T(8,128)(2,1)} %get-tuple-element.115), channel_id=1, source_target_pairs={{0,2},{2,0},{4,6},{6,4},{8,10},{10,8},{12,14},{14,12},{16,18},{18,... | collective-permute-start | bytes 6291464 | tf_op jit(solution)/shard_map/ppermute | solution.py:311
  264.7 44.6 %collective-permute-start.4 = (bf16[8,64,2048]{2,1,0:T(8,128)(2,1)S(1)}, bf16[8,64,2048]{2,1,0:T(8,128)(2,1)}, u32[]{:S(2)}, u32[]{:S(2)}) collective-permute-start(bf16[8,64,2048]{2,1,0:T(8,128)(2,1)S(1)} %get-tuple-element.116), channel_id=1, source_target_pairs={{0,2},{2,0},{4,6},{6,4},{8,10},{10,8},{12,14},{14,12},{16,18},{18,... | collective-permute-start | bytes 6291464 | tf_op jit(solution)/shard_map/ppermute | solution.py:311
  334.5 49.0 %collective-permute-start.7 = (bf16[8,64,2048]{2,1,0:T(8,128)(2,1)}, bf16[8,64,2048]{2,1,0:T(8,128)(2,1)}, u32[]{:S(2)}, u32[]{:S(2)}) collective-permute-start(bf16[8,64,2048]{2,1,0:T(8,128)(2,1)} %get-tuple-element.125), channel_id=1, source_target_pairs={{0,2},{2,0},{4,6},{6,4},{8,10},{10,8},{12,14},{14,12},{16,18},{18,... | collective-permute-start | bytes 6291464 | tf_op jit(solution)/shard_map/ppermute | solution.py:311
  334.8 48.6 %collective-permute-start.8 = (bf16[8,64,2048]{2,1,0:T(8,128)(2,1)}, bf16[8,64,2048]{2,1,0:T(8,128)(2,1)}, u32[]{:S(2)}, u32[]{:S(2)}) collective-permute-start(bf16[8,64,2048]{2,1,0:T(8,128)(2,1)} %get-tuple-element.126), channel_id=1, source_target_pairs={{0,2},{2,0},{4,6},{6,4},{8,10},{10,8},{12,14},{14,12},{16,18},{18,... | collective-permute-start | bytes 6291464 | tf_op jit(solution)/shard_map/ppermute | solution.py:311
  355.0 28.5 %collective-permute-start.5 = (bf16[1,2,2,64,2048]{4,3,2,1,0:T(8,128)(2,1)}, bf16[1,2,2,64,2048]{4,3,2,1,0:T(8,128)(2,1)}, u32[]{:S(2)}, u32[]{:S(2)}) collective-permute-start(bf16[1,2,2,64,2048]{4,3,2,1,0:T(8,128)(2,1)} %dynamic-slice_bitcast_fusion.9), channel_id=1, source_target_pairs={{0,4},{2,6},{4,0},{6,2},{8,12},{10,14},{12,8},{14,10},{16,20},{18,... | collective-permute-start | bytes 3145736 | tf_op jit(solution)/shard_map/ppermute | solution.py:311
  356.2 27.3 %collective-permute-start.6 = (bf16[1,2,2,64,2048]{4,3,2,1,0:T(8,128)(2,1)S(1)}, bf16[1,2,2,64,2048]{4,3,2,1,0:T(8,128)(2,1)}, u32[]{:S(2)}, u32[]{:S(2)}) collective-permute-start(bf16[1,2,2,64,2048]{4,3,2,1,0:T(8,128)(2,1)S(1)} %dynamic-slice_bitcast_fusion.8), channel_id=1, source_target_pairs={{0,1},{1,0},{2,3},{3,2},{4,5},{5,4},{6,7},{7,6},{8,9},{9,8},{10,11... | collective-permute-start | bytes 3145736 | tf_op jit(solution)/shard_map/ppermute | solution.py:311
  413.2 268.6 %reduce-scatter.2.cloned.1.call-start = ((), (), s32[]{:S(2)}) async-start(), calls=%async_computation.5 | async-start | bytes 4325376 | tf_op jit(solution)/shard_map/reduce_scatter | solution.py:640
  413.3 47.2 %collective-permute-start.9 = (bf16[1,2,64,2048]{3,2,1,0:T(8,128)(2,1)}, bf16[1,2,64,2048]{3,2,1,0:T(8,128)(2,1)}, u32[]{:S(2)}, u32[]{:S(2)}) collective-permute-start(bf16[1,2,64,2048]{3,2,1,0:T(8,128)(2,1)} %dynamic-slice_bitcast_fusion.15), channel_id=1, source_target_pairs={{0,1},{1,0},{2,3},{3,2},{4,5},{5,4},{6,7},{7,6},{8,9},{9,8},{10,11... | collective-permute-start | bytes 1572872 | tf_op jit(solution)/shard_map/ppermute | solution.py:311
  414.4 46.1 %collective-permute-start.10 = (bf16[1,2,64,2048]{3,2,1,0:T(8,128)(2,1)}, bf16[1,2,64,2048]{3,2,1,0:T(8,128)(2,1)}, u32[]{:S(2)}, u32[]{:S(2)}) collective-permute-start(bf16[1,2,64,2048]{3,2,1,0:T(8,128)(2,1)} %dynamic-slice_bitcast_fusion.14), channel_id=1, source_target_pairs={{0,4},{2,6},{4,0},{6,2},{8,12},{10,14},{12,8},{14,10},{16,20},{18,... | collective-permute-start | bytes 1572872 | tf_op jit(solution)/shard_map/ppermute | solution.py:311
  415.3 45.2 %collective-permute-start.11 = (bf16[1,2,2,64,2048]{4,3,2,1,0:T(8,128)(2,1)}, bf16[1,2,2,64,2048]{4,3,2,1,0:T(8,128)(2,1)}, u32[]{:S(2)}, u32[]{:S(2)}) collective-permute-start(bf16[1,2,2,64,2048]{4,3,2,1,0:T(8,128)(2,1)} %dynamic-slice_bitcast_fusion.7), channel_id=1, source_target_pairs={{0,4},{2,6},{4,0},{6,2},{8,12},{10,14},{12,8},{14,10},{16,20},{18,... | collective-permute-start | bytes 3145736 | tf_op jit(solution)/shard_map/ppermute | solution.py:311
  416.5 44.1 %collective-permute-start.12 = (bf16[1,2,2,64,2048]{4,3,1,2,0:T(8,128)(2,1)}, bf16[1,2,2,64,2048]{4,3,1,2,0:T(8,128)(2,1)}, u32[]{:S(2)}, u32[]{:S(2)}) collective-permute-start(bf16[1,2,2,64,2048]{4,3,1,2,0:T(8,128)(2,1)} %dynamic-slice_bitcast_fusion.6), channel_id=1, source_target_pairs={{0,1},{1,0},{2,3},{3,2},{4,5},{5,4},{6,7},{7,6},{8,9},{9,8},{10,11... | collective-permute-start | bytes 3145736 | tf_op jit(solution)/shard_map/ppermute | solution.py:311
  466.2 42.0 %collective-permute-start.13 = (bf16[1,2,64,2048]{3,2,1,0:T(8,128)(2,1)S(1)}, bf16[1,2,64,2048]{3,2,1,0:T(8,128)(2,1)S(1)}, u32[]{:S(2)}, u32[]{:S(2)}) collective-permute-start(bf16[1,2,64,2048]{3,2,1,0:T(8,128)(2,1)S(1)} %broadcast_select_fusion.1), channel_id=1, source_target_pairs={{0,16},{2,18},{4,20},{6,22},{8,24},{10,26},{12,28},{14,30},{16,0},... | collective-permute-start | bytes 1572872 | tf_op jit(solution)/shard_map/ppermute | solution.py:311
  467.6 40.6 %collective-permute-start.14 = (bf16[1,2,64,2048]{3,2,1,0:T(8,128)(2,1)S(1)}, bf16[1,2,64,2048]{3,2,1,0:T(8,128)(2,1)S(1)}, u32[]{:S(2)}, u32[]{:S(2)}) collective-permute-start(bf16[1,2,64,2048]{3,2,1,0:T(8,128)(2,1)S(1)} %dynamic-slice_bitcast_fusion.13), channel_id=1, source_target_pairs={{0,1},{1,0},{2,3},{3,2},{4,5},{5,4},{6,7},{7,6},{8,9},{9,8},{10,11... | collective-permute-start | bytes 1572872 | tf_op jit(solution)/shard_map/ppermute | solution.py:311
  468.9 39.4 %collective-permute-start.15 = (bf16[1,2,64,2048]{3,2,1,0:T(8,128)(2,1)S(1)}, bf16[1,2,64,2048]{3,2,1,0:T(8,128)(2,1)S(1)}, u32[]{:S(2)}, u32[]{:S(2)}) collective-permute-start(bf16[1,2,64,2048]{3,2,1,0:T(8,128)(2,1)S(1)} %dynamic-slice_bitcast_fusion.12), channel_id=1, source_target_pairs={{0,4},{2,6},{4,0},{6,2},{8,12},{10,14},{12,8},{14,10},{16,20},{18,... | collective-permute-start | bytes 1572872 | tf_op jit(solution)/shard_map/ppermute | solution.py:311
  511.7 28.0 %collective-permute-start.16 = (bf16[1,64,2048]{2,1,0:T(8,128)(2,1)S(1)}, bf16[1,64,2048]{2,1,0:T(8,128)(2,1)S(1)}, u32[]{:S(2)}, u32[]{:S(2)}) collective-permute-start(bf16[1,64,2048]{2,1,0:T(8,128)(2,1)S(1)} %dynamic-slice_bitcast_fusion.19), channel_id=1, source_target_pairs={{0,8},{2,10},{4,12},{6,14},{8,0},{10,2},{12,4},{14,6},{16,24},{18,... | collective-permute-start | bytes 786440 | tf_op jit(solution)/shard_map/ppermute | solution.py:311
  512.5 27.3 %collective-permute-start.17 = (bf16[1,2,64,2048]{3,2,1,0:T(8,128)(2,1)S(1)}, bf16[1,2,64,2048]{3,2,1,0:T(8,128)(2,1)S(1)}, u32[]{:S(2)}, u32[]{:S(2)}) collective-permute-start(bf16[1,2,64,2048]{3,2,1,0:T(8,128)(2,1)S(1)} %broadcast_select_fusion), channel_id=1, source_target_pairs={{0,16},{2,18},{4,20},{6,22},{8,24},{10,26},{12,28},{14,30},{16,0},... | collective-permute-start | bytes 1572872 | tf_op jit(solution)/shard_map/ppermute | solution.py:311
  555.8 13.7 %collective-permute-start.19 = (bf16[1,256,1024]{2,1,0:T(8,128)(2,1)S(1)}, bf16[1,256,1024]{2,1,0:T(8,128)(2,1)S(1)}, u32[]{:S(2)}, u32[]{:S(2)}) collective-permute-start(bf16[1,256,1024]{2,1,0:T(8,128)(2,1)S(1)} %dynamic-slice_convert_fusion.2), channel_id=1, source_target_pairs={{1,0},{2,3},{5,4},{6,7},{9,8},{10,11},{13,12},{14,15},{17,16},{18,... | collective-permute-start | bytes 1572872 | tf_op jit(solution)/shard_map/ppermute | solution.py:683
  557.1 38.5 %collective-permute-start.26 = (bf16[2,256,1024]{2,1,0:T(8,128)(2,1)S(1)}, bf16[2,256,1024]{2,1,0:T(8,128)(2,1)S(1)}, u32[]{:S(2)}, u32[]{:S(2)}) collective-permute-start(bf16[2,256,1024]{2,1,0:T(8,128)(2,1)S(1)} %dynamic-slice_convert_fusion.1), channel_id=1, source_target_pairs={{1,2},{2,1},{5,6},{6,5},{9,10},{10,9},{13,14},{14,13},{17,18},{18,... | collective-permute-start | bytes 3145736 | tf_op jit(solution)/shard_map/ppermute | solution.py:683
  557.9 38.2 %collective-permute-start.25 = (bf16[3,256,1024]{2,1,0:T(8,128)(2,1)S(1)}, bf16[3,256,1024]{2,1,0:T(8,128)(2,1)S(1)}, u32[]{:S(2)}, u32[]{:S(2)}) collective-permute-start(bf16[3,256,1024]{2,1,0:T(8,128)(2,1)S(1)} %dynamic-slice_convert_fusion), channel_id=1, source_target_pairs={{0,1},{3,2},{4,5},{7,6},{8,9},{11,10},{12,13},{15,14},{16,17},{19,... | collective-permute-start | bytes 4718600 | tf_op jit(solution)/shard_map/ppermute | solution.py:683
  582.3 13.7 %collective-permute-start.20 = (bf16[8,64,1536]{2,1,0:T(8,128)(2,1)S(1)}, bf16[8,64,1536]{2,1,0:T(8,128)(2,1)S(1)}, u32[]{:S(2)}, u32[]{:S(2)}) collective-permute-start(bf16[8,64,1536]{2,1,0:T(8,128)(2,1)S(1)} %get-tuple-element.317), channel_id=1, source_target_pairs={{0,2},{2,0},{4,6},{6,4},{8,10},{10,8},{12,14},{14,12},{16,18},{18,... | collective-permute-start | bytes 4718600 | tf_op jit(solution)/shard_map/ppermute | solution.py:311
  597.3 12.6 %collective-permute-start.29 = (f32[8,48,128]{2,1,0:T(8,128)S(1)}, f32[8,48,128]{2,1,0:T(8,128)}, u32[]{:S(2)}, u32[]{:S(2)}) collective-permute-start(f32[8,48,128]{2,1,0:T(8,128)S(1)} %pad_maximum_fusion.7), channel_id=1, source_target_pairs={{0,1},{1,0},{2,3},{3,2},{4,5},{5,4},{6,7},{7,6},{8,9},{9,8},{10,11... | collective-permute-start | bytes 589832 | tf_op jit(solution)/shard_map/ppermute | solution.py:311
  601.7 20.6 %collective-permute-start.27 = (bf16[1,2,2,64,1536]{4,3,2,1,0:T(8,128)(2,1)}, bf16[1,2,2,64,1536]{4,3,2,1,0:T(8,128)(2,1)}, u32[]{:S(2)}, u32[]{:S(2)}) collective-permute-start(bf16[1,2,2,64,1536]{4,3,2,1,0:T(8,128)(2,1)} %dynamic-slice_bitcast_fusion.11), channel_id=1, source_target_pairs={{0,4},{2,6},{4,0},{6,2},{8,12},{10,14},{12,8},{14,10},{16,20},{18,... | collective-permute-start | bytes 2359304 | tf_op jit(solution)/shard_map/ppermute | solution.py:311
  601.7 22.1 %collective-permute-start.28 = (bf16[1,2,2,64,1536]{4,3,2,1,0:T(8,128)(2,1)}, bf16[1,2,2,64,1536]{4,3,2,1,0:T(8,128)(2,1)}, u32[]{:S(2)}, u32[]{:S(2)}) collective-permute-start(bf16[1,2,2,64,1536]{4,3,2,1,0:T(8,128)(2,1)} %dynamic-slice_bitcast_fusion.10), channel_id=1, source_target_pairs={{0,1},{1,0},{2,3},{3,2},{4,5},{5,4},{6,7},{7,6},{8,9},{9,8},{10,11... | collective-permute-start | bytes 2359304 | tf_op jit(solution)/shard_map/ppermute | solution.py:311
  625.6 16.1 %collective-permute-start.32 = (f32[16,48,128]{2,1,0:T(8,128)}, f32[16,48,128]{2,1,0:T(8,128)}, u32[]{:S(2)}, u32[]{:S(2)}) collective-permute-start(f32[16,48,128]{2,1,0:T(8,128)} %pad_maximum_fusion.5), channel_id=1, source_target_pairs={{0,2},{2,0},{4,6},{6,4},{8,10},{10,8},{12,14},{14,12},{16,18},{18,... | collective-permute-start | bytes 1179656 | tf_op jit(solution)/shard_map/ppermute | solution.py:311
  650.6 19.9 %collective-permute-start.33 = (bf16[1,2,64,1536]{3,2,1,0:T(8,128)(2,1)}, bf16[1,2,64,1536]{3,2,1,0:T(8,128)(2,1)}, u32[]{:S(2)}, u32[]{:S(2)}) collective-permute-start(bf16[1,2,64,1536]{3,2,1,0:T(8,128)(2,1)} %broadcast_select_fusion.2), channel_id=1, source_target_pairs={{0,16},{2,18},{4,20},{6,22},{8,24},{10,26},{12,28},{14,30},{16,0},... | collective-permute-start | bytes 1179656 | tf_op jit(solution)/shard_map/ppermute | solution.py:311
  (112 other events, 1861.4 us)
Sparse Core Ops, SparseCore 0:
  11.4 96.8 all-gather.3
  111.7 113.8 all-gather.5
  413.3 55.6 all-gather.7
  471.1 142.7 reduce-scatter.1
